TPU v7x, 128 devices: a whole 4x4x4 slice. The times are simulated.
128 devices in a mesh: member: 8 (over z_lo, x), grid: 16 (over y, z_hi, core).
Axes of the slice: x: 4, y: 4, z: 4 (z_hi: 2, z_lo: 2; z = z_hi * 2 + z_lo), core: 2. Of those that a mesh axis runs over, the one named last changes fastest.
Arguments:
- latent: bfloat16 [8, 32768, 1024], P('member', 'grid'), may hold values from -6 to 6
- w_in: bfloat16 [1024, 1024], P(('member', 'grid')), may hold values from -0.1875 to 0.1875
- b_in: float32 [1024], replicated, may hold values from -3 to 3
- w_out: bfloat16 [100, 1024], replicated, may hold values from -0.1875 to 0.1875
- b_out: float32 [100], replicated, may hold values from -3 to 3
- targets: float32 [100, 32768], P(None, 'grid'), may hold values from -6 to 6
- var_weight: float32 [100], replicated, may hold values from 0.5 to 5
- plan: int32 [3, 8], replicated, may hold values from 0 to 7, as said below
Outputs:
- loss: float32 [], replicated
- grad_latent: bfloat16 [8, 32768, 1024], P('member', 'grid')
- grad_w_in: float32 [1024, 1024], P(('member', 'grid'))
- grad_b_in: float32 [1024], replicated
- grad_w_out: float32 [100, 1024], replicated
- grad_b_out: float32 [100], replicated
Inputs may be any that keep to these rules, and one draw needn't show every extreme that they name: `plan`: each row is a perfect pairing of the 8 members: no member is its own partner, the partner of a member's partner is the member, and no pair occurs in two rows.
All inputs are finite; a program needn't handle non-finite values.
Results may differ from a plain program's by a relative error of at most 0.0095.
Values may be sent and summed in bfloat16 or wider, within the bound.
No kernel may reach another device: no remote copies, remote signals or barrier semaphores. Data moves between devices by JAX's collectives and lax.ppermute only.
A program may use at most 128 MiB of HBM per device.

v0:
```python
import jax
import jax.numpy as jnp
from jax import lax
from jax.sharding import PartitionSpec as P

DELTA = 0.25


def make_fold(mine, partner_rows):

    def fold(carry, piece, start):
        count = piece.shape[0]
        labels = jnp.arange(count, dtype=jnp.int32)
        weights = jnp.sum((partner_rows[:, None] == labels[None, :]).astype(jnp.float32), axis=0)
        diff = mine[None] - piece
        root = jnp.sqrt(diff * diff + DELTA * DELTA)
        slope_sum = jnp.einsum("k,kvp->vp", weights, diff / root)
        spread_sum = jnp.einsum("k,kvp->vp", weights, root - DELTA)
        return (slope_sum, spread_sum)

    return fold


def shards(latent, w_in, b_in, w_out, b_out, targets, var_weight, plan):
    hidden_in = latent[0]
    points = hidden_in.shape[0]
    rounds = plan.shape[0]
    w_full = lax.all_gather(w_in, ("member", "grid"), axis=0, tiled=True)
    member = lax.axis_index("member")
    grid_index = lax.axis_index("grid")
    members = lax.axis_size("member")
    grid_count = lax.axis_size("grid")
    total = points * grid_count
    place = (grid_index * points + jnp.arange(points, dtype=jnp.int32)).astype(jnp.float32)
    area = jnp.cos(1.4 * (place + 0.5) / total)
    scale_map = area[None, :] * var_weight[:, None]
    partner_rows = lax.dynamic_index_in_dim(plan, member, 1, keepdims=False)
    pre = jnp.dot(hidden_in, w_full, preferred_element_type=jnp.float32) + b_in[None, :]
    act = jax.nn.gelu(pre).astype(jnp.bfloat16)
    field = jnp.dot(w_out, act.T, preferred_element_type=jnp.float32) + b_out[:, None]
    pre, act, field = (pre, act, field)
    fold_all = make_fold(field, partner_rows)
    slope_sum, spread_sum = fold_all(
        (
            jnp.zeros((w_out.shape[0], points), jnp.float32),
            jnp.zeros((w_out.shape[0], points), jnp.float32),
        ),
        lax.all_gather(field[None], "member", axis=0, tiled=True),
        jnp.int32(0),
    )
    miss = field - targets
    miss_root = jnp.sqrt(miss * miss + DELTA * DELTA)
    cot = scale_map * (miss / miss_root - slope_sum / rounds)
    terms = scale_map * (miss_root - DELTA - spread_sum / (2.0 * rounds))
    cot_b = cot.astype(jnp.bfloat16)
    dact = jnp.dot(cot_b.T, w_out, preferred_element_type=jnp.float32)
    _, pull = jax.vjp(jax.nn.gelu, pre)
    dpre = pull(dact)[0]
    dpre_b = dpre.astype(jnp.bfloat16)
    grad_hidden = jnp.dot(dpre_b, w_full.T, preferred_element_type=jnp.float32).astype(jnp.bfloat16)
    kappa = 4.0 / jnp.sqrt(jnp.float32(members * total))
    out_term = jnp.dot(cot_b, act, preferred_element_type=jnp.float32)
    sum_w2, sum_b2, sum_b1, sum_loss = lax.psum(
        (out_term, jnp.sum(cot, axis=1), jnp.sum(dpre, axis=0), jnp.sum(terms)), ("member", "grid")
    )
    row_count = w_in.shape[0]
    full_term = jnp.dot(hidden_in.T, dpre_b, preferred_element_type=jnp.float32)
    summed = lax.psum(full_term, ("member", "grid"))
    offset = (member * grid_count + grid_index) * row_count
    own_rows = lax.dynamic_slice_in_dim(summed, offset, row_count, 0)
    loss = sum_loss / (members * total * w_out.shape[0])
    return (
        loss,
        grad_hidden[None],
        own_rows * kappa,
        sum_b1 * kappa,
        sum_w2 * kappa,
        sum_b2 * kappa,
    )


def solution(mesh):
    placed = (
        P("member", "grid", None),
        P(("member", "grid"), None),
        P(),
        P(),
        P(),
        P(None, "grid"),
        P(),
        P(),
    )
    return jax.shard_map(
        shards,
        mesh=mesh,
        in_specs=placed,
        out_specs=(P(), P("member", "grid", None), P(("member", "grid"), None), P(), P(), P()),
        check_vma=False,
    )
```

profile of v0, /device:TPU:1, one launch (start us, length us, event | category | flops | bytes accessed | tf_op | source)
XLA Modules:
  0.0 495.4 jit_solution(9077674508747040754)
XLA Ops:
  7.2 0.0 copy-start
  7.2 0.0 all-gather.5.cloned.1.call-start
  7.2 0.7 all-gather.5.cloned.1.call-update
  7.9 0.0 copy-start.5
  7.9 0.0 all-gather.7.cloned.1.call-start
  8.0 199.0 %all-gather.5.cloned.1.call-done = bf16[1024,1024]{1,0:T(8,128)(2,1)} async-done(((bf16[8,1024]{1,0:T(8,128)(2,1)}), bf16[1024,1024]{1,0:T(8,128)(2,1)}) %all-gather.5.cloned.1.call-update) | async-done | bytes 2097168 | tf_op jit(solution)/shard_map/all_gather | solution.py:28
  207.0 12.5 %multiply_convert_fusion = (bf16[2048,1024]{1,0:T(8,128)(2,1)S(1)}, f32[2048,1024]{1,0:T(8,128)}) fusion(f32[1024]{0:T(1024)} %param.10, bf16[1024,1024]{1,0:T(8,128)(2,1)} %all-gather.5.cloned.1.call-done, bf16[1,2048,1024]{2,1,0:T(8,128)(2,1)} %param.8), kind=kOutput, calls=%fused_computation.8 | convolution fusion | flops 4315938816 | bytes 18878464 | tf_op jit(solution)/shard_map/dot_general | solution.py:38
  219.5 2.0 copy-done.1
  221.5 0.0 copy-done
  221.5 0.0 copy-done.5
  221.5 2.4 convolution_add_fusion
  223.9 0.0 all-gather.7.cloned.1.call-update
  223.9 0.0 all-reduce.4.cloned.1.call-start
  224.0 0.0 copy-done.6
  224.0 0.2 dynamic-slice_reduce_fusion
  224.2 0.1 multiply_cosine_fusion
  224.2 0.1 convert_reduce_fusion
  224.3 75.7 %all-gather.7.cloned.1.call-done = f32[8,100,2048]{2,1,0:T(8,128)} async-done(((f32[1,100,2048]{2,1,0:T(8,128)}), f32[8,100,2048]{2,1,0:T(8,128)}) %all-gather.7.cloned.1.call-update) | async-done | bytes 6553616 | tf_op jit(solution)/shard_map/all_gather | solution.py:48
  300.1 5.8 %fusion.6 = (bf16[8,100,2048]{2,1,0:T(8,128)(2,1)S(1)}, bf16[8,100,2048]{2,1,0:T(8,128)(2,1)S(1)}) fusion(f32[8,100,2048]{2,1,0:T(8,128)} %all-gather.7.cloned.1.call-done, f32[100,2048]{1,0:T(8,128)} %bitcast.49), kind=kLoop, calls=%fused_computation.10 | loop fusion | flops 11468800 | bytes 13926400 | tf_op jit(solution)/shard_map/div | solution.py:17
  305.9 0.0 copy-start.3
  305.9 0.0 copy-start.4
  305.9 0.0 copy-start.7
  305.9 0.0 copy-start.2
  305.9 0.0 slice-start.1
  305.9 2.4 fusion.8
  308.4 0.0 copy-start.10
  308.4 2.4 fusion.10
  310.8 0.0 copy-done.3
  310.8 0.0 copy-done.4
  310.8 0.0 copy-done.7
  310.9 1.9 fusion.29
  312.8 1.5 fusion.24
  314.3 0.0 slice-done
  314.3 0.0 copy-start.8
  314.3 7.0 %fusion.30 = (f32[1024]{0:T(1024)S(1)}, bf16[2048,1024]{1,0:T(8,128)(2,1)S(1)}) fusion(f32[2048,1024]{1,0:T(8,128)S(1)} %bitcast.51, f32[1024]{0:T(1024)S(1)} %copy-done.10, bf16[100,1024]{1,0:T(8,128)(2,1)S(1)} %copy-done, bf16[100,2048]{1,0:T(8,128)(2,1)S(1)} %get-tuple-element.30), kind=kOutput, calls=%fused_computation.47 | convolution fusion | flops 465566720 | bytes 13205504 | tf_op jit(solution)/shard_map/dot_general | solution.py:56
  321.3 2.0 copy-done.11
  323.3 0.0 copy-done.8
  323.3 6.1 %fusion.16 = f32[1024,1024]{0,1:T(8,128)} fusion(bf16[1,2048,1024]{2,1,0:T(8,128)(2,1)S(1)} %copy-done.8, bf16[2048,1024]{1,0:T(8,128)(2,1)S(1)} %get-tuple-element.37), kind=kOutput, calls=%fused_computation.22 | convolution fusion | flops 4294967296 | bytes 12582912 | tf_op jit(solution)/shard_map/dot_general | solution.py:67
  329.4 0.0 all-reduce.4.cloned.1.call-update
  329.5 65.0 %all-reduce = (f32[]{:T(128)}, f32[1024]{0:T(1024)S(1)}, f32[100]{0:T(128)S(1)}) all-reduce(f32[]{:T(128)} %get-tuple-element.33, f32[1024]{0:T(1024)S(1)} %get-tuple-element.36, f32[100]{0:T(128)S(1)} %get-tuple-element.29), channel_id=1, replica_groups=mesh['member'=8,'grid'=16] {'member','grid'}, use_global_device_ids=true, to_apply=%region_2.3 | all-reduce | flops 1125 | bytes 9000 | tf_op jit(solution)/shard_map/psum | solution.py:63
  395.1 0.5 broadcast_multiply_fusion.2
  395.6 0.6 broadcast_multiply_fusion.1
  396.2 0.0 copy-done.9
  396.2 8.3 %convert_bitcast_fusion = bf16[1,2048,1024]{2,1,0:T(8,128)(2,1)} fusion(bf16[1024,1024]{1,0:T(8,128)(2,1)S(1)} %copy-done.9, bf16[2048,1024]{1,0:T(8,128)(2,1)} %copy-done.11), kind=kOutput, calls=%fused_computation.20 | convolution fusion | flops 4297064448 | bytes 10485760 | tf_op jit(solution)/shard_map/dot_general | solution.py:60
  404.6 79.3 %all-reduce.4.cloned.1.call-done = (f32[1024,1024]{0,1:T(8,128)}, f32[100,1024]{1,0:T(8,128)}) async-done(((f32[1024,1024]{0,1:T(8,128)}, f32[100,1024]{1,0:T(8,128)}), (f32[1024,1024]{0,1:T(8,128)}, f32[100,1024]{1,0:T(8,128)})) %all-reduce.4.cloned.1.call-update) | async-done | bytes 4603920 | tf_op jit(solution)/shard_map/psum | solution.py:68
  483.9 1.2 dynamic-slice_multiply_fusion
  485.1 0.8 copy.16
  485.9 1.8 broadcast_multiply_fusion
  (9 shorter events, 0.0 us)
Async XLA Ops:
  7.2 214.3 %copy-start = (bf16[100,1024]{1,0:T(8,128)(2,1)S(1)}, bf16[100,1024]{1,0:T(8,128)(2,1)}, u32[]{:S(2)}) copy-start(bf16[100,1024]{1,0:T(8,128)(2,1)} %param.11) | copy-start | bytes 614404
  7.2 199.8 %all-gather.5.cloned.1.call-start = ((), (), s32[]{:S(2)}) async-start(), calls=%async_computation | async-start | bytes 2113536 | tf_op jit(solution)/shard_map/all_gather | solution.py:28
  7.9 213.6 %copy-start.5 = (f32[100]{0:T(128)S(1)}, f32[100]{0:T(128)}, u32[]{:S(2)}) copy-start(f32[100]{0:T(128)} %param.12) | copy-start | bytes 1204
  7.9 292.1 %all-gather.7.cloned.1.call-start = ((), (), s32[]{:S(2)}) async-start(), calls=%async_computation.1 | async-start | bytes 7667712 | tf_op jit(solution)/shard_map/all_gather | solution.py:48
  219.5 2.0 copy-start.1
  219.5 4.5 copy-start.6
  223.9 260.0 %all-reduce.4.cloned.1.call-start = ((), (), s32[]{:S(2)}) async-start(), calls=%async_computation.2 | async-start | bytes 9240576 | tf_op jit(solution)/shard_map/psum | solution.py:68
  300.1 14.2 %slice-start = ((s8[8388608]{0:T(1024)(128)(4,1)}), s8[4194304]{0:T(1024)(128)(4,1)S(1)}, s32[]{:S(2)}) async-start(s8[8388608]{0:T(1024)(128)(4,1)} %bitcast.50), calls=%async_computation.3 | async-start | bytes 8388608
  305.9 5.0 %copy-start.3 = (f32[2048,100]{0,1:T(8,128)S(1)}, f32[2048,100]{0,1:T(8,128)}, u32[]{:S(2)}) copy-start(f32[2048,100]{0,1:T(8,128)} %convolution_add_fusion) | copy-start | bytes 2457604
  305.9 5.0 %copy-start.4 = (f32[100,2048]{1,0:T(8,128)S(1)}, f32[100,2048]{1,0:T(8,128)}, u32[]{:S(2)}) copy-start(f32[100,2048]{1,0:T(8,128)} %param.13) | copy-start | bytes 2457604
  305.9 5.0 %copy-start.7 = (f32[100]{0:T(128)S(1)}, f32[100]{0:T(128)}, u32[]{:S(2)}) copy-start(f32[100]{0:T(128)} %param.14) | copy-start | bytes 1204
  305.9 6.9 %copy-start.2 = (bf16[2048,1024]{1,0:T(8,128)(2,1)S(1)}, bf16[2048,1024]{1,0:T(8,128)(2,1)}, u32[]{:S(2)}) copy-start(bf16[2048,1024]{1,0:T(8,128)(2,1)} %copy-done.1) | copy-start | bytes 12582916
  305.9 8.4 %slice-start.1 = ((s8[8388608]{0:T(1024)(128)(4,1)}), s8[4194304]{0:T(1024)(128)(4,1)S(1)}, s32[]{:S(2)}) async-start(s8[8388608]{0:T(1024)(128)(4,1)} %bitcast.50), calls=%async_computation.4 | async-start | bytes 8388608
  308.4 5.9 %copy-start.10 = (f32[1024]{0:T(1024)S(1)}, f32[1024]{0:T(1024)}, u32[]{:S(2)}) copy-start(f32[1024]{0:T(1024)} %param.10) | copy-start | bytes 12292
  314.3 9.0 %copy-start.8 = (bf16[1,2048,1024]{2,1,0:T(8,128)(2,1)S(1)}, bf16[1,2048,1024]{2,1,0:T(8,128)(2,1)}, u32[]{:S(2)}) copy-start(bf16[1,2048,1024]{2,1,0:T(8,128)(2,1)} %param.8) | copy-start | bytes 12582916
  321.3 2.0 copy-start.11
  323.3 72.9 %copy-start.9 = (bf16[1024,1024]{1,0:T(8,128)(2,1)S(1)}, bf16[1024,1024]{1,0:T(8,128)(2,1)}, u32[]{:S(2)}) copy-start(bf16[1024,1024]{1,0:T(8,128)(2,1)} %all-gather.5.cloned.1.call-done) | copy-start | bytes 6291460
Sparse Core Ops, SparseCore 0:
  9.7 197.2 all-gather.4
  224.0 75.9 all-gather.6
  329.6 154.2 all-reduce.3
where the time goes:
time: 496 us; the launch traced here: 495 us
  waiting for transfers between devices  355 us (72%)
  blocking collectives  65 us (13%)
  matrix products  42.8 us (9%)
  between operations  15.7 us (3%)
  other arithmetic  12 us (2%)
  local copies, waits for them, and re-layouts  5 us (1%)
    all_gather x1, waiting for transfers between devices, shards(): w_full = lax.all_gather(w_in, ('member', 'grid'), axis=0, tiled=True)  199 us
    psum x1, waiting for transfers between devices, shards(): summed = lax.psum(full_term, ('member', 'grid'))  79.3 us
    all_gather x1, waiting for transfers between devices, shards(): lax.all_gather(field[None], 'member', axis=0, tiled=True)  75.7 us
    psum x1, blocking collectives, shards(): lax.psum((out_term, jnp.sum(cot, axis=1), jnp.sum(dpre, axis=0), jnp.sum(...  65 us
    dot_general x1, matrix products, shards(): jnp.dot(hidden_in, w_full, preferred_element_type=jnp.float32)  12.5 us
  transfers between devices with their start and end apart: 3, of which 3 were waited for; matrix products, arithmetic and copies ran while one was open for 2% of the time, Pallas kernels for 0%

commit v1 on v0

v1 whole, which is shorter than its diff:
```python
import jax
import jax.numpy as jnp
from jax import lax
from jax.sharding import PartitionSpec as P

DELTA = 0.25
BOTH = ("member", "grid")


def shards(latent, w_in, b_in, w_out, b_out, targets, var_weight, plan):
    hidden_in = latent[0]
    points, width = hidden_in.shape
    half = width // 2
    variables = w_out.shape[0]
    rounds, members = plan.shape
    member = lax.axis_index("member")
    grid_index = lax.axis_index("grid")
    grid_count = lax.axis_size("grid")
    devices = members * grid_count
    rows = w_in.shape[0]
    total = points * grid_count
    block = points // members
    core = lax.rem(grid_index, 2)
    swap = [(i, i ^ 1) for i in range(devices)]

    halves = jnp.stack([w_in[:, :half], w_in[:, half:]])
    send = jnp.broadcast_to(halves[None], (devices // 2, 2, rows, half))
    w_mine = lax.all_to_all(send.reshape(devices * rows, half), BOTH, 0, 0, tiled=True)
    w_other = lax.ppermute(w_mine, BOTH, swap)

    def part(a, which):
        return lax.dynamic_slice_in_dim(a, which * half, half, a.ndim - 1)

    w_halves = (w_mine, w_other)
    b_halves = (part(b_in, core), part(b_in, 1 - core))
    o_halves = (part(w_out, core), part(w_out, 1 - core))

    pres, acts, field = [], [], b_out[:, None]
    for w, b, o in zip(w_halves, b_halves, o_halves):
        pre = jnp.dot(hidden_in, w, preferred_element_type=jnp.float32) + b[None, :]
        act = jax.nn.gelu(pre).astype(jnp.bfloat16)
        field = field + jnp.dot(o, act.T, preferred_element_type=jnp.float32)
        pres.append(pre)
        acts.append(act)

    out = field.reshape(variables, members, block).transpose(1, 0, 2)
    fields = lax.all_to_all(out, "member", 0, 0, tiled=True)
    place = grid_index * points + member * block + jnp.arange(block, dtype=jnp.int32)
    area = jnp.cos(1.4 * (place.astype(jnp.float32) + 0.5) / total)
    scale_map = area[None, :] * var_weight[:, None]
    target = lax.dynamic_slice_in_dim(targets, member * block, block, 1)
    slopes, spreads = 0.0, 0.0
    for r in range(rounds):
        partners = [lax.dynamic_index_in_dim(fields, plan[r, m], 0) for m in range(members)]
        diff = fields - jnp.concatenate(partners)
        root = jnp.sqrt(diff * diff + DELTA * DELTA)
        slopes = slopes + diff / root
        spreads = spreads + (root - DELTA)
    miss = fields - target[None]
    miss_root = jnp.sqrt(miss * miss + DELTA * DELTA)
    cot = scale_map[None] * (miss / miss_root - slopes / rounds)
    terms = scale_map[None] * (miss_root - DELTA - spreads / (2.0 * rounds))
    sum_b2 = jnp.sum(cot, axis=(0, 2))
    sum_loss = jnp.sum(terms)
    back = lax.all_to_all(cot.astype(jnp.bfloat16), "member", 0, 0, tiled=True)
    cot_b = back.transpose(1, 0, 2).reshape(variables, points)

    grads1, grads2, sums1, dpres = [], [], [], []
    for pre, act, o in zip(pres, acts, o_halves):
        dact = jnp.dot(cot_b.T, o, preferred_element_type=jnp.float32)
        _, pull = jax.vjp(jax.nn.gelu, pre)
        dpre = pull(dact)[0]
        dpre_b = dpre.astype(jnp.bfloat16)
        dpres.append(dpre_b)
        grads1.append(jnp.dot(hidden_in.T, dpre_b, preferred_element_type=jnp.float32))
        grads2.append(jnp.dot(cot_b, act, preferred_element_type=jnp.float32))
        sums1.append(jnp.sum(dpre, axis=0))
    grad_hidden = sum(
        jnp.dot(d, w.T, preferred_element_type=jnp.float32) for d, w in zip(dpres, w_halves)
    ).astype(jnp.bfloat16)

    tail = jnp.concatenate([sum_b2, sum_loss[None], jnp.zeros((half - variables - 1,), jnp.float32)])
    def table(i):
        t = jnp.concatenate([grads2[i], sums1[i][None], (tail if i == 0 else 0 * tail)[None]])
        t = jnp.pad(t, ((0, devices - t.shape[0]), (0, 0)))
        t = t.reshape(16, 8, 8, half // 8).transpose(0, 2, 1, 3)
        return t.reshape(devices * 8, half // 8)

    def whole(i):
        return jnp.concatenate([grads1[i], table(i)], axis=1)

    got = lax.ppermute(whole(1).astype(jnp.bfloat16), BOTH, swap)
    mine = (whole(0) + got.astype(jnp.float32)).astype(jnp.bfloat16)
    parts = lax.all_to_all(mine, BOTH, 0, 0, tiled=True)
    summed = jnp.sum(parts.reshape(devices // 2, 2, rows, -1).astype(jnp.float32), axis=0)
    own_rows = jnp.concatenate([summed[0, :, :half], summed[1, :, :half]], axis=1)
    small = jnp.concatenate([summed[0, :, half:], summed[1, :, half:]], axis=1)
    spread_small = jnp.broadcast_to(small[None], (devices,) + small.shape)
    everyone = lax.all_to_all(spread_small, BOTH, 0, 0)
    tables = everyone.reshape(16, 8, 8, 2, half // 8).transpose(0, 2, 3, 1, 4).reshape(devices, width)
    tails = tables[variables + 1, :half] + tables[variables + 1, half:]
    kappa = 4.0 / jnp.sqrt(jnp.float32(members * total))
    loss = tails[variables] / (members * total * variables)
    return (
        loss,
        grad_hidden[None],
        own_rows * kappa,
        tables[variables] * kappa,
        tables[:variables] * kappa,
        tails[:variables] * kappa,
    )


def solution(mesh):
    placed = (
        P("member", "grid", None),
        P(BOTH, None),
        P(),
        P(),
        P(),
        P(None, "grid"),
        P(),
        P(),
    )
    return jax.shard_map(
        shards,
        mesh=mesh,
        in_specs=placed,
        out_specs=(P(), P("member", "grid", None), P(BOTH, None), P(), P(), P()),
        check_vma=False,
    )
```

time: 496 us -> 198 us (0.40)
  waiting for transfers between devices: 355 us -> 43 us
  blocking collectives: 65 us -> 0 us
  between operations: 15.7 us -> 48.6 us
  starting transfers between devices: 0.12 us -> 29.8 us
  local copies, waits for them, and re-layouts: 5 us -> 12.2 us
  matrix products: 42.8 us -> 49.8 us
    all_gather x2 -> x0, waiting for transfers between devices: 275 us -> none  [the longest x1 199 us: shards(): w_full = lax.all_gather(w_in, ('member', 'grid'), axis=0, tiled=True)]
    psum x1 -> x0, waiting for transfers between devices: 79.3 us -> none  [shards(): summed = lax.psum(full_term, ('member', 'grid'))]
    psum x1 -> x0, blocking collectives: 65 us -> none  [shards(): lax.psum((out_term, jnp.sum(cot, axis=1), jnp.sum(dpre, axis=0), jnp.sum(...]
    all_to_all x0 -> x5, waiting for transfers between devices: none -> 43 us  [the longest x1 18.1 us: shards(): lax.all_to_all(send.reshape(devices * rows, half), BOTH, 0, 0, tiled=True)]
    all_to_all x0 -> x5, starting transfers between devices: none -> 29 us  [the longest x1 11.5 us: shards(): lax.all_to_all(send.reshape(devices * rows, half), BOTH, 0, 0, tiled=True)]
    dot_general x8 -> x12, matrix products: 42.8 us -> 49.8 us  [the longest x2 16 us: shards(): jnp.dot(d, w.T, preferred_element_type=jnp.float32)]
    div x1 -> x0, other arithmetic: 5.79 us -> none  [fold(): slope_sum = jnp.einsum('k,kvp->vp', weights, diff / root)]
    convert_element_type x0 -> x2, other arithmetic: none -> 5.16 us  [the longest x1 3.4 us: shards(): back = lax.all_to_all(cot.astype(jnp.bfloat16), 'member', 0, 0, tiled=True)]
  transfers between devices with their start and end apart: 3 -> 7, of which waited for: 3 -> 4; matrix products, arithmetic and copies ran while one was open for 2% -> 22% of each run, Pallas kernels for 0% -> 0%
where the time goes in v1:
time: 198 us; the launch traced here: 196 us
  matrix products  49.8 us (25%)
  between operations  48.6 us (25%)
  waiting for transfers between devices  43 us (22%)
  starting transfers between devices  29.8 us (15%)
  other arithmetic  12.9 us (7%)
  local copies, waits for them, and re-layouts  12.2 us (6%)
    all_to_all x1, waiting for transfers between devices, shards(): lax.all_to_all(send.reshape(devices * rows, half), BOTH, 0, 0, tiled=True)  18.1 us
    dot_general x2, matrix products, shards(): jnp.dot(d, w.T, preferred_element_type=jnp.float32)  16 us
    all_to_all x1, waiting for transfers between devices, shards(): parts = lax.all_to_all(mine, BOTH, 0, 0, tiled=True)  14.5 us
    dot_general x2, matrix products, shards(): pre = jnp.dot(hidden_in, w, preferred_element_type=jnp.float32) + b[None, :]  13.8 us
    all_to_all x1, starting transfers between devices, shards(): lax.all_to_all(send.reshape(devices * rows, half), BOTH, 0, 0, tiled=True)  11.5 us
    dot_general x2, matrix products, shards(): dact = jnp.dot(cot_b.T, o, preferred_element_type=jnp.float32)  9.99 us
    dot_general x2, matrix products, shards(): jnp.dot(hidden_in.T, dpre_b, preferred_element_type=jnp.float32)  7.51 us
    all_to_all x1, waiting for transfers between devices, shards(): back = lax.all_to_all(cot.astype(jnp.bfloat16), 'member', 0, 0, tiled=True)  6.39 us
  transfers between devices with their start and end apart: 7, of which 4 were waited for; matrix products, arithmetic and copies ran while one was open for 22% of the time, Pallas kernels for 0%

profile of v1, /device:TPU:1, one launch (start us, length us, event | category | flops | bytes accessed | tf_op | source)
XLA Modules:
  0.0 196.4 jit_solution(7349802099423567630)
XLA Ops:
  0.6 0.8 slice_bitcast_fusion.3
  1.4 1.1 broadcast_in_dim.19
  2.5 11.5 %all-to-all-start = ((bf16[128,8,512]{2,1,0:T(8,128)(2,1)}), bf16[128,8,512]{2,1,0:T(8,128)(2,1)S(1)}, u32[]{:S(2)}, u32[]{:S(2)}) async-start(bf16[128,8,512]{2,1,0:T(8,128)(2,1)} %bitcast.2), calls=%async_computation | async-start | bytes 2097152 | tf_op jit(solution)/shard_map/all_to_all | solution.py:28
  14.0 0.8 fusion.60
  14.9 18.1 %all-to-all-done = bf16[128,8,512]{2,1,0:T(8,128)(2,1)S(1)} async-done(((bf16[128,8,512]{2,1,0:T(8,128)(2,1)}), bf16[128,8,512]{2,1,0:T(8,128)(2,1)S(1)}, u32[]{:S(2)}, u32[]{:S(2)}) %all-to-all-start) | async-done | bytes 1048608 | tf_op jit(solution)/shard_map/all_to_all | solution.py:28
  33.0 8.2 %fusion.18 = (bf16[2048,512]{0,1:T(8,128)(2,1)S(1)}, f32[512,2048]{1,0:T(8,128)}) fusion(f32[512]{0:T(512)S(1)} %get-tuple-element.39, bf16[1,2048,1024]{2,1,0:T(8,128)(2,1)} %param.8, bf16[128,8,512]{2,1,0:T(8,128)(2,1)S(1)} %all-to-all-done), kind=kOutput, calls=%fused_computation.27 | convolution fusion | flops 2157969408 | bytes 11536384 | tf_op jit(solution)/shard_map/dot_general | solution.py:40
  41.2 0.5 convolution_add_fusion.1
  41.7 5.6 %fusion.15 = (bf16[2048,512]{0,1:T(8,128)(2,1)S(1)}, f32[512,2048]{1,0:T(8,128)}) fusion(f32[512]{0:T(512)S(1)} %get-tuple-element.38, bf16[1024,512]{1,0:T(8,128)(2,1)S(1)} %collective-permute-done, bf16[1,2048,1024]{2,1,0:T(8,128)(2,1)S(1)} %copy-done.8), kind=kOutput, calls=%fused_computation.22 | convolution fusion | flops 2157969408 | bytes 11536384 | tf_op jit(solution)/shard_map/dot_general | solution.py:40
  47.3 0.5 convolution_add_fusion
  47.8 0.3 copy.64
  48.1 1.2 copy.67
  49.3 3.7 %all-to-all-start.1 = ((f32[8,100,256]{2,1,0:T(8,128)}), f32[8,100,256]{2,1,0:T(8,128)S(1)}, u32[]{:S(2)}, u32[]{:S(2)}) async-start(f32[8,100,256]{2,1,0:T(8,128)} %bitcast.155), calls=%async_computation.1 | async-start | bytes 1703936 | tf_op jit(solution)/shard_map/all_to_all | solution.py:47
  53.1 0.7 fusion.62
  54.9 0.6 fusion.63
  100.2 1.0 broadcast_multiply_fusion
  101.6 3.4 %fusion.59 = (bf16[8,100,256]{2,1,0:T(8,128)(2,1)}, f32[8,100,256]{2,1,0:T(8,128)}, f32[]{:T(128)}) fusion(f32[8,100,256]{2,1,0:T(8,128)S(1)} %all-to-all-done.1, f32[8,100,256]{2,1,0:T(8,128)S(1)} %dynamic-slice_dynamic-update-slice_fusion, f32[8,100,256]{2,1,0:T(8,128)S(1)} %get-tuple-element.11, f32[8,100,256]{2,1,0:T(8,128)S(1)} %get-tuple-element.9, ...), kind=kLoop, calls=%fused_computation.120 | loop fusion | flops 6553599 | bytes 4710404 | tf_op jit(solution)/shard_map/convert_element_type | solution.py:65
  105.0 4.9 %all-to-all-start.2 = ((bf16[8,100,256]{2,1,0:T(8,128)(2,1)}), bf16[8,100,256]{2,1,0:T(8,128)(2,1)S(1)}, u32[]{:S(2)}, u32[]{:S(2)}) async-start(bf16[8,100,256]{2,1,0:T(8,128)(2,1)} %get-tuple-element.6), calls=%async_computation.2 | async-start | bytes 851968 | tf_op jit(solution)/shard_map/all_to_all | solution.py:65
  109.9 1.3 reduce_sum.46
  111.2 0.7 fusion.61
  111.9 0.7 fusion.55
  112.6 6.4 %all-to-all-done.2 = bf16[8,100,256]{2,1,0:T(8,128)(2,1)S(1)} async-done(((bf16[8,100,256]{2,1,0:T(8,128)(2,1)}), bf16[8,100,256]{2,1,0:T(8,128)(2,1)S(1)}, u32[]{:S(2)}, u32[]{:S(2)}) %all-to-all-start.2) | async-done | bytes 409632 | tf_op jit(solution)/shard_map/all_to_all | solution.py:65
  119.3 0.8 convolution_convert_fusion
  120.0 1.2 copy-done.12
  121.2 3.7 %fusion.65 = (bf16[512]{0:T(512)(128)(2,1)S(1)}, bf16[2048,512]{0,1:T(8,128)(2,1)S(1)}) fusion(f32[512,2048]{1,0:T(8,128)S(1)} %copy-done.12, f32[512]{0:T(512)S(1)} %get-tuple-element.38, bf16[100,2048]{1,0:T(8,128)(2,1)S(1)} %bitcast.152, bf16[100,1024]{1,0:T(8,128)(2,1)S(1)} %copy-done, s32[]{:T(128)S(6)} %select_n.85), kind=kOutput, calls=%fused_computation.126 | convolution fusion | flops 232783360 | bytes 6827012 | tf_op jit(solution)/shard_map/dot_general | solution.py:70
  125.0 2.4 %fusion.34 = bf16[1024,512]{0,1:T(8,128)(2,1)S(1)} fusion(bf16[1,2048,1024]{2,1,0:T(8,128)(2,1)S(1)} %copy-done.9, bf16[2048,512]{0,1:T(8,128)(2,1)S(1)} %get-tuple-element.73), kind=kOutput, calls=%fused_computation.43 | convolution fusion | flops 2148007936 | bytes 7340032 | tf_op jit(solution)/shard_map/dot_general | solution.py:75
  127.7 1.1 pad_maximum_fusion
  128.8 0.8 collective-permute-start.1
  129.7 6.3 %fusion.64 = (f32[512]{0:T(512)S(1)}, bf16[2048,512]{0,1:T(8,128)(2,1)}) fusion(f32[512,2048]{1,0:T(8,128)} %get-tuple-element.67, f32[512]{0:T(512)S(1)} %get-tuple-element.39, bf16[100,2048]{1,0:T(8,128)(2,1)S(1)} %bitcast.153, bf16[100,1024]{1,0:T(8,128)(2,1)S(1)} %copy-done, s32[]{:T(128)S(6)} %select_n.84), kind=kOutput, calls=%fused_computation.125 | convolution fusion | flops 232783360 | bytes 6828036 | tf_op jit(solution)/shard_map/dot_general | solution.py:70
  135.9 0.8 fusion.66
  137.2 5.2 %fusion.28 = f32[1024,512]{0,1:T(8,128)S(1)} fusion(bf16[1,2048,1024]{2,1,0:T(8,128)(2,1)} %param.8, bf16[2048,512]{0,1:T(8,128)(2,1)} %get-tuple-element.71), kind=kOutput, calls=%fused_computation.41 | convolution fusion | flops 2147483648 | bytes 8388608 | tf_op jit(solution)/shard_map/dot_general | solution.py:75
  142.4 1.8 fusion.27
  144.1 1.4 copy.60
  145.6 4.1 %all-to-all-start.3 = ((bf16[128,8,576]{2,1,0:T(8,128)(2,1)}), bf16[128,8,576]{2,1,0:T(8,128)(2,1)S(1)}, u32[]{:S(2)}, u32[]{:S(2)}) async-start(bf16[128,8,576]{2,1,0:T(8,128)(2,1)} %bitcast.44), calls=%async_computation.3 | async-start | bytes 2621440 | tf_op jit(solution)/shard_map/all_to_all | solution.py:94
  149.7 7.3 %fusion.39 = f32[2048,1024]{1,0:T(8,128)} fusion(bf16[2048,512]{0,1:T(8,128)(2,1)} %get-tuple-element.71, bf16[128,8,512]{2,1,0:T(8,128)(2,1)S(1)} %copy-done.4), kind=kOutput, calls=%fused_computation.48 | convolution fusion | flops 2147483648 | bytes 11534336 | tf_op jit(solution)/shard_map/dot_general | solution.py:79
  157.0 14.5 %all-to-all-done.3 = bf16[128,8,576]{2,1,0:T(8,128)(2,1)S(1)} async-done(((bf16[128,8,576]{2,1,0:T(8,128)(2,1)}), bf16[128,8,576]{2,1,0:T(8,128)(2,1)S(1)}, u32[]{:S(2)}, u32[]{:S(2)}) %all-to-all-start.3) | async-done | bytes 1179680 | tf_op jit(solution)/shard_map/all_to_all | solution.py:94
  171.5 0.2 convert_reduce_fusion
  171.8 0.8 broadcast_in_dim.49
  172.6 4.8 %all-to-all-start.4 = ((f32[128,8,128]{2,1,0:T(8,128)}), f32[128,8,128]{2,1,0:T(8,128)S(1)}, u32[]{:S(2)}, u32[]{:S(2)}) async-start(f32[128,8,128]{2,1,0:T(8,128)} %broadcast_in_dim.49), calls=%async_computation.4 | async-start | bytes 1048576 | tf_op jit(solution)/shard_map/all_to_all | solution.py:99
  177.4 8.8 %fusion.12 = bf16[1,2048,1024]{2,1,0:T(8,128)(2,1)} fusion(f32[2048,1024]{1,0:T(8,128)} %fusion.39, bf16[1024,512]{1,0:T(8,128)(2,1)} %copy-done.10, bf16[2048,512]{0,1:T(8,128)(2,1)} %copy-done.11), kind=kOutput, calls=%fused_computation.17 | convolution fusion | flops 2151677952 | bytes 15728640 | tf_op jit(solution)/shard_map/dot_general | solution.py:79
  186.2 0.6 maximum_multiply_fusion
  186.8 4.1 %all-to-all-done.4 = f32[128,8,128]{2,1,0:T(8,128)S(1)} async-done(((f32[128,8,128]{2,1,0:T(8,128)}), f32[128,8,128]{2,1,0:T(8,128)S(1)}, u32[]{:S(2)}, u32[]{:S(2)}) %all-to-all-start.4) | async-done | bytes 524320 | tf_op jit(solution)/shard_map/all_to_all | solution.py:99
  190.8 0.6 reshape.143
  191.4 0.3 copy.61
  191.8 0.3 reshape.144
  192.1 0.8 slice_multiply_fusion
  192.9 0.6 slice_multiply_fusion.1
  193.5 0.6 slice.150
  194.1 0.5 fusion.56
  (58 shorter events, 1.6 us)
Async XLA Ops:
  0.6 40.6 %copy-start = (bf16[100,1024]{1,0:T(8,128)(2,1)S(1)}, bf16[100,1024]{1,0:T(8,128)(2,1)}, u32[]{:S(2)}) copy-start(bf16[100,1024]{1,0:T(8,128)(2,1)} %param.11) | copy-start | bytes 614404
  2.5 30.4 %all-to-all-start = ((bf16[128,8,512]{2,1,0:T(8,128)(2,1)}), bf16[128,8,512]{2,1,0:T(8,128)(2,1)S(1)}, u32[]{:S(2)}, u32[]{:S(2)}) async-start(bf16[128,8,512]{2,1,0:T(8,128)(2,1)} %bitcast.2), calls=%async_computation | async-start | bytes 2097152 | tf_op jit(solution)/shard_map/all_to_all | solution.py:28
  32.9 8.3 %copy-start.3 = (bf16[128,8,512]{2,1,0:T(8,128)(2,1)}, bf16[128,8,512]{2,1,0:T(8,128)(2,1)S(1)}, u32[]{:S(2)}) copy-start(bf16[128,8,512]{2,1,0:T(8,128)(2,1)S(1)} %all-to-all-done) | copy-start | bytes 3145732
  32.9 8.8 %collective-permute-start = (bf16[1024,512]{1,0:T(8,128)(2,1)S(1)}, bf16[1024,512]{1,0:T(8,128)(2,1)S(1)}, u32[]{:S(2)}, u32[]{:S(2)}) collective-permute-start(bf16[1024,512]{1,0:T(8,128)(2,1)S(1)} %bitcast.161), channel_id=1, source_target_pairs={{0,1},{1,0},{2,3},{3,2},{4,5},{5,4},{6,7},{7,6},{8,9},{9,8},{10,11... | collective-permute-start | bytes 3145736 | tf_op jit(solution)/shard_map/ppermute | solution.py:29
  33.0 8.2 %copy-start.7 = (f32[100]{0:T(128)S(1)}, f32[100]{0:T(128)}, u32[]{:S(2)}) copy-start(f32[100]{0:T(128)} %param.12) | copy-start | bytes 1204
  33.0 8.7 %copy-start.8 = (bf16[1,2048,1024]{2,1,0:T(8,128)(2,1)S(1)}, bf16[1,2048,1024]{2,1,0:T(8,128)(2,1)}, u32[]{:S(2)}) copy-start(bf16[1,2048,1024]{2,1,0:T(8,128)(2,1)} %param.8) | copy-start | bytes 12582916
  41.2 6.1 %copy-start.1 = (bf16[2048,512]{0,1:T(8,128)(2,1)}, bf16[2048,512]{0,1:T(8,128)(2,1)S(1)}, u32[]{:S(2)}) copy-start(bf16[2048,512]{0,1:T(8,128)(2,1)S(1)} %get-tuple-element.66) | copy-start | bytes 6291460
  41.7 5.6 %copy-start.10 = (bf16[1024,512]{1,0:T(8,128)(2,1)}, bf16[1024,512]{1,0:T(8,128)(2,1)S(1)}, u32[]{:S(2)}) copy-start(bf16[1024,512]{1,0:T(8,128)(2,1)S(1)} %collective-permute-done) | copy-start | bytes 3145732
  47.8 5.3 %copy-start.5 = (s32[3,8]{1,0:T(4,128)S(1)}, s32[3,8]{1,0:T(4,128)}, u32[]{:S(2)}) copy-start(s32[3,8]{1,0:T(4,128)} %param.15) | copy-start | bytes 292
  47.8 52.5 %copy-start.6 = (f32[100]{0:T(128)S(1)}, f32[100]{0:T(128)}, u32[]{:S(2)}) copy-start(f32[100]{0:T(128)} %param.14) | copy-start | bytes 1204
  49.3 51.9 %all-to-all-start.1 = ((f32[8,100,256]{2,1,0:T(8,128)}), f32[8,100,256]{2,1,0:T(8,128)S(1)}, u32[]{:S(2)}, u32[]{:S(2)}) async-start(f32[8,100,256]{2,1,0:T(8,128)} %bitcast.155), calls=%async_computation.1 | async-start | bytes 1703936 | tf_op jit(solution)/shard_map/all_to_all | solution.py:47
  105.0 14.0 %all-to-all-start.2 = ((bf16[8,100,256]{2,1,0:T(8,128)(2,1)}), bf16[8,100,256]{2,1,0:T(8,128)(2,1)S(1)}, u32[]{:S(2)}, u32[]{:S(2)}) async-start(bf16[8,100,256]{2,1,0:T(8,128)(2,1)} %get-tuple-element.6), calls=%async_computation.2 | async-start | bytes 851968 | tf_op jit(solution)/shard_map/all_to_all | solution.py:65
  119.0 2.2 %copy-start.12 = (f32[512,2048]{1,0:T(8,128)S(1)}, f32[512,2048]{1,0:T(8,128)}, u32[]{:S(2)}) copy-start(f32[512,2048]{1,0:T(8,128)} %get-tuple-element.69) | copy-start | bytes 12582916
  121.2 3.7 %copy-start.9 = (bf16[1,2048,1024]{2,1,0:T(8,128)(2,1)S(1)}, bf16[1,2048,1024]{2,1,0:T(8,128)(2,1)}, u32[]{:S(2)}) copy-start(bf16[1,2048,1024]{2,1,0:T(8,128)(2,1)} %param.8) | copy-start | bytes 12582916
  124.9 2.4 %copy-start.11 = (bf16[2048,512]{0,1:T(8,128)(2,1)}, bf16[2048,512]{0,1:T(8,128)(2,1)S(1)}, u32[]{:S(2)}) copy-start(bf16[2048,512]{0,1:T(8,128)(2,1)S(1)} %get-tuple-element.73) | copy-start | bytes 6291460
  128.8 13.5 %collective-permute-start.1 = (bf16[1024,576]{0,1:T(8,128)(2,1)}, bf16[1024,576]{0,1:T(8,128)(2,1)}, u32[]{:S(2)}, u32[]{:S(2)}) collective-permute-start(bf16[1024,576]{0,1:T(8,128)(2,1)} %pad_maximum_fusion), channel_id=1, source_target_pairs={{0,1},{1,0},{2,3},{3,2},{4,5},{5,4},{6,7},{7,6},{8,9},{9,8},{10,11... | collective-permute-start | bytes 3538952 | tf_op jit(solution)/shard_map/ppermute | solution.py:92
  129.7 6.3 %copy-start.2 = (bf16[2048,512]{0,1:T(8,128)(2,1)S(1)}, bf16[2048,512]{0,1:T(8,128)(2,1)}, u32[]{:S(2)}) copy-start(bf16[2048,512]{0,1:T(8,128)(2,1)} %copy-done.1) | copy-start | bytes 6291460
  142.4 7.3 %copy-start.4 = (bf16[128,8,512]{2,1,0:T(8,128)(2,1)S(1)}, bf16[128,8,512]{2,1,0:T(8,128)(2,1)}, u32[]{:S(2)}) copy-start(bf16[128,8,512]{2,1,0:T(8,128)(2,1)} %copy-done.3) | copy-start | bytes 3145732
  145.6 25.9 %all-to-all-start.3 = ((bf16[128,8,576]{2,1,0:T(8,128)(2,1)}), bf16[128,8,576]{2,1,0:T(8,128)(2,1)S(1)}, u32[]{:S(2)}, u32[]{:S(2)}) async-start(bf16[128,8,576]{2,1,0:T(8,128)(2,1)} %bitcast.44), calls=%async_computation.3 | async-start | bytes 2621440 | tf_op jit(solution)/shard_map/all_to_all | solution.py:94
  172.6 18.2 %all-to-all-start.4 = ((f32[128,8,128]{2,1,0:T(8,128)}), f32[128,8,128]{2,1,0:T(8,128)S(1)}, u32[]{:S(2)}, u32[]{:S(2)}) async-start(f32[128,8,128]{2,1,0:T(8,128)} %broadcast_in_dim.49), calls=%async_computation.4 | async-start | bytes 1048576 | tf_op jit(solution)/shard_map/all_to_all | solution.py:99

commit v2 on v1

--- a/solution.py
+++ b/solution.py
@@ -1,10 +1,58 @@
 import jax
 import jax.numpy as jnp
 from jax import lax
+from jax.experimental import pallas as pl
+from jax.experimental.pallas import tpu as pltpu
 from jax.sharding import PartitionSpec as P
 
 DELTA = 0.25
 BOTH = ("member", "grid")
+VMEM_BYTES = 48 << 20
+
+
+def pair_kernel(plan_ref, f_ref, t_ref, s_ref, cot_ref, b2_ref, l_ref):
+    n, v, blk = f_ref.shape
+    rounds = plan_ref.shape[0]
+    vp = cot_ref.shape[1]
+    D = DELTA
+    b2_ref[...] = jnp.zeros_like(b2_ref); l_ref[...] = jnp.zeros_like(l_ref)
+    cot_ref[...] = jnp.zeros_like(cot_ref)
+    RB = 16
+    def body(m, _):
+        for r0 in range(0, v, RB):
+            rs = slice(r0, min(r0+RB, v))
+            f = f_ref[m, rs, :]
+            sc = s_ref[rs, :]
+            d = f - t_ref[rs, :]
+            q = d*d + D*D
+            inv = lax.rsqrt(q)
+            slope = d*inv
+            spread = q*inv - D
+            ps = jnp.zeros_like(f); pr = jnp.zeros_like(f)
+            for r in range(rounds):
+                x = f - f_ref[plan_ref[r, m], rs, :]
+                y = x*x + D*D
+                iv = lax.rsqrt(y)
+                ps += x*iv
+                pr += y*iv - D
+            cot = sc*(slope - ps*(1.0/rounds))
+            b2_ref[rs, :] += cot
+            l_ref[rs, :] += sc*(spread - pr*(0.5/rounds))
+            h = min(RB, v-r0)
+            cb = cot.astype(jnp.bfloat16)
+            if h < RB:
+                cb = jnp.concatenate([cb.astype(jnp.float32), jnp.zeros((RB-h, blk), jnp.float32)]).astype(jnp.bfloat16)
+            cot_ref[m, r0:r0+RB, :] = cb
+        return 0
+    lax.fori_loop(0, n, body, 0)
+
+def pair(plan, f, t, s):
+    n, v, blk = f.shape
+    vp = -(-v//16)*16
+    vm = pl.BlockSpec(memory_space=pltpu.VMEM)
+    return pl.pallas_call(pair_kernel, in_specs=[pl.BlockSpec(memory_space=pltpu.SMEM), vm, vm, vm], out_specs=[vm]*3,
+        out_shape=[jax.ShapeDtypeStruct((n,vp,blk),jnp.bfloat16), jax.ShapeDtypeStruct((v,blk),jnp.float32), jax.ShapeDtypeStruct((v,blk),jnp.float32)],
+        compiler_params=pltpu.CompilerParams(vmem_limit_bytes=VMEM_BYTES), name="pair_terms")(plan,f,t,s)
 
 
 def shards(latent, w_in, b_in, w_out, b_out, targets, var_weight, plan):
@@ -49,21 +97,13 @@
     area = jnp.cos(1.4 * (place.astype(jnp.float32) + 0.5) / total)
     scale_map = area[None, :] * var_weight[:, None]
     target = lax.dynamic_slice_in_dim(targets, member * block, block, 1)
-    slopes, spreads = 0.0, 0.0
-    for r in range(rounds):
-        partners = [lax.dynamic_index_in_dim(fields, plan[r, m], 0) for m in range(members)]
-        diff = fields - jnp.concatenate(partners)
-        root = jnp.sqrt(diff * diff + DELTA * DELTA)
-        slopes = slopes + diff / root
-        spreads = spreads + (root - DELTA)
-    miss = fields - target[None]
-    miss_root = jnp.sqrt(miss * miss + DELTA * DELTA)
-    cot = scale_map[None] * (miss / miss_root - slopes / rounds)
-    terms = scale_map[None] * (miss_root - DELTA - spreads / (2.0 * rounds))
-    sum_b2 = jnp.sum(cot, axis=(0, 2))
-    sum_loss = jnp.sum(terms)
-    back = lax.all_to_all(cot.astype(jnp.bfloat16), "member", 0, 0, tiled=True)
-    cot_b = back.transpose(1, 0, 2).reshape(variables, points)
+    cot, b2_terms, loss_terms = pair(plan, fields, target, scale_map)
+    sum_b2 = jnp.sum(b2_terms, axis=1)
+    sum_loss = jnp.sum(loss_terms)
+    back = lax.all_to_all(cot, "member", 0, 0, tiled=True)
+    cot_b = back.transpose(1, 0, 2).reshape(-1, points)
+    extra = cot_b.shape[0] - variables
+    o_halves = [jnp.pad(o, ((0, extra), (0, 0))) for o in o_halves]
 
     grads1, grads2, sums1, dpres = [], [], [], []
     for pre, act, o in zip(pres, acts, o_halves):
@@ -81,7 +121,7 @@
 
     tail = jnp.concatenate([sum_b2, sum_loss[None], jnp.zeros((half - variables - 1,), jnp.float32)])
     def table(i):
-        t = jnp.concatenate([grads2[i], sums1[i][None], (tail if i == 0 else 0 * tail)[None]])
+        t = jnp.concatenate([grads2[i][:variables], sums1[i][None], (tail if i == 0 else 0 * tail)[None]])
         t = jnp.pad(t, ((0, devices - t.shape[0]), (0, 0)))
         t = t.reshape(16, 8, 8, half // 8).transpose(0, 2, 1, 3)
         return t.reshape(devices * 8, half // 8)

time: 198 us -> 166 us (0.84)
  between operations: 48.6 us -> 2.77 us
  waiting for transfers between devices: 43 us -> 55.7 us
  matrix products: 49.8 us -> 55 us
  other arithmetic: 12.9 us -> 8.96 us
  Pallas kernels: 0 us -> 2.61 us
    all_to_all x1, waiting for transfers between devices: 0.01 us -> 12.7 us  [shards(): fields = lax.all_to_all(out, 'member', 0, 0, tiled=True)]
    convert_element_type x1 -> x0, other arithmetic: 3.4 us -> none  [shards(): back = lax.all_to_all(cot.astype(jnp.bfloat16), 'member', 0, 0, tiled=True)]
    dot_general x2, matrix products: 7.51 us -> 10.5 us  [shards(): jnp.dot(hidden_in.T, dpre_b, preferred_element_type=jnp.float32)]
    pallas_call x0 -> x1, Pallas kernels: none -> 2.61 us  [pair(): pl.pallas_call(pair_kernel, in_specs=[pl.BlockSpec(memory_space=pltpu.SME...]
  transfers between devices with their start and end apart: 7 -> 7, of which waited for: 4 -> 5; matrix products, arithmetic and copies ran while one was open for 22% -> 25% of each run, Pallas kernels for 0% -> 0%
where the time goes in v2:
time: 166 us; the launch traced here: 165 us
  waiting for transfers between devices  55.7 us (34%)
  matrix products  55 us (33%)
  starting transfers between devices  28.4 us (17%)
  local copies, waits for them, and re-layouts  11.9 us (7%)
  other arithmetic  8.96 us (5%)
  between operations  2.77 us (2%)
  Pallas kernels  2.61 us (2%)
    all_to_all x1, waiting for transfers between devices, shards(): lax.all_to_all(send.reshape(devices * rows, half), BOTH, 0, 0, tiled=True)  17.1 us
    dot_general x2, matrix products, shards(): jnp.dot(d, w.T, preferred_element_type=jnp.float32)  15.8 us
    all_to_all x1, waiting for transfers between devices, shards(): parts = lax.all_to_all(mine, BOTH, 0, 0, tiled=True)  14.4 us
    dot_general x2, matrix products, shards(): pre = jnp.dot(hidden_in, w, preferred_element_type=jnp.float32) + b[None, :]  13.8 us
    all_to_all x1, waiting for transfers between devices, shards(): fields = lax.all_to_all(out, 'member', 0, 0, tiled=True)  12.7 us
    all_to_all x1, starting transfers between devices, shards(): lax.all_to_all(send.reshape(devices * rows, half), BOTH, 0, 0, tiled=True)  11.5 us
    dot_general x2, matrix products, shards(): dact = jnp.dot(cot_b.T, o, preferred_element_type=jnp.float32)  10.8 us
    dot_general x2, matrix products, shards(): jnp.dot(hidden_in.T, dpre_b, preferred_element_type=jnp.float32)  10.5 us
  transfers between devices with their start and end apart: 7, of which 5 were waited for; matrix products, arithmetic and copies ran while one was open for 25% of the time, Pallas kernels for 0%

profile of v2, /device:TPU:1, one launch (start us, length us, event | category | flops | bytes accessed | tf_op | source)
XLA Modules:
  0.0 165.3 jit_solution(15902357618631559194)
XLA Ops:
  0.6 0.7 slice_bitcast_fusion.3
  1.4 1.1 broadcast_in_dim.19
  2.5 11.5 %all-to-all-start = ((bf16[128,8,512]{2,1,0:T(8,128)(2,1)}), bf16[128,8,512]{2,1,0:T(8,128)(2,1)S(1)}, u32[]{:S(2)}, u32[]{:S(2)}) async-start(bf16[128,8,512]{2,1,0:T(8,128)(2,1)} %bitcast.2), calls=%async_computation | async-start | bytes 2097152 | tf_op jit(solution)/shard_map/all_to_all | solution.py:76
  14.0 0.8 fusion.57
  14.8 1.0 constant_dynamic-slice_fusion.1
  15.8 17.1 %all-to-all-done = bf16[128,8,512]{2,1,0:T(8,128)(2,1)S(1)} async-done(((bf16[128,8,512]{2,1,0:T(8,128)(2,1)}), bf16[128,8,512]{2,1,0:T(8,128)(2,1)S(1)}, u32[]{:S(2)}, u32[]{:S(2)}) %all-to-all-start) | async-done | bytes 1048608 | tf_op jit(solution)/shard_map/all_to_all | solution.py:76
  32.9 8.2 %fusion.18 = (bf16[2048,512]{0,1:T(8,128)(2,1)S(1)}, f32[512,2048]{1,0:T(8,128)}) fusion(f32[512]{0:T(512)S(1)} %get-tuple-element.21, bf16[1,2048,1024]{2,1,0:T(8,128)(2,1)} %param.8, bf16[128,8,512]{2,1,0:T(8,128)(2,1)S(1)} %all-to-all-done), kind=kOutput, calls=%fused_computation.27 | convolution fusion | flops 2157969408 | bytes 11536384 | tf_op jit(solution)/shard_map/dot_general | solution.py:88
  41.1 0.5 convolution_add_fusion.1
  41.7 5.6 %fusion.15 = (bf16[2048,512]{0,1:T(8,128)(2,1)S(1)}, f32[512,2048]{1,0:T(8,128)}) fusion(f32[512]{0:T(512)S(1)} %get-tuple-element.20, bf16[1024,512]{1,0:T(8,128)(2,1)S(1)} %collective-permute-done, bf16[1,2048,1024]{2,1,0:T(8,128)(2,1)S(1)} %copy-done.8), kind=kOutput, calls=%fused_computation.22 | convolution fusion | flops 2157969408 | bytes 11536384 | tf_op jit(solution)/shard_map/dot_general | solution.py:88
  47.2 0.5 convolution_add_fusion
  47.7 0.3 copy.46
  48.1 1.2 copy.48
  49.3 3.5 %all-to-all-start.1 = ((f32[8,100,256]{2,1,0:T(8,128)}), f32[8,100,256]{2,1,0:T(8,128)S(1)}, u32[]{:S(2)}, u32[]{:S(2)}) async-start(f32[8,100,256]{2,1,0:T(8,128)} %bitcast.131), calls=%async_computation.1 | async-start | bytes 1703936 | tf_op jit(solution)/shard_map/all_to_all | solution.py:95
  52.9 1.0 broadcast_multiply_fusion
  53.9 12.7 %all-to-all-done.1.f_ref = f32[8,100,256]{2,1,0:T(8,128)S(1)} async-done(((f32[8,100,256]{2,1,0:T(8,128)}), f32[8,100,256]{2,1,0:T(8,128)S(1)}, u32[]{:S(2)}, u32[]{:S(2)}) %all-to-all-start.1) | async-done | bytes 819232 | tf_op jit(solution)/shard_map/all_to_all | solution.py:95
  66.6 2.6 %pair_terms.1 = (bf16[8,112,256]{2,1,0:T(8,128)(2,1)}, f32[100,256]{1,0:T(8,128)S(1)}, f32[100,256]{1,0:T(8,128)S(1)}) custom-call(s32[3,8]{1,0:T(4,128)S(1)} %copy-done, f32[8,100,256]{2,1,0:T(8,128)S(1)} %all-to-all-done.1.f_ref, f32[100,256]{1,0:T(8,128)S(1)} %get-tuple-element.33.t_ref, f32[100,256]{1,0:T(8,128)S(1)} %get-tuple-element.32.s_ref), custom_call_target="tpu_custom_call" | custom-call | tf_op jit(solution)/shard_map/pair_terms/pallas_call | solution.py:53
  69.2 3.7 %all-to-all-start.2 = ((bf16[8,112,256]{2,1,0:T(8,128)(2,1)}), bf16[8,112,256]{2,1,0:T(8,128)(2,1)S(1)}, u32[]{:S(2)}, u32[]{:S(2)}) async-start(bf16[8,112,256]{2,1,0:T(8,128)(2,1)} %get-tuple-element.9), calls=%async_computation.2 | async-start | bytes 917504 | tf_op jit(solution)/shard_map/all_to_all | solution.py:103
  72.9 0.6 reduce_sum.47
  73.6 0.7 fusion.58
  74.3 0.7 fusion.51
  75.1 7.1 %all-to-all-done.2 = bf16[8,112,256]{2,1,0:T(8,128)(2,1)S(1)} async-done(((bf16[8,112,256]{2,1,0:T(8,128)(2,1)}), bf16[8,112,256]{2,1,0:T(8,128)(2,1)S(1)}, u32[]{:S(2)}, u32[]{:S(2)}) %all-to-all-start.2) | async-done | bytes 458784 | tf_op jit(solution)/shard_map/all_to_all | solution.py:103
  82.1 0.8 copy-done.2
  82.9 1.1 copy.45
  84.0 2.4 %fusion.61 = bf16[112,512]{1,0:T(8,128)(2,1)S(1)} fusion(bf16[112,2048]{1,0:T(8,128)(2,1)S(1)} %bitcast.127, bf16[2048,512]{0,1:T(8,128)(2,1)} %copy-done.1), kind=kOutput, calls=%fused_computation.94 | convolution fusion | flops 234881024 | bytes 2670592 | tf_op jit(solution)/shard_map/dot_general | solution.py:116
  86.4 6.2 %fusion.60 = (bf16[512]{0:T(512)(128)(2,1)S(1)}, bf16[2048,512]{0,1:T(8,128)(2,1)}) fusion(f32[512,2048]{1,0:T(8,128)} %get-tuple-element.27, f32[512]{0:T(512)S(1)} %get-tuple-element.20, bf16[112,2048]{1,0:T(8,128)(2,1)S(1)} %bitcast.128, bf16[100,512]{1,0:T(8,128)(2,1)} %copy-done.5), kind=kOutput, calls=%fused_computation.93 | convolution fusion | flops 257949184 | bytes 6855680 | tf_op jit(solution)/shard_map/dot_general | solution.py:110
  93.1 5.3 %fusion.34 = bf16[1024,512]{0,1:T(8,128)(2,1)S(1)} fusion(bf16[1,2048,1024]{2,1,0:T(8,128)(2,1)} %param.8, bf16[2048,512]{0,1:T(8,128)(2,1)} %get-tuple-element.31), kind=kOutput, calls=%fused_computation.43 | convolution fusion | flops 2148007936 | bytes 7340032 | tf_op jit(solution)/shard_map/dot_general | solution.py:115
  98.4 1.1 pad_maximum_fusion
  99.5 0.8 collective-permute-start.1
  100.3 4.6 %fusion.59 = (f32[512]{0:T(512)S(1)}, bf16[2048,512]{0,1:T(8,128)(2,1)}) fusion(f32[512,2048]{1,0:T(8,128)S(1)} %copy-done.11, f32[512]{0:T(512)S(1)} %get-tuple-element.21, bf16[112,2048]{1,0:T(8,128)(2,1)S(1)} %bitcast.129, bf16[100,512]{1,0:T(8,128)(2,1)S(1)} %get-tuple-element.13), kind=kOutput, calls=%fused_computation.92 | convolution fusion | flops 257949184 | bytes 6856704 | tf_op jit(solution)/shard_map/dot_general | solution.py:110
  104.9 0.8 fusion.42
  106.2 5.2 %fusion.28 = f32[1024,512]{0,1:T(8,128)S(1)} fusion(bf16[1,2048,1024]{2,1,0:T(8,128)(2,1)} %param.8, bf16[2048,512]{0,1:T(8,128)(2,1)} %get-tuple-element.29), kind=kOutput, calls=%fused_computation.41 | convolution fusion | flops 2147483648 | bytes 8388608 | tf_op jit(solution)/shard_map/dot_general | solution.py:115
  111.3 1.8 %fusion.27 = bf16[1024,576]{0,1:T(8,128)(2,1)S(1)} fusion(f32[1024,64]{0,1:T(8,128)S(1)} %copy.36, f32[1024,512]{0,1:T(8,128)S(1)} %fusion.28, bf16[1024,576]{0,1:T(8,128)(2,1)} %collective-permute-done.1), kind=kLoop, calls=%fused_computation.40 | loop fusion | flops 2359296 | bytes 4718592 | tf_op jit(solution)/shard_map/convert_element_type | solution.py:133
  113.1 1.4 copy.41
  114.5 4.1 %all-to-all-start.3 = ((bf16[128,8,576]{2,1,0:T(8,128)(2,1)}), bf16[128,8,576]{2,1,0:T(8,128)(2,1)S(1)}, u32[]{:S(2)}, u32[]{:S(2)}) async-start(bf16[128,8,576]{2,1,0:T(8,128)(2,1)} %bitcast.20), calls=%async_computation.3 | async-start | bytes 2621440 | tf_op jit(solution)/shard_map/all_to_all | solution.py:134
  118.6 7.3 %fusion.39 = f32[2048,1024]{1,0:T(8,128)} fusion(bf16[2048,512]{0,1:T(8,128)(2,1)} %get-tuple-element.29, bf16[128,8,512]{2,1,0:T(8,128)(2,1)S(1)} %copy-done.4), kind=kOutput, calls=%fused_computation.47 | convolution fusion | flops 2147483648 | bytes 11534336 | tf_op jit(solution)/shard_map/dot_general | solution.py:119
  126.0 14.4 %all-to-all-done.3 = bf16[128,8,576]{2,1,0:T(8,128)(2,1)S(1)} async-done(((bf16[128,8,576]{2,1,0:T(8,128)(2,1)}), bf16[128,8,576]{2,1,0:T(8,128)(2,1)S(1)}, u32[]{:S(2)}, u32[]{:S(2)}) %all-to-all-start.3) | async-done | bytes 1179680 | tf_op jit(solution)/shard_map/all_to_all | solution.py:134
  140.7 0.8 broadcast_in_dim.46
  141.5 4.8 %all-to-all-start.4 = ((f32[128,8,128]{2,1,0:T(8,128)}), f32[128,8,128]{2,1,0:T(8,128)S(1)}, u32[]{:S(2)}, u32[]{:S(2)}) async-start(f32[128,8,128]{2,1,0:T(8,128)} %broadcast_in_dim.46), calls=%async_computation.4 | async-start | bytes 1048576 | tf_op jit(solution)/shard_map/all_to_all | solution.py:139
  146.3 8.4 %fusion.12 = bf16[1,2048,1024]{2,1,0:T(8,128)(2,1)} fusion(f32[2048,1024]{1,0:T(8,128)} %fusion.39, bf16[1024,512]{1,0:T(8,128)(2,1)S(1)} %copy-done.10, bf16[2048,512]{0,1:T(8,128)(2,1)} %get-tuple-element.31), kind=kOutput, calls=%fused_computation.17 | convolution fusion | flops 2151677952 | bytes 15728640 | tf_op jit(solution)/shard_map/dot_general | solution.py:119
  154.7 0.6 maximum_multiply_fusion
  155.4 4.4 %all-to-all-done.4 = f32[128,8,128]{2,1,0:T(8,128)S(1)} async-done(((f32[128,8,128]{2,1,0:T(8,128)}), f32[128,8,128]{2,1,0:T(8,128)S(1)}, u32[]{:S(2)}, u32[]{:S(2)}) %all-to-all-start.4) | async-done | bytes 524320 | tf_op jit(solution)/shard_map/all_to_all | solution.py:139
  159.7 0.6 reshape.117
  160.3 0.3 copy.42
  160.7 0.3 reshape.118
  161.0 0.6 slice.66
  161.6 0.5 fusion.52
  162.1 0.6 slice_multiply_fusion.1
  162.7 0.8 slice_multiply_fusion
  (46 shorter events, 1.4 us)
Async XLA Ops:
  2.5 30.4 %all-to-all-start = ((bf16[128,8,512]{2,1,0:T(8,128)(2,1)}), bf16[128,8,512]{2,1,0:T(8,128)(2,1)S(1)}, u32[]{:S(2)}, u32[]{:S(2)}) async-start(bf16[128,8,512]{2,1,0:T(8,128)(2,1)} %bitcast.2), calls=%async_computation | async-start | bytes 2097152 | tf_op jit(solution)/shard_map/all_to_all | solution.py:76
  15.8 31.4 %copy-start.5 = (bf16[100,512]{1,0:T(8,128)(2,1)}, bf16[100,512]{1,0:T(8,128)(2,1)S(1)}, u32[]{:S(2)}) copy-start(bf16[100,512]{1,0:T(8,128)(2,1)S(1)} %get-tuple-element.12) | copy-start | bytes 307204
  32.9 8.3 %copy-start.3 = (bf16[128,8,512]{2,1,0:T(8,128)(2,1)}, bf16[128,8,512]{2,1,0:T(8,128)(2,1)S(1)}, u32[]{:S(2)}) copy-start(bf16[128,8,512]{2,1,0:T(8,128)(2,1)S(1)} %all-to-all-done) | copy-start | bytes 3145732
  32.9 8.7 %collective-permute-start = (bf16[1024,512]{1,0:T(8,128)(2,1)S(1)}, bf16[1024,512]{1,0:T(8,128)(2,1)S(1)}, u32[]{:S(2)}, u32[]{:S(2)}) collective-permute-start(bf16[1024,512]{1,0:T(8,128)(2,1)S(1)} %bitcast.136), channel_id=1, source_target_pairs={{0,1},{1,0},{2,3},{3,2},{4,5},{5,4},{6,7},{7,6},{8,9},{9,8},{10,11... | collective-permute-start | bytes 3145736 | tf_op jit(solution)/shard_map/ppermute | solution.py:77
  32.9 8.2 %copy-start.6 = (f32[100]{0:T(128)S(1)}, f32[100]{0:T(128)}, u32[]{:S(2)}) copy-start(f32[100]{0:T(128)} %param.12) | copy-start | bytes 1204
  32.9 8.7 %copy-start.8 = (bf16[1,2048,1024]{2,1,0:T(8,128)(2,1)S(1)}, bf16[1,2048,1024]{2,1,0:T(8,128)(2,1)}, u32[]{:S(2)}) copy-start(bf16[1,2048,1024]{2,1,0:T(8,128)(2,1)} %param.8) | copy-start | bytes 12582916
  41.6 5.6 %copy-start.9 = (bf16[1024,512]{1,0:T(8,128)(2,1)}, bf16[1024,512]{1,0:T(8,128)(2,1)S(1)}, u32[]{:S(2)}) copy-start(bf16[1024,512]{1,0:T(8,128)(2,1)S(1)} %collective-permute-done) | copy-start | bytes 3145732
  47.2 2.1 %copy-start.1 = (bf16[2048,512]{0,1:T(8,128)(2,1)}, bf16[2048,512]{0,1:T(8,128)(2,1)S(1)}, u32[]{:S(2)}) copy-start(bf16[2048,512]{0,1:T(8,128)(2,1)S(1)} %get-tuple-element.26) | copy-start | bytes 6291460
  47.7 5.2 %copy-start.7 = (f32[100]{0:T(128)S(1)}, f32[100]{0:T(128)}, u32[]{:S(2)}) copy-start(f32[100]{0:T(128)} %param.14) | copy-start | bytes 1204
  47.7 18.9 %copy-start = (s32[3,8]{1,0:T(4,128)S(1)}, s32[3,8]{1,0:T(4,128)}, u32[]{:S(2)}) copy-start(s32[3,8]{1,0:T(4,128)} %plan_ref.1) | copy-start | bytes 292
  49.3 17.3 %all-to-all-start.1 = ((f32[8,100,256]{2,1,0:T(8,128)}), f32[8,100,256]{2,1,0:T(8,128)S(1)}, u32[]{:S(2)}, u32[]{:S(2)}) async-start(f32[8,100,256]{2,1,0:T(8,128)} %bitcast.131), calls=%async_computation.1 | async-start | bytes 1703936 | tf_op jit(solution)/shard_map/all_to_all | solution.py:95
  69.2 12.9 %all-to-all-start.2 = ((bf16[8,112,256]{2,1,0:T(8,128)(2,1)}), bf16[8,112,256]{2,1,0:T(8,128)(2,1)S(1)}, u32[]{:S(2)}, u32[]{:S(2)}) async-start(bf16[8,112,256]{2,1,0:T(8,128)(2,1)} %get-tuple-element.9), calls=%async_computation.2 | async-start | bytes 917504 | tf_op jit(solution)/shard_map/all_to_all | solution.py:103
  82.1 0.8 copy-start.2
  93.0 7.3 %copy-start.11 = (f32[512,2048]{1,0:T(8,128)S(1)}, f32[512,2048]{1,0:T(8,128)}, u32[]{:S(2)}) copy-start(f32[512,2048]{1,0:T(8,128)} %get-tuple-element.25) | copy-start | bytes 12582916
  99.5 11.8 %collective-permute-start.1 = (bf16[1024,576]{0,1:T(8,128)(2,1)}, bf16[1024,576]{0,1:T(8,128)(2,1)}, u32[]{:S(2)}, u32[]{:S(2)}) collective-permute-start(bf16[1024,576]{0,1:T(8,128)(2,1)} %pad_maximum_fusion), channel_id=1, source_target_pairs={{0,1},{1,0},{2,3},{3,2},{4,5},{5,4},{6,7},{7,6},{8,9},{9,8},{10,11... | collective-permute-start | bytes 3538952 | tf_op jit(solution)/shard_map/ppermute | solution.py:132
  111.3 7.3 %copy-start.4 = (bf16[128,8,512]{2,1,0:T(8,128)(2,1)S(1)}, bf16[128,8,512]{2,1,0:T(8,128)(2,1)}, u32[]{:S(2)}) copy-start(bf16[128,8,512]{2,1,0:T(8,128)(2,1)} %copy-done.3) | copy-start | bytes 3145732
  114.5 25.8 %all-to-all-start.3 = ((bf16[128,8,576]{2,1,0:T(8,128)(2,1)}), bf16[128,8,576]{2,1,0:T(8,128)(2,1)S(1)}, u32[]{:S(2)}, u32[]{:S(2)}) async-start(bf16[128,8,576]{2,1,0:T(8,128)(2,1)} %bitcast.20), calls=%async_computation.3 | async-start | bytes 2621440 | tf_op jit(solution)/shard_map/all_to_all | solution.py:134
  118.6 27.6 %copy-start.10 = (bf16[1024,512]{1,0:T(8,128)(2,1)S(1)}, bf16[1024,512]{1,0:T(8,128)(2,1)}, u32[]{:S(2)}) copy-start(bf16[1024,512]{1,0:T(8,128)(2,1)} %copy-done.9) | copy-start | bytes 3145732
  141.5 18.2 %all-to-all-start.4 = ((f32[128,8,128]{2,1,0:T(8,128)}), f32[128,8,128]{2,1,0:T(8,128)S(1)}, u32[]{:S(2)}, u32[]{:S(2)}) async-start(f32[128,8,128]{2,1,0:T(8,128)} %broadcast_in_dim.46), calls=%async_computation.4 | async-start | bytes 1048576 | tf_op jit(solution)/shard_map/all_to_all | solution.py:139

commit v3 on v2

v3 whole, which is shorter than its diff:
```python
import math

import jax
import jax.numpy as jnp
from jax import lax
from jax.experimental import pallas as pl
from jax.experimental.pallas import tpu as pltpu
from jax.sharding import PartitionSpec as P

DELTA = 0.25
BOTH = ("member", "grid")
VMEM_BYTES = 60 << 20
VMEM_SMALL = 24 << 20


GELU_A = 0.7978845608028654
GELU_B = 0.044715
WHOLE = pl.BlockSpec(memory_space=pltpu.VMEM)
HBM = pl.BlockSpec(memory_space=pltpu.HBM)


def shape(dims, kind):
    return jax.ShapeDtypeStruct(dims, kind)


def cost(flops, moved, special=0):
    return pl.CostEstimate(flops=flops, bytes_accessed=moved, transcendentals=special)


def load(src, dst, sem):
    copy = pltpu.make_async_copy(src, dst, sem)
    copy.start()
    return copy


def forward_kernel(first, parts, lat, w, b, o, extra, f_ref):
    points = lat.shape[0]
    half = w.shape[1]
    tile = points // parts
    rows, block = f_ref.shape[1:]
    for i in range(parts):
        sl = slice(i * tile, (i + 1) * tile)
        f = None
        for n in range(0, half, 256):
            cols = slice(n, n + 256)
            pre = jnp.dot(lat[sl, :], w[:, cols], preferred_element_type=jnp.float32) + b[:, cols]
            t = jnp.tanh(pre * (GELU_A + (GELU_A * GELU_B) * (pre * pre)))
            act = (pre * (0.5 + 0.5 * t)).astype(jnp.bfloat16)
            g = lax.dot_general(
                o[:, cols], act, (((1,), (1,)), ((), ())), preferred_element_type=jnp.float32
            )
            f = g if f is None else f + g
        for q in range(tile // block):
            at = i * (tile // block) + q
            piece = f[:rows, q * block : (q + 1) * block]
            f_ref[at] = piece + (extra[...] if first else extra[at])


def forward_half(first, lat, w, b, o, extra, rows, blocks):
    points, width = lat.shape
    half = w.shape[1]
    return pl.pallas_call(
        lambda *refs: forward_kernel(first, 4, *refs),
        in_specs=[WHOLE] * 5,
        out_specs=WHOLE,
        out_shape=shape((blocks, rows, points // blocks), jnp.float32),
        compiler_params=pltpu.CompilerParams(vmem_limit_bytes=VMEM_SMALL),
        cost_estimate=cost(2 * points * half * (width + rows), points * 2 * width, points * half),
        name="forward_half",
    )(lat, w, b, o, extra)


def slope_kernel(parts, lat_ref, w_ref, b, act_ref, g_ref, act_v, g_v, lat, w, sems, out_sems):
    points = lat.shape[0]
    half = w.shape[1]
    tile = points // parts
    slices = [slice(i * tile, (i + 1) * tile) for i in range(parts)]

    def fetch(i):
        return load(lat_ref.at[slices[i]], lat.at[slices[i]], sems.at[i])

    ready_w = load(w_ref, w, sems.at[parts])
    ready = [fetch(0)]
    ready_w.wait()
    out = []
    for i, sl in enumerate(slices):
        ready[i].wait()
        if i + 1 < parts:
            ready.append(fetch(i + 1))
        for n in range(0, half, 256):
            cols = slice(n, n + 256)
            pre = jnp.dot(lat[sl, :], w[:, cols], preferred_element_type=jnp.float32) + b[:, cols]
            sq = pre * pre
            t = jnp.tanh(pre * (GELU_A + (GELU_A * GELU_B) * sq))
            gate = 0.5 + 0.5 * t
            act_v[sl, cols] = (pre * gate).astype(jnp.bfloat16)
            inner = (0.5 * pre) * (1.0 - t * t) * (GELU_A + (3.0 * GELU_A * GELU_B) * sq)
            g_v[sl, cols] = (gate + inner).astype(jnp.bfloat16)
        out.append(load(act_v.at[sl], act_ref.at[sl], out_sems.at[2 * i]))
        out.append(load(g_v.at[sl], g_ref.at[sl], out_sems.at[2 * i + 1]))
    for copy in out:
        copy.wait()


def slope_half(lat, w, b):
    points, width = lat.shape
    half = w.shape[1]
    parts = 4
    return pl.pallas_call(
        lambda *refs: slope_kernel(parts, *refs),
        in_specs=[HBM] * 2 + [WHOLE],
        out_specs=[HBM] * 2,
        out_shape=[shape((points, half), jnp.bfloat16)] * 2,
        scratch_shapes=[
            pltpu.VMEM((points, half), jnp.bfloat16),
            pltpu.VMEM((points, half), jnp.bfloat16),
            pltpu.VMEM((points, width), jnp.bfloat16),
            pltpu.VMEM((width, half), jnp.bfloat16),
            pltpu.SemaphoreType.DMA((parts + 1,)),
            pltpu.SemaphoreType.DMA((2 * parts,)),
        ],
        compiler_params=pltpu.CompilerParams(vmem_limit_bytes=VMEM_BYTES),
        cost_estimate=cost(2 * points * half * width, points * (2 * width + 4 * half), points * half),
        name="slope_half",
    )(lat, w, b)


def backward_kernel(variables, parts, *refs):
    cot_ref, g_ref, lat_ref, act_ref, o, tail, dpre_ref, pack_ref = refs[:8]
    cot, g, lat, act, dpre_v, pack, table, sems, out_sems = refs[8:]
    blocks, rows, block = cot.shape
    points, half = g.shape
    width = lat.shape[1]
    kind = pack.dtype
    tile = points // parts
    cut = width // parts
    slices = [slice(i * tile, (i + 1) * tile) for i in range(parts)]

    def fetch(i):
        sl = slices[i]
        return (
            load(g_ref.at[sl], g.at[sl], sems.at[1 + 2 * i]),
            load(act_ref.at[sl], act.at[sl], sems.at[2 + 2 * i]),
        )

    def fetch_lat(i):
        cols = pl.ds(i * cut, cut)
        return load(lat_ref.at[:, cols], lat.at[:, cols], sems.at[1 + 2 * parts + i])

    ready_cot = load(cot_ref, cot, sems.at[0])
    ready = [fetch(0), fetch(1)]
    ready_lat = []
    ready_cot.wait()
    b1, w2 = None, None
    out = []
    for i in range(parts):
        for copy in ready[i]:
            copy.wait()
        if i + 2 < parts:
            ready.append(fetch(i + 2))
        else:
            ready_lat.append(fetch_lat(i + 2 - parts))
        for q in range(i * blocks // parts, (i + 1) * blocks // parts):
            sl = slice(q * block, (q + 1) * block)
            dact = lax.dot_general(
                cot[q], o[...], (((0,), (0,)), ((), ())), preferred_element_type=jnp.float32
            )
            dpre = dact * g[sl, :].astype(jnp.float32)
            dpre_v[sl, :] = dpre.astype(jnp.bfloat16)
            s = jnp.sum(dpre.reshape(-1, 8, half), axis=0)
            b1 = s if b1 is None else b1 + s
            a = jnp.dot(cot[q], act[sl, :], preferred_element_type=jnp.float32)
            w2 = a if w2 is None else w2 + a
        sl = slice(i * tile, (i + 1) * tile)
        out.append(load(dpre_v.at[sl], dpre_ref.at[sl], out_sems.at[i]))
    table[...] = jnp.zeros_like(table)
    table[:rows, :] = w2
    table[variables : variables + 1, :] = jnp.sum(b1, axis=0, keepdims=True)
    if kind == jnp.float32:
        table[variables + 1 : variables + 2, : tail.shape[1]] = tail[...]
    side = half // 8
    lanes = half // (2 * side)
    pack[:, half + side :] = jnp.zeros((width, 128 - side), kind)
    for i in range(parts):
        ready_lat[i].wait()
        if i + 2 < parts:
            ready_lat.append(fetch_lat(i + 2))
        sl = slice(i * cut, (i + 1) * cut)
        pack[sl, :half] = lax.dot_general(
            lat[:, sl], dpre_v[...], (((0,), (0,)), ((), ())), preferred_element_type=jnp.float32
        ).astype(kind)
        for unit in range(i * cut // 16, (i + 1) * cut // 16):
            r, c = unit // lanes, unit % lanes
            piece = table[8 * r : 8 * r + 8, 2 * side * c : 2 * side * (c + 1)]
            both = jnp.concatenate([piece[:, :side], piece[:, side:]], axis=0)
            pack[16 * unit : 16 * unit + 16, half : half + side] = both.astype(kind)
        out.append(load(pack.at[sl], pack_ref.at[sl], out_sems.at[parts + i]))
    for copy in out:
        copy.wait()


def backward_half(cot, o, g, lat, act, tail, variables, kind):
    blocks, rows, block = cot.shape
    points, half = g.shape
    width = lat.shape[1]
    parts = 4
    return pl.pallas_call(
        lambda *refs: backward_kernel(variables, parts, *refs),
        in_specs=[HBM] * 4 + [WHOLE] * 2,
        out_specs=[HBM] * 2,
        out_shape=[shape((points, half), jnp.bfloat16), shape((width, half + 128), kind)],
        scratch_shapes=[
            pltpu.VMEM(cot.shape, jnp.bfloat16),
            pltpu.VMEM(g.shape, jnp.bfloat16),
            pltpu.VMEM(lat.shape, jnp.bfloat16),
            pltpu.VMEM(act.shape, jnp.bfloat16),
            pltpu.VMEM((points, half), jnp.bfloat16),
            pltpu.VMEM((width, half + 128), kind),
            pltpu.VMEM((width // 8, half), jnp.float32),
            pltpu.SemaphoreType.DMA((1 + 3 * parts,)),
            pltpu.SemaphoreType.DMA((2 * parts,)),
        ],
        compiler_params=pltpu.CompilerParams(vmem_limit_bytes=VMEM_BYTES),
        cost_estimate=cost(2 * points * half * (width + 2 * rows), points * (2 * width + 6 * half)),
        name="backward_half",
    )(cot, g, lat, act, o, tail)


def finish_kernel(kappa, all_ref, w2_ref, b1_ref, tail_ref):
    variables, width = w2_ref.shape
    half = width // 2
    lanes = half // 128
    side = 64
    for r in range(-(-(variables + 2) // 8)):
        for c in range(lanes):
            a = all_ref[r * 2 * lanes + 2 * c]
            b = all_ref[r * 2 * lanes + 2 * c + 1]
            for h in range(2):
                piece = jnp.concatenate(
                    [a[:, h * side : (h + 1) * side], b[:, h * side : (h + 1) * side]], axis=1
                )
                cols = slice(h * half + 128 * c, h * half + 128 * (c + 1))
                low = 8 * r
                keep = min(8, variables - low)
                if keep > 0:
                    w2_ref[low : low + keep, cols] = piece[:keep] * kappa
                at = variables - low
                if 0 <= at < 8:
                    b1_ref[:, cols] = piece[at : at + 1] * kappa
                at = variables + 1 - low
                if 0 <= at < 8:
                    tail_ref[:, cols] = piece[at : at + 1]


def finish(everyone, variables, width, kappa):
    return pl.pallas_call(
        lambda *refs: finish_kernel(kappa, *refs),
        in_specs=[WHOLE],
        out_specs=[WHOLE] * 3,
        out_shape=[
            shape((variables, width), jnp.float32),
            shape((1, width), jnp.float32),
            shape((1, width), jnp.float32),
        ],
        compiler_params=pltpu.CompilerParams(vmem_limit_bytes=VMEM_SMALL),
        name="finish",
    )(everyone)


def pair_kernel(plan_ref, f_ref, t_ref, s_ref, cot_ref, tail_ref, b2_ref, l_ref):
    n, v, blk = f_ref.shape
    rounds = plan_ref.shape[0]
    vp = cot_ref.shape[1]
    D = DELTA
    b2_ref[...] = jnp.zeros_like(b2_ref); l_ref[...] = jnp.zeros_like(l_ref)
    cot_ref[...] = jnp.zeros_like(cot_ref)
    RB = 16
    def body(m, _):
        for r0 in range(0, v, RB):
            rs = slice(r0, min(r0+RB, v))
            f = f_ref[m, rs, :]
            sc = s_ref[rs, :]
            d = f - t_ref[rs, :]
            q = d*d + D*D
            inv = lax.rsqrt(q)
            slope = d*inv
            spread = q*inv - D
            ps = jnp.zeros_like(f); pr = jnp.zeros_like(f)
            for r in range(rounds):
                x = f - f_ref[plan_ref[r, m], rs, :]
                y = x*x + D*D
                iv = lax.rsqrt(y)
                ps += x*iv
                pr += y*iv - D
            cot = sc*(slope - ps*(1.0/rounds))
            b2_ref[rs, :] += cot
            l_ref[rs, :] += sc*(spread - pr*(0.5/rounds))
            h = min(RB, v-r0)
            cb = cot.astype(jnp.bfloat16)
            if h < RB:
                cb = jnp.concatenate([cb.astype(jnp.float32), jnp.zeros((RB-h, blk), jnp.float32)]).astype(jnp.bfloat16)
            cot_ref[m, r0:r0+RB, :] = cb
        return 0
    lax.fori_loop(0, n, body, 0)
    tail_ref[:, :128] = jnp.sum(b2_ref[...].T, axis=0, keepdims=True)
    tail_ref[:, 128:] = jnp.full((1, 128), jnp.sum(l_ref[...]), jnp.float32)

def pair(plan, f, t, s):
    n, v, blk = f.shape
    vp = -(-v//16)*16
    vm = pl.BlockSpec(memory_space=pltpu.VMEM)
    return pl.pallas_call(pair_kernel, in_specs=[pl.BlockSpec(memory_space=pltpu.SMEM), vm, vm, vm], out_specs=[vm]*2,
        out_shape=[jax.ShapeDtypeStruct((n,vp,blk),jnp.bfloat16), jax.ShapeDtypeStruct((1,256),jnp.float32)],
        scratch_shapes=[pltpu.VMEM((128,blk),jnp.float32), pltpu.VMEM((v,blk),jnp.float32)],
        compiler_params=pltpu.CompilerParams(vmem_limit_bytes=VMEM_SMALL), name="pair_terms")(plan,f,t,s)


def shards(latent, w_in, b_in, w_out, b_out, targets, var_weight, plan):
    hidden_in = latent[0]
    points, width = hidden_in.shape
    half = width // 2
    variables = w_out.shape[0]
    rounds, members = plan.shape
    member = lax.axis_index("member")
    grid_index = lax.axis_index("grid")
    grid_count = lax.axis_size("grid")
    devices = members * grid_count
    rows = w_in.shape[0]
    total = points * grid_count
    block = points // members
    core = lax.rem(grid_index, 2)
    swap = [(i, i ^ 1) for i in range(devices)]

    halves = jnp.stack([w_in[:, :half], w_in[:, half:]])
    send = jnp.broadcast_to(halves[None], (devices // 2, 2, rows, half))
    w_mine = lax.all_to_all(send.reshape(devices * rows, half), BOTH, 0, 0, tiled=True)
    w_other = lax.ppermute(w_mine, BOTH, swap)

    def part(a, which):
        return lax.dynamic_slice_in_dim(a, which * half, half, a.ndim - 1)

    tall = -(-variables // 8) * 8
    taller = -(-variables // 16) * 16
    out_pad = jnp.pad(w_out, ((0, taller - variables), (0, 0)))
    b_row = b_in[None, :]
    w_halves = (w_mine, w_other)
    b_halves = (part(b_row, core), part(b_row, 1 - core))
    o_halves = (part(out_pad, core), part(out_pad, 1 - core))

    bias = jnp.pad(b_out, (0, tall - variables))[:, None]
    partial = forward_half(
        True, hidden_in, w_mine, b_halves[0], o_halves[0], bias, tall, members
    )
    out = forward_half(
        False, hidden_in, w_other, b_halves[1], o_halves[1], partial, tall, members
    )

    fields = lax.all_to_all(out, "member", 0, 0, tiled=True)
    place = grid_index * points + member * block + jnp.arange(block, dtype=jnp.int32)
    area = jnp.cos(1.4 * (place.astype(jnp.float32) + 0.5) / total)
    scale_map = jnp.pad(area[None, :] * var_weight[:, None], ((0, tall - variables), (0, 0)))
    target = lax.dynamic_slice_in_dim(targets, member * block, block, 1)
    target = jnp.pad(target, ((0, tall - variables), (0, 0)))
    act1, g1 = slope_half(hidden_in, w_other, b_halves[1])
    act0, g0 = slope_half(hidden_in, w_mine, b_halves[0])
    fields, act1, g1 = lax.optimization_barrier((fields, act1, g1))
    cot, tail = pair(plan, fields, target, scale_map)
    back = lax.all_to_all(cot, "member", 0, 0, tiled=True)
    back, act0, g0 = lax.optimization_barrier((back, act0, g0))
    d1, pack1 = backward_half(
        back, o_halves[1], g1, hidden_in, act1, tail, variables, jnp.bfloat16
    )
    got = lax.ppermute(pack1, BOTH, swap)
    d0, pack0 = backward_half(
        back, o_halves[0], g0, hidden_in, act0, tail, variables, jnp.float32
    )
    mine = (pack0 + got.astype(jnp.float32)).astype(jnp.bfloat16)
    grad_hidden = sum(
        jnp.dot(d, w.T, preferred_element_type=jnp.float32) for d, w in zip((d0, d1), w_halves)
    ).astype(jnp.bfloat16)
    parts = lax.all_to_all(mine, BOTH, 0, 0, tiled=True)
    summed = jnp.sum(parts.reshape(devices // 2, 2, rows, -1).astype(jnp.float32), axis=0)
    own_rows = jnp.concatenate([summed[0, :, :half], summed[1, :, :half]], axis=1)
    small = jnp.concatenate([summed[0, :, half : half + 64], summed[1, :, half : half + 64]], axis=1)
    spread_small = jnp.broadcast_to(small[None], (devices,) + small.shape)
    everyone = lax.all_to_all(spread_small, BOTH, 0, 0)
    kappa = 4.0 / math.sqrt(members * total)
    grad_out, grad_bias, tails = finish(everyone, variables, width, kappa)
    tails = tails[0, :half] + tails[0, half:]
    loss = tails[128] / (members * total * variables)
    return (
        loss,
        grad_hidden[None],
        own_rows * kappa,
        grad_bias[0],
        grad_out,
        tails[:variables] * kappa,
    )


def solution(mesh):
    placed = (
        P("member", "grid", None),
        P(BOTH, None),
        P(),
        P(),
        P(),
        P(None, "grid"),
        P(),
        P(),
    )
    return jax.shard_map(
        shards,
        mesh=mesh,
        in_specs=placed,
        out_specs=(P(), P("member", "grid", None), P(BOTH, None), P(), P(), P()),
        check_vma=False,
    )
```

time: 166 us -> 152 us (0.916)
  Pallas kernels: 2.61 us -> 48 us
  matrix products: 55 us -> 16 us
  waiting for transfers between devices: 55.7 us -> 24.3 us
  blocking collectives: 0 us -> 30.2 us
  starting transfers between devices: 28.4 us -> 18.7 us
  local copies, waits for them, and re-layouts: 11.9 us -> 6.3 us
  other arithmetic: 8.96 us -> 4.6 us
    pallas_call x0 -> x7, Pallas kernels: none -> 45.4 us  [the longest x2 17.6 us: backward_half(): pl.pallas_call(lambda *refs: backward_kernel(variables, parts, *refs), in...]
    dot_general x10 -> x0, matrix products: 39.2 us -> none  [the longest x2 13.8 us: shards(): pre = jnp.dot(hidden_in, w, preferred_element_type=jnp.float32) + b[None, :]]
    all_to_all x0 -> x1, blocking collectives: none -> 30.2 us  [shards(): lax.all_to_all(send.reshape(devices * rows, half), BOTH, 0, 0, tiled=True)]
    all_to_all x1 -> x0, waiting for transfers between devices: 17.1 us -> none  [shards(): lax.all_to_all(send.reshape(devices * rows, half), BOTH, 0, 0, tiled=True)]
    all_to_all x1 -> x0, starting transfers between devices: 11.5 us -> none  [shards(): lax.all_to_all(send.reshape(devices * rows, half), BOTH, 0, 0, tiled=True)]
    all_to_all x1, waiting for transfers between devices: 12.7 us -> 4.96 us  [shards(): fields = lax.all_to_all(out, 'member', 0, 0, tiled=True)]
    all_to_all x1, waiting for transfers between devices: 7.09 us -> 0.73 us  [shards(): back = lax.all_to_all(cot, 'member', 0, 0, tiled=True)]
    reshape x11 -> x0, local copies, waits for them, and re-layouts: 4 us -> none  [the longest x2 1.26 us: shards(): out = field.reshape(variables, members, block).transpose(1, 0, 2)]
  transfers between devices with their start and end apart: 7 -> 6, of which waited for: 5 -> 4; matrix products, arithmetic and copies ran while one was open for 25% -> 11% of each run, Pallas kernels for 0% -> 20%
where the time goes in v3:
time: 152 us; the launch traced here: 151 us
  Pallas kernels  48 us (32%)
  blocking collectives  30.2 us (20%)
  waiting for transfers between devices  24.3 us (16%)
  starting transfers between devices  18.7 us (12%)
  matrix products  16 us (11%)
  local copies, waits for them, and re-layouts  6.3 us (4%)
  other arithmetic  4.6 us (3%)
  between operations  2.7 us (2%)
    all_to_all x1, blocking collectives, shards(): lax.all_to_all(send.reshape(devices * rows, half), BOTH, 0, 0, tiled=True)  30.2 us
    pallas_call x2, Pallas kernels, backward_half(): pl.pallas_call(lambda *refs: backward_kernel(variables, parts, *refs), in...  17.6 us
    pallas_call x2, Pallas kernels, slope_half(): pl.pallas_call(lambda *refs: slope_kernel(parts, *refs), in_specs=[HBM] *...  17.1 us
    dot_general x2, matrix products, shards(): jnp.dot(d, w.T, preferred_element_type=jnp.float32)  16 us
    all_to_all x1, waiting for transfers between devices, shards(): parts = lax.all_to_all(mine, BOTH, 0, 0, tiled=True)  14.5 us
    pallas_call x2, Pallas kernels, forward_half(): pl.pallas_call(lambda *refs: forward_kernel(first, 4, *refs), in_specs=[W...  9.73 us
    all_to_all x1, starting transfers between devices, shards(): parts = lax.all_to_all(mine, BOTH, 0, 0, tiled=True)  5.73 us
    all_to_all x1, waiting for transfers between devices, shards(): fields = lax.all_to_all(out, 'member', 0, 0, tiled=True)  4.96 us
  transfers between devices with their start and end apart: 6, of which 4 were waited for; matrix products, arithmetic and copies ran while one was open for 11% of the time, Pallas kernels for 20%

profile of v3, /device:TPU:1, one launch (start us, length us, event | category | flops | bytes accessed | tf_op | source)
XLA Modules:
  0.0 150.8 jit_solution(16689934856816438850)
XLA Ops:
  0.6 0.0 copy-start
  0.6 0.0 copy-start.14
  0.7 0.0 copy-start.12
  0.7 0.0 copy-start.11
  0.7 0.8 slice_bitcast_fusion.3
  1.5 0.1 broadcast_in_dim.8
  1.6 30.2 %all_to_all.35 = bf16[128,8,512]{2,1,0:T(8,128)(2,1)S(1)} all-to-all(bf16[128,8,512]{2,1,0:T(8,128)(2,1)S(1)} %bitcast.48), channel_id=1, replica_groups=mesh['member'=8,'grid'=16] {'member','grid'}, dimensions={0} | all-to-all | bytes 2097152 | tf_op jit(solution)/shard_map/all_to_all | solution.py:336
  31.8 0.0 collective-permute-start
  31.9 0.0 copy-done.14
  31.9 0.1 copy.14.refs_4_
  32.0 0.1 fusion.5
  32.1 0.0 copy-start.3
  32.1 0.0 copy-start.8
  32.1 2.3 %copy-done.8 = bf16[1,2048,1024]{2,1,0:T(8,128)(2,1)S(1)} copy-done((bf16[1,2048,1024]{2,1,0:T(8,128)(2,1)S(1)}, bf16[1,2048,1024]{2,1,0:T(8,128)(2,1)}, u32[]{:S(2)}) %copy-start.8) | copy-done | bytes 4194328
  34.5 3.8 %forward_half.2.refs_4_ = f32[8,104,256]{2,1,0:T(8,128)S(1)} custom-call(bf16[2048,1024]{1,0:T(8,128)(2,1)S(1)} %bitcast.45, bf16[1024,512]{1,0:T(8,128)(2,1)S(1)} %bitcast.35, f32[1,512]{1,0:T(1,128)S(1)} %bitcast.37, bf16[112,512]{1,0:T(8,128)(2,1)S(1)} %get-tuple-element.44.refs_3_.refs_4_, f32[104,1]{1,0:T(8,128)S(1)} %copy.14.refs_4_), custom_call_target="tpu_custom_call" | custom-call | flops 2365587456 | bytes 4194304 | tf_op jit(solution)/shard_map/forward_half/pallas_call | solution.py:62
  38.3 0.0 collective-permute-done.refs_1_
  38.3 5.9 %forward_half.3 = f32[8,104,256]{2,1,0:T(8,128)} custom-call(bf16[2048,1024]{1,0:T(8,128)(2,1)S(1)} %bitcast.46, bf16[1024,512]{1,0:T(8,128)(2,1)} %collective-permute-done.refs_1_, f32[1,512]{1,0:T(1,128)S(1)} %bitcast.39, bf16[112,512]{1,0:T(8,128)(2,1)S(1)} %get-tuple-element.45.refs_3_.refs_4_, f32[8,104,256]{2,1,0:T(8,128)S(1)} %forward_half.2.refs_4_), custom_call_target="tpu_custom_call" | custom-call | flops 2365587456 | bytes 4194304 | tf_op jit(solution)/shard_map/forward_half/pallas_call | solution.py:62
  44.3 3.7 %all-to-all-start.1 = ((f32[8,104,256]{2,1,0:T(8,128)}), f32[8,104,256]{2,1,0:T(8,128)S(1)}, u32[]{:S(2)}, u32[]{:S(2)}) async-start(f32[8,104,256]{2,1,0:T(8,128)} %forward_half.3), calls=%async_computation.1 | async-start | bytes 1703936 | tf_op jit(solution)/shard_map/all_to_all | solution.py:358
  48.0 0.0 copy-done
  48.1 0.1 broadcast_multiply_fusion
  48.2 0.0 copy-start.5
  48.2 8.5 %slope_half.2 = (bf16[2048,512]{1,0:T(8,128)(2,1)}, bf16[2048,512]{1,0:T(8,128)(2,1)}) custom-call(bf16[2048,1024]{1,0:T(8,128)(2,1)} %bitcast.41, bf16[1024,512]{1,0:T(8,128)(2,1)} %collective-permute-done.refs_1_, f32[1,512]{1,0:T(1,128)} %bitcast.40), custom_call_target="tpu_custom_call" | custom-call | flops 2147483648 | bytes 8388608 | tf_op jit(solution)/shard_map/slope_half/pallas_call | solution.py:109
  56.7 5.0 %all-to-all-done.1.f_ref = f32[8,104,256]{2,1,0:T(8,128)S(1)} async-done(((f32[8,104,256]{2,1,0:T(8,128)}), f32[8,104,256]{2,1,0:T(8,128)S(1)}, u32[]{:S(2)}, u32[]{:S(2)}) %all-to-all-start.1) | async-done | bytes 852000 | tf_op jit(solution)/shard_map/all_to_all | solution.py:358
  61.7 2.7 %pair_terms.1 = (bf16[8,112,256]{2,1,0:T(8,128)(2,1)}, f32[1,256]{1,0:T(1,128)S(1)}) custom-call(s32[3,8]{1,0:T(4,128)S(1)} %copy-done.5, f32[8,104,256]{2,1,0:T(8,128)S(1)} %all-to-all-done.1.f_ref, f32[104,256]{1,0:T(8,128)S(1)} %pad.17.t_ref, f32[104,256]{1,0:T(8,128)S(1)} %pad.18.s_ref), custom_call_target="tpu_custom_call" | custom-call | tf_op jit(solution)/shard_map/pair_terms/pallas_call | solution.py:312
  64.4 0.6 copy-done.9
  64.9 3.7 %all-to-all-start.2 = ((bf16[8,112,256]{2,1,0:T(8,128)(2,1)}), bf16[8,112,256]{2,1,0:T(8,128)(2,1)S(1)}, u32[]{:S(2)}, u32[]{:S(2)}) async-start(bf16[8,112,256]{2,1,0:T(8,128)(2,1)} %get-tuple-element.28), calls=%async_computation.2 | async-start | bytes 917504 | tf_op jit(solution)/shard_map/all_to_all | solution.py:368
  68.6 8.5 %slope_half.3 = (bf16[2048,512]{1,0:T(8,128)(2,1)}, bf16[2048,512]{1,0:T(8,128)(2,1)}) custom-call(bf16[2048,1024]{1,0:T(8,128)(2,1)} %bitcast.42, bf16[1024,512]{1,0:T(8,128)(2,1)} %bitcast.36, f32[1,512]{1,0:T(1,128)} %bitcast.38), custom_call_target="tpu_custom_call" | custom-call | flops 2147483648 | bytes 8388608 | tf_op jit(solution)/shard_map/slope_half/pallas_call | solution.py:109
  77.1 0.7 all-to-all-done.2.refs_0_
  77.9 0.8 copy-done.10
  78.7 8.7 %backward_half.3 = (bf16[2048,512]{1,0:T(8,128)(2,1)}, bf16[1024,640]{1,0:T(8,128)(2,1)}) custom-call(bf16[8,112,256]{2,1,0:T(8,128)(2,1)} %copy-done.10, bf16[2048,512]{1,0:T(8,128)(2,1)} %get-tuple-element.36.refs_1_, bf16[2048,1024]{1,0:T(8,128)(2,1)} %bitcast.43, bf16[2048,512]{1,0:T(8,128)(2,1)} %get-tuple-element.37.refs_3_, ...), custom_call_target="tpu_custom_call" | custom-call | flops 2617245696 | bytes 10485760 | tf_op jit(solution)/shard_map/backward_half/pallas_call | solution.py:207
  87.4 0.9 collective-permute-start.1
  88.3 8.9 %backward_half.2 = (bf16[2048,512]{1,0:T(8,128)(2,1)}, f32[1024,640]{1,0:T(8,128)}) custom-call(bf16[8,112,256]{2,1,0:T(8,128)(2,1)} %copy-done.10, bf16[2048,512]{1,0:T(8,128)(2,1)} %get-tuple-element.32.refs_1_, bf16[2048,1024]{1,0:T(8,128)(2,1)} %bitcast.44, bf16[2048,512]{1,0:T(8,128)(2,1)} %get-tuple-element.33.refs_3_, bf16[112,512]{1,0:T(8,128)(2,1)} %copy-done.3, ...), custom_call_target="tpu_custom_call" | custom-call | flops 2617245696 | bytes 10485760 | tf_op jit(solution)/shard_map/backward_half/pallas_call | solution.py:207
  97.2 0.0 collective-permute-done.1
  97.2 3.1 %fusion.1 = bf16[128,8,640]{2,1,0:T(8,128)(2,1)} fusion(f32[1024,640]{1,0:T(8,128)} %get-tuple-element.35, bf16[1024,640]{1,0:T(8,128)(2,1)S(1)} %collective-permute-done.1), kind=kLoop, calls=%fused_computation.4 | loop fusion | flops 1966080 | bytes 5242880 | tf_op jit(solution)/shard_map/all_to_all | solution.py:381
  100.2 5.7 %all-to-all-start.3 = ((bf16[128,8,640]{2,1,0:T(8,128)(2,1)}), bf16[128,8,640]{2,1,0:T(8,128)(2,1)S(1)}, u32[]{:S(2)}, u32[]{:S(2)}) async-start(bf16[128,8,640]{2,1,0:T(8,128)(2,1)} %fusion.1), calls=%async_computation.3 | async-start | bytes 2621440 | tf_op jit(solution)/shard_map/all_to_all | solution.py:381
  106.0 0.0 copy-done.2
  106.0 7.2 %fusion.3 = f32[2048,1024]{1,0:T(8,128)} fusion(bf16[2048,512]{1,0:T(8,128)(2,1)} %get-tuple-element.40, bf16[128,8,512]{2,1,0:T(8,128)(2,1)S(1)} %copy-done.2), kind=kOutput, calls=%fused_computation.23 | convolution fusion | flops 2147483648 | bytes 11534336 | tf_op jit(solution)/shard_map/dot_general | solution.py:379
  113.2 14.5 %all-to-all-done.3 = bf16[128,8,640]{2,1,0:T(8,128)(2,1)S(1)} async-done(((bf16[128,8,640]{2,1,0:T(8,128)(2,1)}), bf16[128,8,640]{2,1,0:T(8,128)(2,1)S(1)}, u32[]{:S(2)}, u32[]{:S(2)}) %all-to-all-start.3) | async-done | bytes 1310752 | tf_op jit(solution)/shard_map/all_to_all | solution.py:381
  127.7 0.2 convert_reduce_fusion
  127.9 0.1 pad_maximum_fusion.1
  128.0 0.8 broadcast_in_dim.10
  128.9 4.8 %all-to-all-start.4 = ((f32[128,8,128]{2,1,0:T(8,128)}), f32[128,8,128]{2,1,0:T(8,128)S(1)}, u32[]{:S(2)}, u32[]{:S(2)}) async-start(f32[128,8,128]{2,1,0:T(8,128)} %broadcast_in_dim.10), calls=%async_computation.4 | async-start | bytes 1048576 | tf_op jit(solution)/shard_map/all_to_all | solution.py:386
  133.6 8.7 %fusion = bf16[1,2048,1024]{2,1,0:T(8,128)(2,1)} fusion(f32[2048,1024]{1,0:T(8,128)} %fusion.3, bf16[2048,512]{1,0:T(8,128)(2,1)} %get-tuple-element.41, bf16[1024,512]{1,0:T(8,128)(2,1)} %collective-permute-done.refs_1_), kind=kOutput, calls=%fused_computation.1 | convolution fusion | flops 2151677952 | bytes 15728640 | tf_op jit(solution)/shard_map/dot_general | solution.py:379
  142.4 0.6 maximum_multiply_fusion
  143.0 4.1 %all-to-all-done.4.refs_0_ = f32[128,8,128]{2,1,0:T(8,128)S(1)} async-done(((f32[128,8,128]{2,1,0:T(8,128)}), f32[128,8,128]{2,1,0:T(8,128)S(1)}, u32[]{:S(2)}, u32[]{:S(2)}) %all-to-all-start.4) | async-done | bytes 524320 | tf_op jit(solution)/shard_map/all_to_all | solution.py:386
  147.1 0.9 finish.1
  148.0 0.5 slice.44
  148.5 0.5 fusion.2
  (27 shorter events, 0.2 us)
Async XLA Ops:
  0.6 47.3 %copy-start = (f32[100,2048]{1,0:T(8,128)S(1)}, f32[100,2048]{1,0:T(8,128)}, u32[]{:S(2)}) copy-start(f32[100,2048]{1,0:T(8,128)} %param.13) | copy-start | bytes 2457604
  0.6 31.2 %copy-start.14 = (f32[100]{0:T(128)S(1)}, f32[100]{0:T(128)}, u32[]{:S(2)}) copy-start(f32[100]{0:T(128)} %param.12) | copy-start | bytes 1204
  0.7 31.3 %copy-start.12 = (f32[1024]{0:T(1024)S(1)}, f32[1024]{0:T(1024)}, u32[]{:S(2)}) copy-start(f32[1024]{0:T(1024)} %param.10) | copy-start | bytes 12292
  0.7 31.4 %copy-start.11 = (bf16[100,1024]{1,0:T(8,128)(2,1)S(1)}, bf16[100,1024]{1,0:T(8,128)(2,1)}, u32[]{:S(2)}) copy-start(bf16[100,1024]{1,0:T(8,128)(2,1)} %param.11) | copy-start | bytes 614404
  31.8 6.5 %copy-start.1 = (bf16[128,8,512]{2,1,0:T(8,128)(2,1)}, bf16[128,8,512]{2,1,0:T(8,128)(2,1)S(1)}, u32[]{:S(2)}) copy-start(bf16[128,8,512]{2,1,0:T(8,128)(2,1)S(1)} %all_to_all.35) | copy-start | bytes 3145732
  31.8 6.5 %collective-permute-start = (bf16[1024,512]{1,0:T(8,128)(2,1)S(1)}, bf16[1024,512]{1,0:T(8,128)(2,1)}, u32[]{:S(2)}, u32[]{:S(2)}) collective-permute-start(bf16[1024,512]{1,0:T(8,128)(2,1)S(1)} %bitcast.34), channel_id=1, source_target_pairs={{0,1},{1,0},{2,3},{3,2},{4,5},{5,4},{6,7},{7,6},{8,9},{9,8},{10,11... | collective-permute-start | bytes 3145736 | tf_op jit(solution)/shard_map/ppermute | solution.py:337
  32.1 6.2 %copy-start.6 = (f32[512]{0:T(512)}, f32[512]{0:T(512)S(1)}, u32[]{:S(2)}) copy-start(f32[512]{0:T(512)S(1)} %get-tuple-element.52) | copy-start | bytes 6148
  32.1 6.3 %copy-start.7 = (f32[512]{0:T(512)}, f32[512]{0:T(512)S(1)}, u32[]{:S(2)}) copy-start(f32[512]{0:T(512)S(1)} %get-tuple-element.53) | copy-start | bytes 6148
  32.1 6.2 %copy-start.3 = (bf16[112,512]{1,0:T(8,128)(2,1)}, bf16[112,512]{1,0:T(8,128)(2,1)S(1)}, u32[]{:S(2)}) copy-start(bf16[112,512]{1,0:T(8,128)(2,1)S(1)} %get-tuple-element.44.refs_3_.refs_4_) | copy-start | bytes 344068
  32.1 6.2 %copy-start.4 = (bf16[112,512]{1,0:T(8,128)(2,1)}, bf16[112,512]{1,0:T(8,128)(2,1)S(1)}, u32[]{:S(2)}) copy-start(bf16[112,512]{1,0:T(8,128)(2,1)S(1)} %get-tuple-element.45.refs_3_.refs_4_) | copy-start | bytes 344068
  32.1 2.4 %copy-start.8 = (bf16[1,2048,1024]{2,1,0:T(8,128)(2,1)S(1)}, bf16[1,2048,1024]{2,1,0:T(8,128)(2,1)}, u32[]{:S(2)}) copy-start(bf16[1,2048,1024]{2,1,0:T(8,128)(2,1)} %param.8) | copy-start | bytes 12582916
  44.3 3.8 %copy-start.13 = (f32[100]{0:T(128)S(1)}, f32[100]{0:T(128)}, u32[]{:S(2)}) copy-start(f32[100]{0:T(128)} %param.14) | copy-start | bytes 1204
  44.3 17.4 %all-to-all-start.1 = ((f32[8,104,256]{2,1,0:T(8,128)}), f32[8,104,256]{2,1,0:T(8,128)S(1)}, u32[]{:S(2)}, u32[]{:S(2)}) async-start(f32[8,104,256]{2,1,0:T(8,128)} %forward_half.3), calls=%async_computation.1 | async-start | bytes 1703936 | tf_op jit(solution)/shard_map/all_to_all | solution.py:358
  48.2 13.5 %copy-start.5 = (s32[3,8]{1,0:T(4,128)S(1)}, s32[3,8]{1,0:T(4,128)}, u32[]{:S(2)}) copy-start(s32[3,8]{1,0:T(4,128)} %plan_ref.1) | copy-start | bytes 292
  64.4 0.6 copy-start.9
  64.9 12.9 %all-to-all-start.2 = ((bf16[8,112,256]{2,1,0:T(8,128)(2,1)}), bf16[8,112,256]{2,1,0:T(8,128)(2,1)S(1)}, u32[]{:S(2)}, u32[]{:S(2)}) async-start(bf16[8,112,256]{2,1,0:T(8,128)(2,1)} %get-tuple-element.28), calls=%async_computation.2 | async-start | bytes 917504 | tf_op jit(solution)/shard_map/all_to_all | solution.py:368
  77.9 0.8 copy-start.10
  87.4 9.8 %collective-permute-start.1 = (bf16[1024,640]{1,0:T(8,128)(2,1)}, bf16[1024,640]{1,0:T(8,128)(2,1)S(1)}, u32[]{:S(2)}, u32[]{:S(2)}) collective-permute-start(bf16[1024,640]{1,0:T(8,128)(2,1)} %get-tuple-element.38), channel_id=1, source_target_pairs={{0,1},{1,0},{2,3},{3,2},{4,5},{5,4},{6,7},{7,6},{8,9},{9,8},{10,11... | collective-permute-start | bytes 3932168 | tf_op jit(solution)/shard_map/ppermute | solution.py:373
  100.2 5.7 %copy-start.2 = (bf16[128,8,512]{2,1,0:T(8,128)(2,1)S(1)}, bf16[128,8,512]{2,1,0:T(8,128)(2,1)}, u32[]{:S(2)}) copy-start(bf16[128,8,512]{2,1,0:T(8,128)(2,1)} %copy-done.1) | copy-start | bytes 3145732
  100.2 27.5 %all-to-all-start.3 = ((bf16[128,8,640]{2,1,0:T(8,128)(2,1)}), bf16[128,8,640]{2,1,0:T(8,128)(2,1)S(1)}, u32[]{:S(2)}, u32[]{:S(2)}) async-start(bf16[128,8,640]{2,1,0:T(8,128)(2,1)} %fusion.1), calls=%async_computation.3 | async-start | bytes 2621440 | tf_op jit(solution)/shard_map/all_to_all | solution.py:381
  128.9 18.2 %all-to-all-start.4 = ((f32[128,8,128]{2,1,0:T(8,128)}), f32[128,8,128]{2,1,0:T(8,128)S(1)}, u32[]{:S(2)}, u32[]{:S(2)}) async-start(f32[128,8,128]{2,1,0:T(8,128)} %broadcast_in_dim.10), calls=%async_computation.4 | async-start | bytes 1048576 | tf_op jit(solution)/shard_map/all_to_all | solution.py:386

commit v4 on v3

--- a/solution.py
+++ b/solution.py
@@ -125,120 +125,188 @@
     )(lat, w, b)
 
 
-def backward_kernel(variables, parts, *refs):
-    cot_ref, g_ref, lat_ref, act_ref, o, tail, dpre_ref, pack_ref = refs[:8]
-    cot, g, lat, act, dpre_v, pack, table, sems, out_sems = refs[8:]
+def cotangent_kernel(variables, parts, *refs):
+    core, cot_ref = refs[:2]
+    g_refs, act_refs = refs[2:4], refs[4:6]
+    o_refs, tail = refs[6:8], refs[8]
+    dpre_refs, pack_ref = refs[9:11], refs[11]
+    cot, g, act, dpre_v, pack, table, sems, out_sems = refs[12:]
     blocks, rows, block = cot.shape
-    points, half = g.shape
-    width = lat.shape[1]
-    kind = pack.dtype
+    points, half = g_refs[0].shape
     tile = points // parts
-    cut = width // parts
-    slices = [slice(i * tile, (i + 1) * tile) for i in range(parts)]
-
-    def fetch(i):
-        sl = slices[i]
+    steps = [(h, i) for h in range(2) for i in range(parts)]
+
+    def fetch(n):
+        h, i = steps[n]
+        sl = slice(i * tile, (i + 1) * tile)
         return (
-            load(g_ref.at[sl], g.at[sl], sems.at[1 + 2 * i]),
-            load(act_ref.at[sl], act.at[sl], sems.at[2 + 2 * i]),
+            load(g_refs[h].at[sl], g.at[h, sl], sems.at[1 + 2 * n]),
+            load(act_refs[h].at[sl], act.at[h, sl], sems.at[2 + 2 * n]),
         )
 
-    def fetch_lat(i):
-        cols = pl.ds(i * cut, cut)
-        return load(lat_ref.at[:, cols], lat.at[:, cols], sems.at[1 + 2 * parts + i])
-
     ready_cot = load(cot_ref, cot, sems.at[0])
-    ready = [fetch(0), fetch(1)]
-    ready_lat = []
+    ready = [fetch(0), fetch(1), fetch(2)]
     ready_cot.wait()
-    b1, w2 = None, None
     out = []
-    for i in range(parts):
-        for copy in ready[i]:
+    for n, (h, i) in enumerate(steps):
+        if i == 0:
+            b1, w2 = None, None
+        for copy in ready[n]:
             copy.wait()
-        if i + 2 < parts:
-            ready.append(fetch(i + 2))
-        else:
-            ready_lat.append(fetch_lat(i + 2 - parts))
+        if n + 3 < len(steps):
+            ready.append(fetch(n + 3))
         for q in range(i * blocks // parts, (i + 1) * blocks // parts):
             sl = slice(q * block, (q + 1) * block)
             dact = lax.dot_general(
-                cot[q], o[...], (((0,), (0,)), ((), ())), preferred_element_type=jnp.float32
+                cot[q], o_refs[h][...], (((0,), (0,)), ((), ())), preferred_element_type=jnp.float32
             )
-            dpre = dact * g[sl, :].astype(jnp.float32)
-            dpre_v[sl, :] = dpre.astype(jnp.bfloat16)
+            dpre = dact * g[h, sl, :].astype(jnp.float32)
+            dpre_v[h, sl, :] = dpre.astype(jnp.bfloat16)
             s = jnp.sum(dpre.reshape(-1, 8, half), axis=0)
             b1 = s if b1 is None else b1 + s
-            a = jnp.dot(cot[q], act[sl, :], preferred_element_type=jnp.float32)
+            a = jnp.dot(cot[q], act[h, sl, :], preferred_element_type=jnp.float32)
             w2 = a if w2 is None else w2 + a
         sl = slice(i * tile, (i + 1) * tile)
-        out.append(load(dpre_v.at[sl], dpre_ref.at[sl], out_sems.at[i]))
-    table[...] = jnp.zeros_like(table)
-    table[:rows, :] = w2
-    table[variables : variables + 1, :] = jnp.sum(b1, axis=0, keepdims=True)
-    if kind == jnp.float32:
-        table[variables + 1 : variables + 2, : tail.shape[1]] = tail[...]
-    side = half // 8
-    lanes = half // (2 * side)
-    pack[:, half + side :] = jnp.zeros((width, 128 - side), kind)
-    for i in range(parts):
-        ready_lat[i].wait()
-        if i + 2 < parts:
-            ready_lat.append(fetch_lat(i + 2))
-        sl = slice(i * cut, (i + 1) * cut)
-        pack[sl, :half] = lax.dot_general(
-            lat[:, sl], dpre_v[...], (((0,), (0,)), ((), ())), preferred_element_type=jnp.float32
-        ).astype(kind)
-        for unit in range(i * cut // 16, (i + 1) * cut // 16):
-            r, c = unit // lanes, unit % lanes
-            piece = table[8 * r : 8 * r + 8, 2 * side * c : 2 * side * (c + 1)]
-            both = jnp.concatenate([piece[:, :side], piece[:, side:]], axis=0)
-            pack[16 * unit : 16 * unit + 16, half : half + side] = both.astype(kind)
-        out.append(load(pack.at[sl], pack_ref.at[sl], out_sems.at[parts + i]))
+        out.append(load(dpre_v.at[h, sl], dpre_refs[h].at[sl], out_sems.at[n]))
+        if i == parts - 1:
+            table[h] = jnp.zeros(table.shape[1:], jnp.float32)
+            table[h, :rows, :] = w2
+            table[h, variables : variables + 1, :] = jnp.sum(b1, axis=0, keepdims=True)
+            if h == 0:
+                table[h, variables + 1 : variables + 2, : tail.shape[1]] = tail[...]
+    lanes = half // 128
+    low = core[0] == 0
+    for unit in range(pack.shape[0] // 16):
+        r, c = unit // lanes, unit % lanes
+        pieces = []
+        for h in range(2):
+            piece = table[h, 8 * r : 8 * r + 8, 128 * c : 128 * (c + 1)]
+            pieces.append(jnp.concatenate([piece[:, :64], piece[:, 64:]], axis=0))
+        first = jnp.where(low, pieces[0], pieces[1])
+        second = jnp.where(low, pieces[1], pieces[0])
+        pack[16 * unit : 16 * unit + 16, :] = jnp.concatenate([first, second], axis=1).astype(jnp.bfloat16)
+    out.append(load(pack, pack_ref, out_sems.at[len(steps)]))
     for copy in out:
         copy.wait()
 
 
-def backward_half(cot, o, g, lat, act, tail, variables, kind):
-    blocks, rows, block = cot.shape
-    points, half = g.shape
+def cotangents(core, cot, gs, acts, o_halves, tail, variables, width):
+    points, half = gs[0].shape
+    parts = 4
+    row = shape((points, half), jnp.bfloat16)
+    return pl.pallas_call(
+        lambda *refs: cotangent_kernel(variables, parts, *refs),
+        in_specs=[pl.BlockSpec(memory_space=pltpu.SMEM)] + [HBM] * 5 + [WHOLE] * 3,
+        out_specs=[HBM] * 3,
+        out_shape=[row, row, shape((width, 128), jnp.bfloat16)],
+        scratch_shapes=[
+            pltpu.VMEM(cot.shape, jnp.bfloat16),
+            pltpu.VMEM((2, points, half), jnp.bfloat16),
+            pltpu.VMEM((2, points, half), jnp.bfloat16),
+            pltpu.VMEM((2, points, half), jnp.bfloat16),
+            pltpu.VMEM((width, 128), jnp.bfloat16),
+            pltpu.VMEM((2, width // 8, half), jnp.float32),
+            pltpu.SemaphoreType.DMA((1 + 4 * parts,)),
+            pltpu.SemaphoreType.DMA((1 + 2 * parts,)),
+        ],
+        compiler_params=pltpu.CompilerParams(vmem_limit_bytes=VMEM_BYTES),
+        cost_estimate=cost(8 * points * half * cot.shape[1], points * 12 * half),
+        name="cotangents",
+    )(core, cot, *gs, *acts, *o_halves, tail)
+
+
+def weight_kernel(parts, lat_ref, d_ref, out_ref, lat, d, total, sems, out_sems):
+    width = lat.shape[1]
+    cut = width // parts
+
+    def fetch(i):
+        cols = pl.ds(i * cut, cut)
+        return load(lat_ref.at[:, cols], lat.at[:, cols], sems.at[i])
+
+    ready_d = load(d_ref, d, sems.at[parts])
+    ready = [fetch(0), fetch(1)]
+    ready_d.wait()
+    out = []
+    for i in range(parts):
+        ready[i].wait()
+        if i + 2 < parts:
+            ready.append(fetch(i + 2))
+        sl = slice(i * cut, (i + 1) * cut)
+        total[sl, :] = lax.dot_general(
+            lat[:, sl], d[...], (((0,), (0,)), ((), ())), preferred_element_type=jnp.float32
+        ).astype(total.dtype)
+        out.append(load(total.at[sl], out_ref.at[sl], out_sems.at[i]))
+    for copy in out:
+        copy.wait()
+
+
+def weight_half(lat, d, kind):
+    points, half = d.shape
     width = lat.shape[1]
     parts = 4
     return pl.pallas_call(
-        lambda *refs: backward_kernel(variables, parts, *refs),
-        in_specs=[HBM] * 4 + [WHOLE] * 2,
-        out_specs=[HBM] * 2,
-        out_shape=[shape((points, half), jnp.bfloat16), shape((width, half + 128), kind)],
+        lambda *refs: weight_kernel(parts, *refs),
+        in_specs=[HBM] * 2,
+        out_specs=HBM,
+        out_shape=shape((width, half), kind),
         scratch_shapes=[
-            pltpu.VMEM(cot.shape, jnp.bfloat16),
-            pltpu.VMEM(g.shape, jnp.bfloat16),
             pltpu.VMEM(lat.shape, jnp.bfloat16),
-            pltpu.VMEM(act.shape, jnp.bfloat16),
-            pltpu.VMEM((points, half), jnp.bfloat16),
-            pltpu.VMEM((width, half + 128), kind),
-            pltpu.VMEM((width // 8, half), jnp.float32),
-            pltpu.SemaphoreType.DMA((1 + 3 * parts,)),
-            pltpu.SemaphoreType.DMA((2 * parts,)),
+            pltpu.VMEM(d.shape, jnp.bfloat16),
+            pltpu.VMEM((width, half), kind),
+            pltpu.SemaphoreType.DMA((parts + 1,)),
+            pltpu.SemaphoreType.DMA((parts,)),
         ],
         compiler_params=pltpu.CompilerParams(vmem_limit_bytes=VMEM_BYTES),
-        cost_estimate=cost(2 * points * half * (width + 2 * rows), points * (2 * width + 6 * half)),
-        name="backward_half",
-    )(cot, g, lat, act, o, tail)
-
-
-def finish_kernel(kappa, all_ref, w2_ref, b1_ref, tail_ref):
+        cost_estimate=cost(2 * points * half * width, points * 2 * (width + half) + width * half * 4),
+        name="weight_half",
+    )(lat, d)
+
+
+def join_kernel(high, flag, table, mine, got, out_ref):
+    rows, half = mine.shape
+    acc = table[0:16, :].astype(jnp.float32)
+    for u in range(1, rows // 16):
+        acc = acc + table[16 * u : 16 * u + 16, :].astype(jnp.float32)
+    small = acc[:8] + acc[8:]
+    rest = small - small.astype(jnp.bfloat16).astype(jnp.float32)
+    line = lax.broadcasted_iota(jnp.int32, small.shape, 0)
+    low = jnp.broadcast_to(rest[high : high + 1], small.shape)
+    small = jnp.where((line == high + 1) & (flag[0] == 1), low, small)
+    both = jnp.concatenate([small, small], axis=0).astype(jnp.bfloat16)
+    for u in range(rows // 16):
+        sl = slice(16 * u, 16 * u + 16)
+        out_ref[sl, :half] = (mine[sl, :] + got[sl, :].astype(jnp.float32)).astype(jnp.bfloat16)
+        out_ref[sl, half:] = both
+
+
+def join(flag, table, mine, got, high):
+    rows, half = mine.shape
+    return pl.pallas_call(
+        lambda *refs: join_kernel(high, *refs),
+        in_specs=[pl.BlockSpec(memory_space=pltpu.SMEM)] + [WHOLE] * 3,
+        out_specs=WHOLE,
+        out_shape=shape((rows, half + 128), jnp.bfloat16),
+        compiler_params=pltpu.CompilerParams(vmem_limit_bytes=VMEM_SMALL),
+        name="join",
+    )(flag, table, mine, got)
+
+
+def finish_kernel(kappa, share, all_ref, own_ref, w2_ref, b1_ref, b2_ref, loss_ref, tail):
     variables, width = w2_ref.shape
     half = width // 2
     lanes = half // 128
-    side = 64
-    for r in range(-(-(variables + 2) // 8)):
+    acc = all_ref[0:16, :half].astype(jnp.float32)
+    for u in range(1, all_ref.shape[0] // 16):
+        acc = acc + all_ref[16 * u : 16 * u + 16, :half].astype(jnp.float32)
+    own_ref[:, :half] = acc[:8] * kappa
+    own_ref[:, half:] = acc[8:] * kappa
+    for r in range(-(-(variables + 3) // 8)):
         for c in range(lanes):
-            a = all_ref[r * 2 * lanes + 2 * c]
-            b = all_ref[r * 2 * lanes + 2 * c + 1]
+            u = r * lanes + c
+            pair_rows = all_ref[16 * u : 16 * u + 16, half:].astype(jnp.float32)
+            a, b = pair_rows[:8], pair_rows[8:]
             for h in range(2):
-                piece = jnp.concatenate(
-                    [a[:, h * side : (h + 1) * side], b[:, h * side : (h + 1) * side]], axis=1
-                )
+                piece = jnp.concatenate([a[:, 64 * h : 64 * h + 64], b[:, 64 * h : 64 * h + 64]], axis=1)
                 cols = slice(h * half + 128 * c, h * half + 128 * (c + 1))
                 low = 8 * r
                 keep = min(8, variables - low)
@@ -247,21 +315,25 @@
                 at = variables - low
                 if 0 <= at < 8:
                     b1_ref[:, cols] = piece[at : at + 1] * kappa
-                at = variables + 1 - low
-                if 0 <= at < 8:
-                    tail_ref[:, cols] = piece[at : at + 1]
-
-
-def finish(everyone, variables, width, kappa):
-    return pl.pallas_call(
-        lambda *refs: finish_kernel(kappa, *refs),
+                    tail[:, cols] = piece[at + 1 : at + 2] + piece[at + 2 : at + 3]
+    both = tail[:, :half] + tail[:, half:]
+    b2_ref[...] = both[:, :128] * kappa
+    loss_ref[...] = both[:, 128:256] * share
+
+
+def finish(everyone, rows, variables, width, kappa, share):
+    return pl.pallas_call(
+        lambda *refs: finish_kernel(kappa, share, *refs),
         in_specs=[WHOLE],
-        out_specs=[WHOLE] * 3,
+        out_specs=[WHOLE] * 5,
         out_shape=[
+            shape((rows, width), jnp.float32),
             shape((variables, width), jnp.float32),
             shape((1, width), jnp.float32),
-            shape((1, width), jnp.float32),
+            shape((1, 128), jnp.float32),
+            shape((1, 128), jnp.float32),
         ],
+        scratch_shapes=[pltpu.VMEM((1, width), jnp.float32)],
         compiler_params=pltpu.CompilerParams(vmem_limit_bytes=VMEM_SMALL),
         name="finish",
     )(everyone)
@@ -367,34 +439,32 @@
     cot, tail = pair(plan, fields, target, scale_map)
     back = lax.all_to_all(cot, "member", 0, 0, tiled=True)
     back, act0, g0 = lax.optimization_barrier((back, act0, g0))
-    d1, pack1 = backward_half(
-        back, o_halves[1], g1, hidden_in, act1, tail, variables, jnp.bfloat16
-    )
-    got = lax.ppermute(pack1, BOTH, swap)
-    d0, pack0 = backward_half(
-        back, o_halves[0], g0, hidden_in, act0, tail, variables, jnp.float32
-    )
-    mine = (pack0 + got.astype(jnp.float32)).astype(jnp.bfloat16)
+    place = member * grid_count + grid_index
+    tail_row = variables + 1
+    flag = (place // 8 == tail_row // 8).astype(jnp.int32)[None]
+    d0, d1, pack = cotangents(
+        core[None], back, (g0, g1), (act0, act1), o_halves, tail, variables, width
+    )
+    tables = lax.all_to_all(pack, BOTH, 0, 0, tiled=True)
+    got = lax.ppermute(weight_half(hidden_in, d1, jnp.bfloat16), BOTH, swap)
+    mine = weight_half(hidden_in, d0, jnp.float32)
+    chunks = join(flag, tables, mine, got, tail_row % 8)
+    chunks, d0, d1 = lax.optimization_barrier((chunks, d0, d1))
+    parts = lax.all_to_all(chunks, BOTH, 0, 0, tiled=True)
     grad_hidden = sum(
         jnp.dot(d, w.T, preferred_element_type=jnp.float32) for d, w in zip((d0, d1), w_halves)
     ).astype(jnp.bfloat16)
-    parts = lax.all_to_all(mine, BOTH, 0, 0, tiled=True)
-    summed = jnp.sum(parts.reshape(devices // 2, 2, rows, -1).astype(jnp.float32), axis=0)
-    own_rows = jnp.concatenate([summed[0, :, :half], summed[1, :, :half]], axis=1)
-    small = jnp.concatenate([summed[0, :, half : half + 64], summed[1, :, half : half + 64]], axis=1)
-    spread_small = jnp.broadcast_to(small[None], (devices,) + small.shape)
-    everyone = lax.all_to_all(spread_small, BOTH, 0, 0)
     kappa = 4.0 / math.sqrt(members * total)
-    grad_out, grad_bias, tails = finish(everyone, variables, width, kappa)
-    tails = tails[0, :half] + tails[0, half:]
-    loss = tails[128] / (members * total * variables)
+    own_rows, grad_out, grad_bias, grad_b_out, loss = finish(
+        parts, rows, variables, width, kappa, 1.0 / (members * total * variables)
+    )
     return (
-        loss,
+        loss[0, 0],
         grad_hidden[None],
-        own_rows * kappa,
+        own_rows,
         grad_bias[0],
         grad_out,
-        tails[:variables] * kappa,
+        grad_b_out[0, :variables],
     )
 
 

time: 152 us -> 141 us (0.928)
  matrix products: 16 us -> 9 us
  other arithmetic: 4.6 us -> 0.13 us
  Pallas kernels: 48 us -> 50.3 us
  between operations: 2.7 us -> 0.98 us
    dot_general x2, matrix products: 16 us -> 9 us  [shards(): jnp.dot(d, w.T, preferred_element_type=jnp.float32)]
    all_to_all x1 -> x0, other arithmetic: 3.05 us -> none  [shards(): parts = lax.all_to_all(mine, BOTH, 0, 0, tiled=True)]
    pallas_call x3 -> x5, Pallas kernels: 18.5 us -> 20.8 us  [the longest x2 11.4 us: weight_half(): pl.pallas_call(lambda *refs: weight_kernel(parts, *refs), in_specs=[HBM]...]
    unnamed x30 -> x34, local copies, waits for them, and re-layouts: 3.78 us -> 5.39 us
  transfers between devices with their start and end apart: 6 -> 6, of which waited for: 4 -> 4; matrix products, arithmetic and copies ran while one was open for 11% -> 7% of each run, Pallas kernels for 20% -> 19%
where the time goes in v4:
time: 141 us; the launch traced here: 140 us
  Pallas kernels  50.3 us (36%)
  blocking collectives  30.2 us (21%)
  waiting for transfers between devices  23.4 us (17%)
  starting transfers between devices  18.5 us (13%)
  matrix products  9 us (6%)
  local copies, waits for them, and re-layouts  7.07 us (5%)
    all_to_all x1, blocking collectives, shards(): lax.all_to_all(send.reshape(devices * rows, half), BOTH, 0, 0, tiled=True)  30.2 us
    pallas_call x2, Pallas kernels, slope_half(): pl.pallas_call(lambda *refs: slope_kernel(parts, *refs), in_specs=[HBM] *...  17.2 us
    all_to_all x1, waiting for transfers between devices, shards(): parts = lax.all_to_all(chunks, BOTH, 0, 0, tiled=True)  12.7 us
    pallas_call x2, Pallas kernels, weight_half(): pl.pallas_call(lambda *refs: weight_kernel(parts, *refs), in_specs=[HBM]...  11.4 us
    pallas_call x2, Pallas kernels, forward_half(): pl.pallas_call(lambda *refs: forward_kernel(first, 4, *refs), in_specs=[W...  9.7 us
    dot_general x2, matrix products, shards(): jnp.dot(d, w.T, preferred_element_type=jnp.float32)  9 us
    pallas_call x1, Pallas kernels, cotangents(): pl.pallas_call(lambda *refs: cotangent_kernel(variables, parts, *refs), i...  7.19 us
    all_to_all x1, starting transfers between devices, shards(): tables = lax.all_to_all(pack, BOTH, 0, 0, tiled=True)  5.71 us
  transfers between devices with their start and end apart: 6, of which 4 were waited for; matrix products, arithmetic and copies ran while one was open for 7% of the time, Pallas kernels for 19%

profile of v4, /device:TPU:1, one launch (start us, length us, event | category | flops | bytes accessed | tf_op | source)
XLA Modules:
  0.0 139.7 jit_solution(4730228465744723438)
XLA Ops:
  0.6 0.0 copy-start
  0.6 0.0 copy-start.16
  0.7 0.0 copy-start.14
  0.7 0.8 slice_bitcast_fusion.1
  1.5 0.1 broadcast_in_dim.26
  1.6 30.2 %all_to_all.43 = bf16[128,8,512]{2,1,0:T(8,128)(2,1)S(1)} all-to-all(bf16[128,8,512]{2,1,0:T(8,128)(2,1)S(1)} %bitcast.44), channel_id=1, replica_groups=mesh['member'=8,'grid'=16] {'member','grid'}, dimensions={0} | all-to-all | bytes 2097152 | tf_op jit(solution)/shard_map/all_to_all | solution.py:408
  31.8 0.0 collective-permute-start
  31.9 0.1 copy.14.refs_4_
  32.0 0.1 fusion.2
  32.1 0.0 copy-start.5
  32.1 0.0 copy-start.6
  32.1 0.0 copy-start.2
  32.1 2.3 %copy-done.2 = bf16[1,2048,1024]{2,1,0:T(8,128)(2,1)S(1)} copy-done((bf16[1,2048,1024]{2,1,0:T(8,128)(2,1)S(1)}, bf16[1,2048,1024]{2,1,0:T(8,128)(2,1)}, u32[]{:S(2)}) %copy-start.2) | copy-done | bytes 4194328
  34.5 3.8 %forward_half.2.refs_4_ = f32[8,104,256]{2,1,0:T(8,128)S(1)} custom-call(bf16[2048,1024]{1,0:T(8,128)(2,1)S(1)} %bitcast.34, bf16[1024,512]{1,0:T(8,128)(2,1)S(1)} %bitcast.38, f32[1,512]{1,0:T(1,128)S(1)} %bitcast.40, bf16[112,512]{1,0:T(8,128)(2,1)S(1)} %get-tuple-element.52.refs_3_.refs_6_, f32[104,1]{1,0:T(8,128)S(1)} %copy.14.refs_4_), custom_call_target="tpu_custom_call" | custom-call | flops 2365587456 | bytes 4194304 | tf_op jit(solution)/shard_map/forward_half/pallas_call | solution.py:62
  38.3 0.0 copy-done.3
  38.3 0.0 copy-done.8
  38.3 0.0 copy-done.5
  38.3 0.0 collective-permute-done.refs_1_
  38.4 0.0 copy-start.15
  38.4 5.9 %forward_half.3 = f32[8,104,256]{2,1,0:T(8,128)} custom-call(bf16[2048,1024]{1,0:T(8,128)(2,1)S(1)} %bitcast.35, bf16[1024,512]{1,0:T(8,128)(2,1)} %collective-permute-done.refs_1_, f32[1,512]{1,0:T(1,128)S(1)} %bitcast.42, bf16[112,512]{1,0:T(8,128)(2,1)S(1)} %get-tuple-element.53.refs_3_.refs_7_, f32[8,104,256]{2,1,0:T(8,128)S(1)} %forward_half.2.refs_4_), custom_call_target="tpu_custom_call" | custom-call | flops 2365587456 | bytes 4194304 | tf_op jit(solution)/shard_map/forward_half/pallas_call | solution.py:62
  44.3 3.6 %all-to-all-start.1 = ((f32[8,104,256]{2,1,0:T(8,128)}), f32[8,104,256]{2,1,0:T(8,128)S(1)}, u32[]{:S(2)}, u32[]{:S(2)}) async-start(f32[8,104,256]{2,1,0:T(8,128)} %forward_half.3), calls=%async_computation.1 | async-start | bytes 1703936 | tf_op jit(solution)/shard_map/all_to_all | solution.py:430
  47.9 0.1 broadcast_multiply_fusion
  48.0 0.0 copy-start.7
  48.1 8.6 %slope_half.2 = (bf16[2048,512]{1,0:T(8,128)(2,1)}, bf16[2048,512]{1,0:T(8,128)(2,1)}) custom-call(bf16[2048,1024]{1,0:T(8,128)(2,1)} %bitcast.30, bf16[1024,512]{1,0:T(8,128)(2,1)} %collective-permute-done.refs_1_, f32[1,512]{1,0:T(1,128)} %bitcast.43), custom_call_target="tpu_custom_call" | custom-call | flops 2147483648 | bytes 8388608 | tf_op jit(solution)/shard_map/slope_half/pallas_call | solution.py:109
  56.7 4.9 %all-to-all-done.1.f_ref = f32[8,104,256]{2,1,0:T(8,128)S(1)} async-done(((f32[8,104,256]{2,1,0:T(8,128)}), f32[8,104,256]{2,1,0:T(8,128)S(1)}, u32[]{:S(2)}, u32[]{:S(2)}) %all-to-all-start.1) | async-done | bytes 852000 | tf_op jit(solution)/shard_map/all_to_all | solution.py:430
  61.6 2.6 %pair_terms.1 = (bf16[8,112,256]{2,1,0:T(8,128)(2,1)}, f32[1,256]{1,0:T(1,128)S(1)}) custom-call(s32[3,8]{1,0:T(4,128)S(1)} %copy-done.7, f32[8,104,256]{2,1,0:T(8,128)S(1)} %all-to-all-done.1.f_ref, f32[104,256]{1,0:T(8,128)S(1)} %pad.17.t_ref, f32[104,256]{1,0:T(8,128)S(1)} %pad.18.s_ref), custom_call_target="tpu_custom_call" | custom-call | tf_op jit(solution)/shard_map/pair_terms/pallas_call | solution.py:384
  64.2 0.6 copy-done.10
  64.7 3.7 %all-to-all-start.2 = ((bf16[8,112,256]{2,1,0:T(8,128)(2,1)}), bf16[8,112,256]{2,1,0:T(8,128)(2,1)S(1)}, u32[]{:S(2)}, u32[]{:S(2)}) async-start(bf16[8,112,256]{2,1,0:T(8,128)(2,1)} %get-tuple-element.32), calls=%async_computation.2 | async-start | bytes 917504 | tf_op jit(solution)/shard_map/all_to_all | solution.py:440
  68.4 8.5 %slope_half.3 = (bf16[2048,512]{1,0:T(8,128)(2,1)}, bf16[2048,512]{1,0:T(8,128)(2,1)}) custom-call(bf16[2048,1024]{1,0:T(8,128)(2,1)} %bitcast.31, bf16[1024,512]{1,0:T(8,128)(2,1)} %bitcast.39, f32[1,512]{1,0:T(1,128)} %bitcast.41), custom_call_target="tpu_custom_call" | custom-call | flops 2147483648 | bytes 8388608 | tf_op jit(solution)/shard_map/slope_half/pallas_call | solution.py:109
  77.0 0.7 all-to-all-done.2.refs_1_
  77.7 0.8 copy-done.12
  78.5 7.2 %cotangents.1 = (bf16[2048,512]{1,0:T(8,128)(2,1)}, bf16[2048,512]{1,0:T(8,128)(2,1)}, bf16[1024,128]{1,0:T(8,128)(2,1)}) custom-call(s32[1]{0:T(128)} %bitcast.1.refs_0_, bf16[8,112,256]{2,1,0:T(8,128)(2,1)} %copy-done.12, bf16[2048,512]{1,0:T(8,128)(2,1)} %get-tuple-element.36.refs_2_, bf16[2048,512]{1,0:T(8,128)(2,1)} %get-tuple-element.37.refs_3_, ...), custom_call_target="tpu_custom_call" | custom-call | flops 939524096 | bytes 12582912 | tf_op jit(solution)/shard_map/cotangents/pallas_call | solution.py:197
  85.7 5.7 %weight_half.3 = bf16[1024,512]{1,0:T(8,128)(2,1)} custom-call(bf16[2048,1024]{1,0:T(8,128)(2,1)} %bitcast.32, bf16[2048,512]{1,0:T(8,128)(2,1)} %get-tuple-element.47.refs_1_), custom_call_target="tpu_custom_call" | custom-call | flops 2147483648 | bytes 8388608 | tf_op jit(solution)/shard_map/weight_half/pallas_call | solution.py:247
  91.4 0.9 collective-permute-start.1
  92.3 5.7 %all-to-all-start.3 = ((bf16[128,8,128]{2,1,0:T(8,128)(2,1)}), bf16[128,8,128]{2,1,0:T(8,128)(2,1)S(1)}, u32[]{:S(2)}, u32[]{:S(2)}) async-start(bf16[128,8,128]{2,1,0:T(8,128)(2,1)} %bitcast.10), calls=%async_computation.3 | async-start | bytes 524288 | tf_op jit(solution)/shard_map/all_to_all | solution.py:448
  98.0 5.7 %weight_half.2.refs_2_ = f32[1024,512]{1,0:T(8,128)} custom-call(bf16[2048,1024]{1,0:T(8,128)(2,1)} %bitcast.33, bf16[2048,512]{1,0:T(8,128)(2,1)} %get-tuple-element.46.refs_1_), custom_call_target="tpu_custom_call" | custom-call | flops 2147483648 | bytes 8388608 | tf_op jit(solution)/shard_map/weight_half/pallas_call | solution.py:247
  103.7 5.1 %all-to-all-done.3 = bf16[128,8,128]{2,1,0:T(8,128)(2,1)S(1)} async-done(((bf16[128,8,128]{2,1,0:T(8,128)(2,1)}), bf16[128,8,128]{2,1,0:T(8,128)(2,1)S(1)}, u32[]{:S(2)}, u32[]{:S(2)}) %all-to-all-start.3) | async-done | bytes 262176 | tf_op jit(solution)/shard_map/all_to_all | solution.py:448
  108.9 0.0 collective-permute-done.1.refs_3_
  108.9 1.6 %copy-done.1 = f32[1024,512]{1,0:T(8,128)S(1)} copy-done((f32[1024,512]{1,0:T(8,128)S(1)}, f32[1024,512]{1,0:T(8,128)}, u32[]{:S(2)}) %copy-start.1) | copy-done | bytes 2097176
  110.5 1.4 join.1
  111.8 4.7 %all-to-all-start.4 = ((bf16[128,8,640]{2,1,0:T(8,128)(2,1)}), bf16[128,8,640]{2,1,0:T(8,128)(2,1)S(1)}, u32[]{:S(2)}, u32[]{:S(2)}) async-start(bf16[128,8,640]{2,1,0:T(8,128)(2,1)} %bitcast.12), calls=%async_computation.4 | async-start | bytes 2621440 | tf_op jit(solution)/shard_map/all_to_all | solution.py:453
  116.5 0.0 copy-start.4
  116.5 0.0 copy-start.11
  116.5 4.5 %fusion.3 = f32[2048,1024]{1,0:T(8,128)S(1)} fusion(bf16[2048,512]{1,0:T(8,128)(2,1)} %get-tuple-element.47.refs_1_, bf16[1024,512]{1,0:T(8,128)(2,1)} %collective-permute-done.refs_1_), kind=kOutput, calls=%fused_computation.14 | convolution fusion | flops 2147483648 | bytes 11534336 | tf_op jit(solution)/shard_map/dot_general | solution.py:455
  121.0 4.5 %fusion = bf16[1,2048,1024]{2,1,0:T(8,128)(2,1)} fusion(f32[2048,1024]{1,0:T(8,128)S(1)} %fusion.3, bf16[2048,512]{1,0:T(8,128)(2,1)S(1)} %copy-done.11, bf16[128,8,512]{2,1,0:T(8,128)(2,1)S(1)} %copy-done.4), kind=kOutput, calls=%fused_computation.1 | convolution fusion | flops 2151677952 | bytes 15728640 | tf_op jit(solution)/shard_map/dot_general | solution.py:455
  125.5 12.7 %all-to-all-done.4 = bf16[128,8,640]{2,1,0:T(8,128)(2,1)S(1)} async-done(((bf16[128,8,640]{2,1,0:T(8,128)(2,1)}), bf16[128,8,640]{2,1,0:T(8,128)(2,1)S(1)}, u32[]{:S(2)}, u32[]{:S(2)}) %all-to-all-start.4) | async-done | bytes 1310752 | tf_op jit(solution)/shard_map/all_to_all | solution.py:453
  138.2 0.9 finish.1
  139.1 0.5 slice_bitcast_fusion.2
  (24 shorter events, 0.1 us)
Async XLA Ops:
  0.6 47.4 %copy-start = (f32[100,2048]{1,0:T(8,128)S(1)}, f32[100,2048]{1,0:T(8,128)}, u32[]{:S(2)}) copy-start(f32[100,2048]{1,0:T(8,128)} %param.13) | copy-start | bytes 2457604
  0.6 31.2 %copy-start.16 = (f32[100]{0:T(128)S(1)}, f32[100]{0:T(128)}, u32[]{:S(2)}) copy-start(f32[100]{0:T(128)} %param.12) | copy-start | bytes 1204
  0.7 31.3 %copy-start.14 = (f32[1024]{0:T(1024)S(1)}, f32[1024]{0:T(1024)}, u32[]{:S(2)}) copy-start(f32[1024]{0:T(1024)} %param.10) | copy-start | bytes 12292
  0.7 31.4 %copy-start.13 = (bf16[100,1024]{1,0:T(8,128)(2,1)S(1)}, bf16[100,1024]{1,0:T(8,128)(2,1)}, u32[]{:S(2)}) copy-start(bf16[100,1024]{1,0:T(8,128)(2,1)} %param.11) | copy-start | bytes 614404
  31.8 6.5 %copy-start.3 = (bf16[128,8,512]{2,1,0:T(8,128)(2,1)}, bf16[128,8,512]{2,1,0:T(8,128)(2,1)S(1)}, u32[]{:S(2)}) copy-start(bf16[128,8,512]{2,1,0:T(8,128)(2,1)S(1)} %all_to_all.43) | copy-start | bytes 3145732
  31.8 6.5 %collective-permute-start = (bf16[1024,512]{1,0:T(8,128)(2,1)S(1)}, bf16[1024,512]{1,0:T(8,128)(2,1)}, u32[]{:S(2)}, u32[]{:S(2)}) collective-permute-start(bf16[1024,512]{1,0:T(8,128)(2,1)S(1)} %bitcast.37), channel_id=1, source_target_pairs={{0,1},{1,0},{2,3},{3,2},{4,5},{5,4},{6,7},{7,6},{8,9},{9,8},{10,11... | collective-permute-start | bytes 3145736 | tf_op jit(solution)/shard_map/ppermute | solution.py:409
  32.1 6.2 %copy-start.8 = (f32[512]{0:T(512)}, f32[512]{0:T(512)S(1)}, u32[]{:S(2)}) copy-start(f32[512]{0:T(512)S(1)} %get-tuple-element.56) | copy-start | bytes 6148
  32.1 6.3 %copy-start.9 = (f32[512]{0:T(512)}, f32[512]{0:T(512)S(1)}, u32[]{:S(2)}) copy-start(f32[512]{0:T(512)S(1)} %get-tuple-element.57) | copy-start | bytes 6148
  32.1 6.2 %copy-start.5 = (bf16[112,512]{1,0:T(8,128)(2,1)}, bf16[112,512]{1,0:T(8,128)(2,1)S(1)}, u32[]{:S(2)}) copy-start(bf16[112,512]{1,0:T(8,128)(2,1)S(1)} %get-tuple-element.52.refs_3_.refs_6_) | copy-start | bytes 344068
  32.1 6.2 %copy-start.6 = (bf16[112,512]{1,0:T(8,128)(2,1)}, bf16[112,512]{1,0:T(8,128)(2,1)S(1)}, u32[]{:S(2)}) copy-start(bf16[112,512]{1,0:T(8,128)(2,1)S(1)} %get-tuple-element.53.refs_3_.refs_7_) | copy-start | bytes 344068
  32.1 2.4 %copy-start.2 = (bf16[1,2048,1024]{2,1,0:T(8,128)(2,1)S(1)}, bf16[1,2048,1024]{2,1,0:T(8,128)(2,1)}, u32[]{:S(2)}) copy-start(bf16[1,2048,1024]{2,1,0:T(8,128)(2,1)} %param.8) | copy-start | bytes 12582916
  38.4 9.5 %copy-start.15 = (f32[100]{0:T(128)S(1)}, f32[100]{0:T(128)}, u32[]{:S(2)}) copy-start(f32[100]{0:T(128)} %param.14) | copy-start | bytes 1204
  44.3 17.3 %all-to-all-start.1 = ((f32[8,104,256]{2,1,0:T(8,128)}), f32[8,104,256]{2,1,0:T(8,128)S(1)}, u32[]{:S(2)}, u32[]{:S(2)}) async-start(f32[8,104,256]{2,1,0:T(8,128)} %forward_half.3), calls=%async_computation.1 | async-start | bytes 1703936 | tf_op jit(solution)/shard_map/all_to_all | solution.py:430
  48.0 13.5 %copy-start.7 = (s32[3,8]{1,0:T(4,128)S(1)}, s32[3,8]{1,0:T(4,128)}, u32[]{:S(2)}) copy-start(s32[3,8]{1,0:T(4,128)} %plan_ref.1) | copy-start | bytes 292
  64.2 0.6 copy-start.10
  64.7 12.9 %all-to-all-start.2 = ((bf16[8,112,256]{2,1,0:T(8,128)(2,1)}), bf16[8,112,256]{2,1,0:T(8,128)(2,1)S(1)}, u32[]{:S(2)}, u32[]{:S(2)}) async-start(bf16[8,112,256]{2,1,0:T(8,128)(2,1)} %get-tuple-element.32), calls=%async_computation.2 | async-start | bytes 917504 | tf_op jit(solution)/shard_map/all_to_all | solution.py:440
  77.7 0.8 copy-start.12
  91.4 17.5 %collective-permute-start.1 = (bf16[1024,512]{1,0:T(8,128)(2,1)}, bf16[1024,512]{1,0:T(8,128)(2,1)S(1)}, u32[]{:S(2)}, u32[]{:S(2)}) collective-permute-start(bf16[1024,512]{1,0:T(8,128)(2,1)} %weight_half.3), channel_id=1, source_target_pairs={{0,1},{1,0},{2,3},{3,2},{4,5},{5,4},{6,7},{7,6},{8,9},{9,8},{10,11... | collective-permute-start | bytes 3145736 | tf_op jit(solution)/shard_map/ppermute | solution.py:449
  92.3 16.6 %all-to-all-start.3 = ((bf16[128,8,128]{2,1,0:T(8,128)(2,1)}), bf16[128,8,128]{2,1,0:T(8,128)(2,1)S(1)}, u32[]{:S(2)}, u32[]{:S(2)}) async-start(bf16[128,8,128]{2,1,0:T(8,128)(2,1)} %bitcast.10), calls=%async_computation.3 | async-start | bytes 524288 | tf_op jit(solution)/shard_map/all_to_all | solution.py:448
  108.9 1.6 %copy-start.1 = (f32[1024,512]{1,0:T(8,128)S(1)}, f32[1024,512]{1,0:T(8,128)}, u32[]{:S(2)}) copy-start(f32[1024,512]{1,0:T(8,128)} %weight_half.2.refs_2_) | copy-start | bytes 6291460
  111.8 26.4 %all-to-all-start.4 = ((bf16[128,8,640]{2,1,0:T(8,128)(2,1)}), bf16[128,8,640]{2,1,0:T(8,128)(2,1)S(1)}, u32[]{:S(2)}, u32[]{:S(2)}) async-start(bf16[128,8,640]{2,1,0:T(8,128)(2,1)} %bitcast.12), calls=%async_computation.4 | async-start | bytes 2621440 | tf_op jit(solution)/shard_map/all_to_all | solution.py:453
  116.5 4.5 %copy-start.4 = (bf16[128,8,512]{2,1,0:T(8,128)(2,1)S(1)}, bf16[128,8,512]{2,1,0:T(8,128)(2,1)}, u32[]{:S(2)}) copy-start(bf16[128,8,512]{2,1,0:T(8,128)(2,1)} %copy-done.3) | copy-start | bytes 3145732
  116.5 4.5 %copy-start.11 = (bf16[2048,512]{1,0:T(8,128)(2,1)S(1)}, bf16[2048,512]{1,0:T(8,128)(2,1)}, u32[]{:S(2)}) copy-start(bf16[2048,512]{1,0:T(8,128)(2,1)} %get-tuple-element.46.refs_1_) | copy-start | bytes 6291460

commit v5 on v4

--- a/solution.py
+++ b/solution.py
@@ -17,6 +17,7 @@
 GELU_B = 0.044715
 WHOLE = pl.BlockSpec(memory_space=pltpu.VMEM)
 HBM = pl.BlockSpec(memory_space=pltpu.HBM)
+ANY = pl.BlockSpec(memory_space=pl.ANY)
 
 
 def shape(dims, kind):
@@ -60,7 +61,7 @@
     points, width = lat.shape
     half = w.shape[1]
     return pl.pallas_call(
-        lambda *refs: forward_kernel(first, 4, *refs),
+        lambda *refs: forward_kernel(first, 2, *refs),
         in_specs=[WHOLE] * 5,
         out_specs=WHOLE,
         out_shape=shape((blocks, rows, points // blocks), jnp.float32),
@@ -80,13 +81,11 @@
         return load(lat_ref.at[slices[i]], lat.at[slices[i]], sems.at[i])
 
     ready_w = load(w_ref, w, sems.at[parts])
-    ready = [fetch(0)]
+    ready = [fetch(i) for i in range(parts)]
     ready_w.wait()
     out = []
     for i, sl in enumerate(slices):
         ready[i].wait()
-        if i + 1 < parts:
-            ready.append(fetch(i + 1))
         for n in range(0, half, 256):
             cols = slice(n, n + 256)
             pre = jnp.dot(lat[sl, :], w[:, cols], preferred_element_type=jnp.float32) + b[:, cols]
@@ -127,10 +126,10 @@
 
 def cotangent_kernel(variables, parts, *refs):
     core, cot_ref = refs[:2]
-    g_refs, act_refs = refs[2:4], refs[4:6]
-    o_refs, tail = refs[6:8], refs[8]
-    dpre_refs, pack_ref = refs[9:11], refs[11]
-    cot, g, act, dpre_v, pack, table, sems, out_sems = refs[12:]
+    g_refs, act_refs, lat_ref = refs[2:4], refs[4:6], refs[6]
+    o_refs, tail = refs[7:9], refs[9]
+    dpre_refs, pack_ref, give_ref = refs[10:12], refs[12], refs[13]
+    cot, g, act, dpre_v, pack, table, lat, give, sems, lat_sem, out_sems, give_sems = refs[14:]
     blocks, rows, block = cot.shape
     points, half = g_refs[0].shape
     tile = points // parts
@@ -145,7 +144,8 @@
         )
 
     ready_cot = load(cot_ref, cot, sems.at[0])
-    ready = [fetch(0), fetch(1), fetch(2)]
+    ready = [fetch(n) for n in range(len(steps))]
+    ready_lat = load(lat_ref, lat, lat_sem)
     ready_cot.wait()
     out = []
     for n, (h, i) in enumerate(steps):
@@ -153,8 +153,6 @@
             b1, w2 = None, None
         for copy in ready[n]:
             copy.wait()
-        if n + 3 < len(steps):
-            ready.append(fetch(n + 3))
         for q in range(i * blocks // parts, (i + 1) * blocks // parts):
             sl = slice(q * block, (q + 1) * block)
             dact = lax.dot_general(
@@ -186,19 +184,28 @@
         second = jnp.where(low, pieces[1], pieces[0])
         pack[16 * unit : 16 * unit + 16, :] = jnp.concatenate([first, second], axis=1).astype(jnp.bfloat16)
     out.append(load(pack, pack_ref, out_sems.at[len(steps)]))
+    ready_lat.wait()
+    cut = lat.shape[1] // parts
+    for m in range(parts):
+        at = slice(m * cut, (m + 1) * cut)
+        give[at, :] = lax.dot_general(
+            lat[:, at], dpre_v[1], (((0,), (0,)), ((), ())), preferred_element_type=jnp.float32
+        ).astype(jnp.bfloat16)
+        out.append(load(give.at[at], give_ref.at[at], give_sems.at[m]))
     for copy in out:
         copy.wait()
 
 
-def cotangents(core, cot, gs, acts, o_halves, tail, variables, width):
+def cotangents(core, cot, gs, acts, lat, o_halves, tail, variables):
+    width = lat.shape[1]
     points, half = gs[0].shape
     parts = 4
     row = shape((points, half), jnp.bfloat16)
     return pl.pallas_call(
         lambda *refs: cotangent_kernel(variables, parts, *refs),
-        in_specs=[pl.BlockSpec(memory_space=pltpu.SMEM)] + [HBM] * 5 + [WHOLE] * 3,
-        out_specs=[HBM] * 3,
-        out_shape=[row, row, shape((width, 128), jnp.bfloat16)],
+        in_specs=[pl.BlockSpec(memory_space=pltpu.SMEM), ANY] + [HBM] * 5 + [WHOLE] * 3,
+        out_specs=[HBM] * 4,
+        out_shape=[row, row, shape((width, 128), jnp.bfloat16), shape((width, half), jnp.bfloat16)],
         scratch_shapes=[
             pltpu.VMEM(cot.shape, jnp.bfloat16),
             pltpu.VMEM((2, points, half), jnp.bfloat16),
@@ -206,63 +213,86 @@
             pltpu.VMEM((2, points, half), jnp.bfloat16),
             pltpu.VMEM((width, 128), jnp.bfloat16),
             pltpu.VMEM((2, width // 8, half), jnp.float32),
+            pltpu.VMEM(lat.shape, jnp.bfloat16),
+            pltpu.VMEM((width, half), jnp.bfloat16),
             pltpu.SemaphoreType.DMA((1 + 4 * parts,)),
+            pltpu.SemaphoreType.DMA,
             pltpu.SemaphoreType.DMA((1 + 2 * parts,)),
+            pltpu.SemaphoreType.DMA((parts,)),
         ],
         compiler_params=pltpu.CompilerParams(vmem_limit_bytes=VMEM_BYTES),
-        cost_estimate=cost(8 * points * half * cot.shape[1], points * 12 * half),
+        cost_estimate=cost(2 * points * half * (4 * cot.shape[1] + width), points * (12 * half + 2 * width)),
         name="cotangents",
-    )(core, cot, *gs, *acts, *o_halves, tail)
-
-
-def weight_kernel(parts, lat_ref, d_ref, out_ref, lat, d, total, sems, out_sems):
+    )(core, cot, *gs, *acts, lat, *o_halves, tail)
+
+
+def weight_kernel(parts, fused, *refs):
+    lat_ref, d_ref = refs[:2]
+    got_ref = refs[2] if fused else None
+    out_ref, lat, d, acc, total, sems, out_sems = refs[2 + fused :][:7]
     width = lat.shape[1]
+    points, half = d.shape
+    tile = points // parts
     cut = width // parts
-
-    def fetch(i):
-        cols = pl.ds(i * cut, cut)
-        return load(lat_ref.at[:, cols], lat.at[:, cols], sems.at[i])
-
-    ready_d = load(d_ref, d, sems.at[parts])
-    ready = [fetch(0), fetch(1)]
-    ready_d.wait()
+    ready = []
+    for i in range(parts):
+        sl = slice(i * tile, (i + 1) * tile)
+        ready.append((load(d_ref.at[sl], d.at[sl], sems.at[2 * i]), load(lat_ref.at[sl], lat.at[sl], sems.at[2 * i + 1])))
+    if fused:
+        got = refs[-1]
+        ready_got = load(got_ref, got, sems.at[2 * parts])
     out = []
     for i in range(parts):
-        ready[i].wait()
-        if i + 2 < parts:
-            ready.append(fetch(i + 2))
-        sl = slice(i * cut, (i + 1) * cut)
-        total[sl, :] = lax.dot_general(
-            lat[:, sl], d[...], (((0,), (0,)), ((), ())), preferred_element_type=jnp.float32
-        ).astype(total.dtype)
-        out.append(load(total.at[sl], out_ref.at[sl], out_sems.at[i]))
+        for copy in ready[i]:
+            copy.wait()
+        if fused and i == parts - 1:
+            ready_got.wait()
+        sl = slice(i * tile, (i + 1) * tile)
+        for m in range(parts):
+            at = slice(m * cut, (m + 1) * cut)
+            term = lax.dot_general(
+                lat[sl, at], d[sl, :], (((0,), (0,)), ((), ())), preferred_element_type=jnp.float32
+            )
+            if i > 0:
+                term = term + acc[at, :]
+            if i < parts - 1:
+                acc[at, :] = term
+                continue
+            if fused:
+                term = term + got[at, :].astype(jnp.float32)
+            total[at, :] = term.astype(jnp.bfloat16)
+            out.append(load(total.at[at], out_ref.at[at], out_sems.at[m]))
     for copy in out:
         copy.wait()
 
 
-def weight_half(lat, d, kind):
+def weight_half(lat, d, *got):
     points, half = d.shape
     width = lat.shape[1]
     parts = 4
+    fused = len(got)
+    small = pltpu.VMEM((width, half), jnp.bfloat16)
     return pl.pallas_call(
-        lambda *refs: weight_kernel(parts, *refs),
-        in_specs=[HBM] * 2,
-        out_specs=HBM,
-        out_shape=shape((width, half), kind),
+        lambda *refs: weight_kernel(parts, fused, *refs),
+        in_specs=[HBM] * 2 + [ANY] * fused,
+        out_specs=ANY,
+        out_shape=shape((width, half), jnp.bfloat16),
         scratch_shapes=[
             pltpu.VMEM(lat.shape, jnp.bfloat16),
             pltpu.VMEM(d.shape, jnp.bfloat16),
-            pltpu.VMEM((width, half), kind),
-            pltpu.SemaphoreType.DMA((parts + 1,)),
+            pltpu.VMEM((width, half), jnp.float32),
+            small,
+            pltpu.SemaphoreType.DMA((2 * parts + 1,)),
             pltpu.SemaphoreType.DMA((parts,)),
-        ],
+        ]
+        + [small] * fused,
         compiler_params=pltpu.CompilerParams(vmem_limit_bytes=VMEM_BYTES),
         cost_estimate=cost(2 * points * half * width, points * 2 * (width + half) + width * half * 4),
         name="weight_half",
-    )(lat, d)
-
-
-def join_kernel(high, flag, table, mine, got, out_ref):
+    )(lat, d, *got)
+
+
+def join_kernel(high, flag, table, mine, out_ref):
     rows, half = mine.shape
     acc = table[0:16, :].astype(jnp.float32)
     for u in range(1, rows // 16):
@@ -275,20 +305,20 @@
     both = jnp.concatenate([small, small], axis=0).astype(jnp.bfloat16)
     for u in range(rows // 16):
         sl = slice(16 * u, 16 * u + 16)
-        out_ref[sl, :half] = (mine[sl, :] + got[sl, :].astype(jnp.float32)).astype(jnp.bfloat16)
+        out_ref[sl, :half] = mine[sl, :]
         out_ref[sl, half:] = both
 
 
-def join(flag, table, mine, got, high):
+def join(flag, table, mine, high):
     rows, half = mine.shape
     return pl.pallas_call(
         lambda *refs: join_kernel(high, *refs),
-        in_specs=[pl.BlockSpec(memory_space=pltpu.SMEM)] + [WHOLE] * 3,
+        in_specs=[pl.BlockSpec(memory_space=pltpu.SMEM)] + [WHOLE] * 2,
         out_specs=WHOLE,
         out_shape=shape((rows, half + 128), jnp.bfloat16),
         compiler_params=pltpu.CompilerParams(vmem_limit_bytes=VMEM_SMALL),
         name="join",
-    )(flag, table, mine, got)
+    )(flag, table, mine)
 
 
 def finish_kernel(kappa, share, all_ref, own_ref, w2_ref, b1_ref, b2_ref, loss_ref, tail):
@@ -442,13 +472,13 @@
     place = member * grid_count + grid_index
     tail_row = variables + 1
     flag = (place // 8 == tail_row // 8).astype(jnp.int32)[None]
-    d0, d1, pack = cotangents(
-        core[None], back, (g0, g1), (act0, act1), o_halves, tail, variables, width
+    d0, d1, pack, give = cotangents(
+        core[None], back, (g0, g1), (act0, act1), hidden_in, o_halves, tail, variables
     )
     tables = lax.all_to_all(pack, BOTH, 0, 0, tiled=True)
-    got = lax.ppermute(weight_half(hidden_in, d1, jnp.bfloat16), BOTH, swap)
-    mine = weight_half(hidden_in, d0, jnp.float32)
-    chunks = join(flag, tables, mine, got, tail_row % 8)
+    got = lax.ppermute(give, BOTH, swap)
+    mine = weight_half(hidden_in, d0, got)
+    chunks = join(flag, tables, mine, tail_row % 8)
     chunks, d0, d1 = lax.optimization_barrier((chunks, d0, d1))
     parts = lax.all_to_all(chunks, BOTH, 0, 0, tiled=True)
     grad_hidden = sum(

time: 141 us -> 137 us (0.972)
  Pallas kernels: 50.3 us -> 45.9 us
    pallas_call x4 -> x3, Pallas kernels: 21.1 us -> 14.1 us  [the longest x2 9.27 us: forward_half(): pl.pallas_call(lambda *refs: forward_kernel(first, 2, *refs), in_specs=[W...]
    pallas_call x1, Pallas kernels: 7.19 us -> 10.7 us  [cotangents(): pl.pallas_call(lambda *refs: cotangent_kernel(variables, parts, *refs), i...]
    unnamed x34 -> x36, local copies, waits for them, and re-layouts: 5.39 us -> 5.94 us
  transfers between devices with their start and end apart: 6 -> 6, of which waited for: 4 -> 4; matrix products, arithmetic and copies ran while one was open for 7% -> 8% of each run, Pallas kernels for 19% -> 18%
where the time goes in v5:
time: 137 us; the launch traced here: 136 us
  Pallas kernels  45.9 us (34%)
  blocking collectives  30.2 us (22%)
  waiting for transfers between devices  23.3 us (17%)
  starting transfers between devices  18.2 us (13%)
  matrix products  9.93 us (7%)
  local copies, waits for them, and re-layouts  7.62 us (6%)
    all_to_all x1, blocking collectives, shards(): lax.all_to_all(send.reshape(devices * rows, half), BOTH, 0, 0, tiled=True)  30.2 us
    pallas_call x2, Pallas kernels, slope_half(): pl.pallas_call(lambda *refs: slope_kernel(parts, *refs), in_specs=[HBM] *...  16.2 us
    all_to_all x1, waiting for transfers between devices, shards(): parts = lax.all_to_all(chunks, BOTH, 0, 0, tiled=True)  11.8 us
    pallas_call x1, Pallas kernels, cotangents(): pl.pallas_call(lambda *refs: cotangent_kernel(variables, parts, *refs), i...  10.7 us
    dot_general x2, matrix products, shards(): jnp.dot(d, w.T, preferred_element_type=jnp.float32)  9.93 us
    pallas_call x2, Pallas kernels, forward_half(): pl.pallas_call(lambda *refs: forward_kernel(first, 2, *refs), in_specs=[W...  9.27 us
    unnamed x36, local copies, waits for them, and re-layouts  5.94 us
    all_to_all x1, waiting for transfers between devices, shards(): fields = lax.all_to_all(out, 'member', 0, 0, tiled=True)  5.34 us
  transfers between devices with their start and end apart: 6, of which 4 were waited for; matrix products, arithmetic and copies ran while one was open for 8% of the time, Pallas kernels for 18%

profile of v5, /device:TPU:1, one launch (start us, length us, event | category | flops | bytes accessed | tf_op | source)
XLA Modules:
  0.0 136.2 jit_solution(15627247021307649181)
XLA Ops:
  0.6 0.0 copy-start
  0.6 0.0 copy-start.17
  0.7 0.0 copy-start.14
  0.7 0.0 copy-start.13
  0.7 0.8 slice_bitcast_fusion.1
  1.5 0.1 broadcast_in_dim.26
  1.6 30.2 %all_to_all.43 = bf16[128,8,512]{2,1,0:T(8,128)(2,1)S(1)} all-to-all(bf16[128,8,512]{2,1,0:T(8,128)(2,1)S(1)} %bitcast.44), channel_id=1, replica_groups=mesh['member'=8,'grid'=16] {'member','grid'}, dimensions={0} | all-to-all | bytes 2097152 | tf_op jit(solution)/shard_map/all_to_all | solution.py:438
  31.8 0.0 collective-permute-start
  31.9 0.0 copy-done.17
  31.9 0.1 copy.14.refs_4_
  32.0 0.0 copy-done.14
  32.0 0.1 fusion.3
  32.1 0.0 copy-start.5
  32.1 0.0 copy-start.6
  32.1 0.0 copy-start.1
  32.1 2.3 %copy-done.1 = bf16[1,2048,1024]{2,1,0:T(8,128)(2,1)S(1)} copy-done((bf16[1,2048,1024]{2,1,0:T(8,128)(2,1)S(1)}, bf16[1,2048,1024]{2,1,0:T(8,128)(2,1)}, u32[]{:S(2)}) %copy-start.1) | copy-done | bytes 4194328
  34.5 3.6 %forward_half.2.refs_4_ = f32[8,104,256]{2,1,0:T(8,128)S(1)} custom-call(bf16[2048,1024]{1,0:T(8,128)(2,1)S(1)} %bitcast.33, bf16[1024,512]{1,0:T(8,128)(2,1)S(1)} %bitcast.37, f32[1,512]{1,0:T(1,128)S(1)} %bitcast.40, bf16[112,512]{1,0:T(8,128)(2,1)S(1)} %get-tuple-element.54.refs_3_.refs_7_, f32[104,1]{1,0:T(8,128)S(1)} %copy.14.refs_4_), custom_call_target="tpu_custom_call" | custom-call | flops 2365587456 | bytes 4194304 | tf_op jit(solution)/shard_map/forward_half/pallas_call | solution.py:63
  38.1 0.0 collective-permute-done.refs_1_
  38.1 0.0 copy-start.15
  38.1 5.7 %forward_half.3 = f32[8,104,256]{2,1,0:T(8,128)} custom-call(bf16[2048,1024]{1,0:T(8,128)(2,1)S(1)} %bitcast.34, bf16[1024,512]{1,0:T(8,128)(2,1)} %collective-permute-done.refs_1_, f32[1,512]{1,0:T(1,128)S(1)} %bitcast.42, bf16[112,512]{1,0:T(8,128)(2,1)S(1)} %get-tuple-element.55.refs_3_.refs_8_, f32[8,104,256]{2,1,0:T(8,128)S(1)} %forward_half.2.refs_4_), custom_call_target="tpu_custom_call" | custom-call | flops 2365587456 | bytes 4194304 | tf_op jit(solution)/shard_map/forward_half/pallas_call | solution.py:63
  43.8 3.6 %all-to-all-start.1 = ((f32[8,104,256]{2,1,0:T(8,128)}), f32[8,104,256]{2,1,0:T(8,128)S(1)}, u32[]{:S(2)}, u32[]{:S(2)}) async-start(f32[8,104,256]{2,1,0:T(8,128)} %forward_half.3), calls=%async_computation.1 | async-start | bytes 1703936 | tf_op jit(solution)/shard_map/all_to_all | solution.py:460
  47.5 0.1 broadcast_multiply_fusion
  47.6 0.0 copy-done
  47.6 0.0 copy-start.7
  47.6 8.1 %slope_half.2 = (bf16[2048,512]{1,0:T(8,128)(2,1)}, bf16[2048,512]{1,0:T(8,128)(2,1)}) custom-call(bf16[2048,1024]{1,0:T(8,128)(2,1)} %bitcast.29, bf16[1024,512]{1,0:T(8,128)(2,1)} %collective-permute-done.refs_1_, f32[1,512]{1,0:T(1,128)} %bitcast.43), custom_call_target="tpu_custom_call" | custom-call | flops 2147483648 | bytes 8388608 | tf_op jit(solution)/shard_map/slope_half/pallas_call | solution.py:108
  55.8 5.3 %all-to-all-done.1.f_ref = f32[8,104,256]{2,1,0:T(8,128)S(1)} async-done(((f32[8,104,256]{2,1,0:T(8,128)}), f32[8,104,256]{2,1,0:T(8,128)S(1)}, u32[]{:S(2)}, u32[]{:S(2)}) %all-to-all-start.1) | async-done | bytes 852000 | tf_op jit(solution)/shard_map/all_to_all | solution.py:460
  61.1 2.6 %pair_terms.1 = (bf16[8,112,256]{2,1,0:T(8,128)(2,1)}, f32[1,256]{1,0:T(1,128)S(1)}) custom-call(s32[3,8]{1,0:T(4,128)S(1)} %copy-done.7, f32[8,104,256]{2,1,0:T(8,128)S(1)} %all-to-all-done.1.f_ref, f32[104,256]{1,0:T(8,128)S(1)} %pad.17.t_ref, f32[104,256]{1,0:T(8,128)S(1)} %pad.18.s_ref), custom_call_target="tpu_custom_call" | custom-call | tf_op jit(solution)/shard_map/pair_terms/pallas_call | solution.py:414
  63.7 0.6 copy-done.10
  64.3 3.7 %all-to-all-start.2 = ((bf16[8,112,256]{2,1,0:T(8,128)(2,1)}), bf16[8,112,256]{2,1,0:T(8,128)(2,1)S(1)}, u32[]{:S(2)}, u32[]{:S(2)}) async-start(bf16[8,112,256]{2,1,0:T(8,128)(2,1)} %get-tuple-element.33), calls=%async_computation.2 | async-start | bytes 917504 | tf_op jit(solution)/shard_map/all_to_all | solution.py:470
  68.0 8.1 %slope_half.3 = (bf16[2048,512]{1,0:T(8,128)(2,1)}, bf16[2048,512]{1,0:T(8,128)(2,1)}) custom-call(bf16[2048,1024]{1,0:T(8,128)(2,1)} %bitcast.30, bf16[1024,512]{1,0:T(8,128)(2,1)} %bitcast.38, f32[1,512]{1,0:T(1,128)} %bitcast.41), custom_call_target="tpu_custom_call" | custom-call | flops 2147483648 | bytes 8388608 | tf_op jit(solution)/shard_map/slope_half/pallas_call | solution.py:108
  76.1 1.2 all-to-all-done.2.refs_1_
  77.3 0.8 copy-done.11
  78.0 10.7 %cotangents.1 = (bf16[2048,512]{1,0:T(8,128)(2,1)}, bf16[2048,512]{1,0:T(8,128)(2,1)}, bf16[1024,128]{1,0:T(8,128)(2,1)}, bf16[1024,512]{1,0:T(8,128)(2,1)}) custom-call(s32[1]{0:T(128)} %bitcast.1.refs_0_, bf16[8,112,256]{2,1,0:T(8,128)(2,1)} %copy-done.11, bf16[2048,512]{1,0:T(8,128)(2,1)} %get-tuple-element.37.refs_2_, ...), custom_call_target="tpu_custom_call" | custom-call | flops 3087007744 | bytes 16777216 | tf_op jit(solution)/shard_map/cotangents/pallas_call | solution.py:204
  88.7 0.9 collective-permute-start.1
  89.6 5.3 %all-to-all-start.3 = ((bf16[128,8,128]{2,1,0:T(8,128)(2,1)}), bf16[128,8,128]{2,1,0:T(8,128)(2,1)S(1)}, u32[]{:S(2)}, u32[]{:S(2)}) async-start(bf16[128,8,128]{2,1,0:T(8,128)(2,1)} %bitcast.45), calls=%async_computation.3 | async-start | bytes 524288 | tf_op jit(solution)/shard_map/all_to_all | solution.py:478
  94.9 0.0 collective-permute-done.1.refs_2_
  94.9 0.0 copy-start.12
  94.9 1.0 copy-done.12
  95.9 4.9 %weight_half.1.refs_2_ = bf16[1024,512]{1,0:T(8,128)(2,1)} custom-call(bf16[2048,1024]{1,0:T(8,128)(2,1)} %bitcast.32, bf16[2048,512]{1,0:T(8,128)(2,1)} %get-tuple-element.48.refs_1_, bf16[1024,512]{1,0:T(8,128)(2,1)} %copy-done.12), custom_call_target="tpu_custom_call" | custom-call | flops 2147483648 | bytes 8388608 | tf_op jit(solution)/shard_map/weight_half/pallas_call | solution.py:275
  100.8 5.0 %all-to-all-done.3 = bf16[128,8,128]{2,1,0:T(8,128)(2,1)S(1)} async-done(((bf16[128,8,128]{2,1,0:T(8,128)(2,1)}), bf16[128,8,128]{2,1,0:T(8,128)(2,1)S(1)}, u32[]{:S(2)}, u32[]{:S(2)}) %all-to-all-start.3) | async-done | bytes 262176 | tf_op jit(solution)/shard_map/all_to_all | solution.py:478
  105.8 1.2 copy-done.2
  107.0 1.3 join.1
  108.2 4.8 %all-to-all-start.4 = ((bf16[128,8,640]{2,1,0:T(8,128)(2,1)}), bf16[128,8,640]{2,1,0:T(8,128)(2,1)S(1)}, u32[]{:S(2)}, u32[]{:S(2)}) async-start(bf16[128,8,640]{2,1,0:T(8,128)(2,1)} %bitcast.12), calls=%async_computation.4 | async-start | bytes 2621440 | tf_op jit(solution)/shard_map/all_to_all | solution.py:483
  113.1 4.2 %fusion.1 = f32[2048,1024]{1,0:T(8,128)S(1)} fusion(bf16[2048,512]{1,0:T(8,128)(2,1)} %get-tuple-element.48.refs_1_, bf16[128,8,512]{2,1,0:T(8,128)(2,1)S(1)} %copy-done.4), kind=kOutput, calls=%fused_computation.12 | convolution fusion | flops 2147483648 | bytes 11534336 | tf_op jit(solution)/shard_map/dot_general | solution.py:485
  117.3 5.7 %fusion = bf16[1,2048,1024]{2,1,0:T(8,128)(2,1)} fusion(f32[2048,1024]{1,0:T(8,128)S(1)} %fusion.1, bf16[2048,512]{1,0:T(8,128)(2,1)S(1)} %copy-done.16, bf16[1024,512]{1,0:T(8,128)(2,1)} %collective-permute-done.refs_1_), kind=kOutput, calls=%fused_computation.1 | convolution fusion | flops 2151677952 | bytes 15728640 | tf_op jit(solution)/shard_map/dot_general | solution.py:485
  123.0 11.8 %all-to-all-done.4 = bf16[128,8,640]{2,1,0:T(8,128)(2,1)S(1)} async-done(((bf16[128,8,640]{2,1,0:T(8,128)(2,1)}), bf16[128,8,640]{2,1,0:T(8,128)(2,1)S(1)}, u32[]{:S(2)}, u32[]{:S(2)}) %all-to-all-start.4) | async-done | bytes 1310752 | tf_op jit(solution)/shard_map/all_to_all | solution.py:483
  134.8 0.9 finish.1
  135.7 0.5 slice_bitcast_fusion.2
  (25 shorter events, 0.1 us)
Async XLA Ops:
  0.6 46.9 %copy-start = (f32[100,2048]{1,0:T(8,128)S(1)}, f32[100,2048]{1,0:T(8,128)}, u32[]{:S(2)}) copy-start(f32[100,2048]{1,0:T(8,128)} %param.13) | copy-start | bytes 2457604
  0.6 31.2 %copy-start.17 = (f32[100]{0:T(128)S(1)}, f32[100]{0:T(128)}, u32[]{:S(2)}) copy-start(f32[100]{0:T(128)} %param.12) | copy-start | bytes 1204
  0.7 31.3 %copy-start.14 = (f32[1024]{0:T(1024)S(1)}, f32[1024]{0:T(1024)}, u32[]{:S(2)}) copy-start(f32[1024]{0:T(1024)} %param.10) | copy-start | bytes 12292
  0.7 31.4 %copy-start.13 = (bf16[100,1024]{1,0:T(8,128)(2,1)S(1)}, bf16[100,1024]{1,0:T(8,128)(2,1)}, u32[]{:S(2)}) copy-start(bf16[100,1024]{1,0:T(8,128)(2,1)} %param.11) | copy-start | bytes 614404
  31.8 6.2 %copy-start.3 = (bf16[128,8,512]{2,1,0:T(8,128)(2,1)}, bf16[128,8,512]{2,1,0:T(8,128)(2,1)S(1)}, u32[]{:S(2)}) copy-start(bf16[128,8,512]{2,1,0:T(8,128)(2,1)S(1)} %all_to_all.43) | copy-start | bytes 3145732
  31.8 6.3 %collective-permute-start = (bf16[1024,512]{1,0:T(8,128)(2,1)S(1)}, bf16[1024,512]{1,0:T(8,128)(2,1)}, u32[]{:S(2)}, u32[]{:S(2)}) collective-permute-start(bf16[1024,512]{1,0:T(8,128)(2,1)S(1)} %bitcast.36), channel_id=1, source_target_pairs={{0,1},{1,0},{2,3},{3,2},{4,5},{5,4},{6,7},{7,6},{8,9},{9,8},{10,11... | collective-permute-start | bytes 3145736 | tf_op jit(solution)/shard_map/ppermute | solution.py:439
  32.1 6.0 %copy-start.8 = (f32[512]{0:T(512)}, f32[512]{0:T(512)S(1)}, u32[]{:S(2)}) copy-start(f32[512]{0:T(512)S(1)} %get-tuple-element.58) | copy-start | bytes 6148
  32.1 6.0 %copy-start.9 = (f32[512]{0:T(512)}, f32[512]{0:T(512)S(1)}, u32[]{:S(2)}) copy-start(f32[512]{0:T(512)S(1)} %get-tuple-element.59) | copy-start | bytes 6148
  32.1 6.0 %copy-start.5 = (bf16[112,512]{1,0:T(8,128)(2,1)}, bf16[112,512]{1,0:T(8,128)(2,1)S(1)}, u32[]{:S(2)}) copy-start(bf16[112,512]{1,0:T(8,128)(2,1)S(1)} %get-tuple-element.54.refs_3_.refs_7_) | copy-start | bytes 344068
  32.1 6.0 %copy-start.6 = (bf16[112,512]{1,0:T(8,128)(2,1)}, bf16[112,512]{1,0:T(8,128)(2,1)S(1)}, u32[]{:S(2)}) copy-start(bf16[112,512]{1,0:T(8,128)(2,1)S(1)} %get-tuple-element.55.refs_3_.refs_8_) | copy-start | bytes 344068
  32.1 2.4 %copy-start.1 = (bf16[1,2048,1024]{2,1,0:T(8,128)(2,1)S(1)}, bf16[1,2048,1024]{2,1,0:T(8,128)(2,1)}, u32[]{:S(2)}) copy-start(bf16[1,2048,1024]{2,1,0:T(8,128)(2,1)} %param.8) | copy-start | bytes 12582916
  38.1 9.3 %copy-start.15 = (f32[100]{0:T(128)S(1)}, f32[100]{0:T(128)}, u32[]{:S(2)}) copy-start(f32[100]{0:T(128)} %param.14) | copy-start | bytes 1204
  43.8 17.3 %all-to-all-start.1 = ((f32[8,104,256]{2,1,0:T(8,128)}), f32[8,104,256]{2,1,0:T(8,128)S(1)}, u32[]{:S(2)}, u32[]{:S(2)}) async-start(f32[8,104,256]{2,1,0:T(8,128)} %forward_half.3), calls=%async_computation.1 | async-start | bytes 1703936 | tf_op jit(solution)/shard_map/all_to_all | solution.py:460
  47.6 13.5 %copy-start.7 = (s32[3,8]{1,0:T(4,128)S(1)}, s32[3,8]{1,0:T(4,128)}, u32[]{:S(2)}) copy-start(s32[3,8]{1,0:T(4,128)} %plan_ref.1) | copy-start | bytes 292
  63.7 0.6 copy-start.10
  64.3 12.9 %all-to-all-start.2 = ((bf16[8,112,256]{2,1,0:T(8,128)(2,1)}), bf16[8,112,256]{2,1,0:T(8,128)(2,1)S(1)}, u32[]{:S(2)}, u32[]{:S(2)}) async-start(bf16[8,112,256]{2,1,0:T(8,128)(2,1)} %get-tuple-element.33), calls=%async_computation.2 | async-start | bytes 917504 | tf_op jit(solution)/shard_map/all_to_all | solution.py:470
  77.3 0.8 copy-start.11
  88.7 6.2 %collective-permute-start.1 = (bf16[1024,512]{1,0:T(8,128)(2,1)}, bf16[1024,512]{1,0:T(8,128)(2,1)S(1)}, u32[]{:S(2)}, u32[]{:S(2)}) collective-permute-start(bf16[1024,512]{1,0:T(8,128)(2,1)} %get-tuple-element.44), channel_id=1, source_target_pairs={{0,1},{1,0},{2,3},{3,2},{4,5},{5,4},{6,7},{7,6},{8,9},{9,8},{10,11... | collective-permute-start | bytes 3145736 | tf_op jit(solution)/shard_map/ppermute | solution.py:479
  89.6 16.1 %all-to-all-start.3 = ((bf16[128,8,128]{2,1,0:T(8,128)(2,1)}), bf16[128,8,128]{2,1,0:T(8,128)(2,1)S(1)}, u32[]{:S(2)}, u32[]{:S(2)}) async-start(bf16[128,8,128]{2,1,0:T(8,128)(2,1)} %bitcast.45), calls=%async_computation.3 | async-start | bytes 524288 | tf_op jit(solution)/shard_map/all_to_all | solution.py:478
  94.9 1.0 copy-start.12
  105.8 1.2 copy-start.2
  107.0 6.1 %copy-start.4 = (bf16[128,8,512]{2,1,0:T(8,128)(2,1)S(1)}, bf16[128,8,512]{2,1,0:T(8,128)(2,1)}, u32[]{:S(2)}) copy-start(bf16[128,8,512]{2,1,0:T(8,128)(2,1)} %copy-done.3) | copy-start | bytes 3145732
  108.2 26.6 %all-to-all-start.4 = ((bf16[128,8,640]{2,1,0:T(8,128)(2,1)}), bf16[128,8,640]{2,1,0:T(8,128)(2,1)S(1)}, u32[]{:S(2)}, u32[]{:S(2)}) async-start(bf16[128,8,640]{2,1,0:T(8,128)(2,1)} %bitcast.12), calls=%async_computation.4 | async-start | bytes 2621440 | tf_op jit(solution)/shard_map/all_to_all | solution.py:483
  113.1 4.2 %copy-start.16 = (bf16[2048,512]{1,0:T(8,128)(2,1)S(1)}, bf16[2048,512]{1,0:T(8,128)(2,1)}, u32[]{:S(2)}) copy-start(bf16[2048,512]{1,0:T(8,128)(2,1)} %get-tuple-element.49) | copy-start | bytes 6291460

commit v6 on v5

--- a/solution.py
+++ b/solution.py
@@ -144,8 +144,8 @@
         )
 
     ready_cot = load(cot_ref, cot, sems.at[0])
-    ready = [fetch(n) for n in range(len(steps))]
-    ready_lat = load(lat_ref, lat, lat_sem)
+    ahead = 2
+    ready = [fetch(n) for n in range(ahead)]
     ready_cot.wait()
     out = []
     for n, (h, i) in enumerate(steps):
@@ -153,6 +153,10 @@
             b1, w2 = None, None
         for copy in ready[n]:
             copy.wait()
+        if n + ahead < len(steps):
+            ready.append(fetch(n + ahead))
+        if n == 0:
+            ready_lat = load(lat_ref, lat, lat_sem)
         for q in range(i * blocks // parts, (i + 1) * blocks // parts):
             sl = slice(q * block, (q + 1) * block)
             dact = lax.dot_general(
@@ -174,16 +178,8 @@
                 table[h, variables + 1 : variables + 2, : tail.shape[1]] = tail[...]
     lanes = half // 128
     low = core[0] == 0
-    for unit in range(pack.shape[0] // 16):
-        r, c = unit // lanes, unit % lanes
-        pieces = []
-        for h in range(2):
-            piece = table[h, 8 * r : 8 * r + 8, 128 * c : 128 * (c + 1)]
-            pieces.append(jnp.concatenate([piece[:, :64], piece[:, 64:]], axis=0))
-        first = jnp.where(low, pieces[0], pieces[1])
-        second = jnp.where(low, pieces[1], pieces[0])
-        pack[16 * unit : 16 * unit + 16, :] = jnp.concatenate([first, second], axis=1).astype(jnp.bfloat16)
-    out.append(load(pack, pack_ref, out_sems.at[len(steps)]))
+    used = -(-(variables + 3) // 8) * lanes
+    units = pack.shape[0] // 16
     ready_lat.wait()
     cut = lat.shape[1] // parts
     for m in range(parts):
@@ -191,7 +187,21 @@
         give[at, :] = lax.dot_general(
             lat[:, at], dpre_v[1], (((0,), (0,)), ((), ())), preferred_element_type=jnp.float32
         ).astype(jnp.bfloat16)
+        for unit in range(m * units // parts, (m + 1) * units // parts):
+            where = slice(16 * unit, 16 * unit + 16)
+            if unit >= used:
+                pack[where, :] = jnp.zeros((16, pack.shape[1]), jnp.bfloat16)
+                continue
+            r, c = unit // lanes, unit % lanes
+            pieces = []
+            for h in range(2):
+                piece = table[h, 8 * r : 8 * r + 8, 128 * c : 128 * (c + 1)]
+                pieces.append(jnp.concatenate([piece[:, :64], piece[:, 64:]], axis=0))
+            first = jnp.where(low, pieces[0], pieces[1])
+            second = jnp.where(low, pieces[1], pieces[0])
+            pack[where, :] = jnp.concatenate([first, second], axis=1).astype(jnp.bfloat16)
         out.append(load(give.at[at], give_ref.at[at], give_sems.at[m]))
+    out.append(load(pack, pack_ref, out_sems.at[len(steps)]))
     for copy in out:
         copy.wait()
 
@@ -199,7 +209,7 @@
 def cotangents(core, cot, gs, acts, lat, o_halves, tail, variables):
     width = lat.shape[1]
     points, half = gs[0].shape
-    parts = 4
+    parts = 1
     row = shape((points, half), jnp.bfloat16)
     return pl.pallas_call(
         lambda *refs: cotangent_kernel(variables, parts, *refs),

time: 137 us -> 136 us (level)
  no operation moved by 1% of the time
where the time goes in v6:
time: 136 us
  Pallas kernels  45.3 us (33%)
  blocking collectives  30.2 us (22%)
  waiting for transfers between devices  23.3 us (17%)
  starting transfers between devices  18.2 us (13%)
  matrix products  9.93 us (7%)
  local copies, waits for them, and re-layouts  7.62 us (6%)
    all_to_all x1, blocking collectives, shards(): lax.all_to_all(send.reshape(devices * rows, half), BOTH, 0, 0, tiled=True)  30.2 us
    pallas_call x2, Pallas kernels, slope_half(): pl.pallas_call(lambda *refs: slope_kernel(parts, *refs), in_specs=[HBM] *...  16.2 us
    all_to_all x1, waiting for transfers between devices, shards(): parts = lax.all_to_all(chunks, BOTH, 0, 0, tiled=True)  11.8 us
    pallas_call x1, Pallas kernels, cotangents(): pl.pallas_call(lambda *refs: cotangent_kernel(variables, parts, *refs), i...  10.2 us
    dot_general x2, matrix products, shards(): jnp.dot(d, w.T, preferred_element_type=jnp.float32)  9.93 us
    pallas_call x2, Pallas kernels, forward_half(): pl.pallas_call(lambda *refs: forward_kernel(first, 2, *refs), in_specs=[W...  9.27 us
    unnamed x36, local copies, waits for them, and re-layouts  5.94 us
    all_to_all x1, waiting for transfers between devices, shards(): fields = lax.all_to_all(out, 'member', 0, 0, tiled=True)  5.34 us
  transfers between devices with their start and end apart: 6, of which 4 were waited for; matrix products, arithmetic and copies ran while one was open for 8% of the time, Pallas kernels for 18%

profile of v6, /device:TPU:1, one launch (start us, length us, event | category | flops | bytes accessed | tf_op | source)
XLA Modules:
  0.0 135.7 jit_solution(10633681640598916993)
XLA Ops:
  0.6 0.0 copy-start
  0.6 0.0 copy-start.17
  0.7 0.0 copy-start.14
  0.7 0.0 copy-start.13
  0.7 0.8 slice_bitcast_fusion.1
  1.5 0.1 broadcast_in_dim.26
  1.6 30.2 %all_to_all.43 = bf16[128,8,512]{2,1,0:T(8,128)(2,1)S(1)} all-to-all(bf16[128,8,512]{2,1,0:T(8,128)(2,1)S(1)} %bitcast.44), channel_id=1, replica_groups=mesh['member'=8,'grid'=16] {'member','grid'}, dimensions={0} | all-to-all | bytes 2097152 | tf_op jit(solution)/shard_map/all_to_all | solution.py:448
  31.8 0.0 collective-permute-start
  31.9 0.1 copy.14.refs_4_
  32.0 0.1 fusion.3
  32.1 0.0 copy-start.5
  32.1 0.0 copy-start.6
  32.1 0.0 copy-start.1
  32.1 2.3 %copy-done.1 = bf16[1,2048,1024]{2,1,0:T(8,128)(2,1)S(1)} copy-done((bf16[1,2048,1024]{2,1,0:T(8,128)(2,1)S(1)}, bf16[1,2048,1024]{2,1,0:T(8,128)(2,1)}, u32[]{:S(2)}) %copy-start.1) | copy-done | bytes 4194328
  34.5 3.6 %forward_half.2.refs_4_ = f32[8,104,256]{2,1,0:T(8,128)S(1)} custom-call(bf16[2048,1024]{1,0:T(8,128)(2,1)S(1)} %bitcast.33, bf16[1024,512]{1,0:T(8,128)(2,1)S(1)} %bitcast.37, f32[1,512]{1,0:T(1,128)S(1)} %bitcast.40, bf16[112,512]{1,0:T(8,128)(2,1)S(1)} %get-tuple-element.54.refs_3_.refs_7_, f32[104,1]{1,0:T(8,128)S(1)} %copy.14.refs_4_), custom_call_target="tpu_custom_call" | custom-call | flops 2365587456 | bytes 4194304 | tf_op jit(solution)/shard_map/forward_half/pallas_call | solution.py:63
  38.1 0.0 collective-permute-done.refs_1_
  38.1 0.0 copy-start.15
  38.1 5.7 %forward_half.3 = f32[8,104,256]{2,1,0:T(8,128)} custom-call(bf16[2048,1024]{1,0:T(8,128)(2,1)S(1)} %bitcast.34, bf16[1024,512]{1,0:T(8,128)(2,1)} %collective-permute-done.refs_1_, f32[1,512]{1,0:T(1,128)S(1)} %bitcast.42, bf16[112,512]{1,0:T(8,128)(2,1)S(1)} %get-tuple-element.55.refs_3_.refs_8_, f32[8,104,256]{2,1,0:T(8,128)S(1)} %forward_half.2.refs_4_), custom_call_target="tpu_custom_call" | custom-call | flops 2365587456 | bytes 4194304 | tf_op jit(solution)/shard_map/forward_half/pallas_call | solution.py:63
  43.8 3.6 %all-to-all-start.1 = ((f32[8,104,256]{2,1,0:T(8,128)}), f32[8,104,256]{2,1,0:T(8,128)S(1)}, u32[]{:S(2)}, u32[]{:S(2)}) async-start(f32[8,104,256]{2,1,0:T(8,128)} %forward_half.3), calls=%async_computation.1 | async-start | bytes 1703936 | tf_op jit(solution)/shard_map/all_to_all | solution.py:470
  47.5 0.1 broadcast_multiply_fusion
  47.6 0.0 copy-done
  47.6 0.0 copy-start.7
  47.6 8.1 %slope_half.2 = (bf16[2048,512]{1,0:T(8,128)(2,1)}, bf16[2048,512]{1,0:T(8,128)(2,1)}) custom-call(bf16[2048,1024]{1,0:T(8,128)(2,1)} %bitcast.29, bf16[1024,512]{1,0:T(8,128)(2,1)} %collective-permute-done.refs_1_, f32[1,512]{1,0:T(1,128)} %bitcast.43), custom_call_target="tpu_custom_call" | custom-call | flops 2147483648 | bytes 8388608 | tf_op jit(solution)/shard_map/slope_half/pallas_call | solution.py:108
  55.8 5.3 %all-to-all-done.1.f_ref = f32[8,104,256]{2,1,0:T(8,128)S(1)} async-done(((f32[8,104,256]{2,1,0:T(8,128)}), f32[8,104,256]{2,1,0:T(8,128)S(1)}, u32[]{:S(2)}, u32[]{:S(2)}) %all-to-all-start.1) | async-done | bytes 852000 | tf_op jit(solution)/shard_map/all_to_all | solution.py:470
  61.1 2.6 %pair_terms.1 = (bf16[8,112,256]{2,1,0:T(8,128)(2,1)}, f32[1,256]{1,0:T(1,128)S(1)}) custom-call(s32[3,8]{1,0:T(4,128)S(1)} %copy-done.7, f32[8,104,256]{2,1,0:T(8,128)S(1)} %all-to-all-done.1.f_ref, f32[104,256]{1,0:T(8,128)S(1)} %pad.17.t_ref, f32[104,256]{1,0:T(8,128)S(1)} %pad.18.s_ref), custom_call_target="tpu_custom_call" | custom-call | tf_op jit(solution)/shard_map/pair_terms/pallas_call | solution.py:424
  63.7 0.6 copy-done.10
  64.3 3.7 %all-to-all-start.2 = ((bf16[8,112,256]{2,1,0:T(8,128)(2,1)}), bf16[8,112,256]{2,1,0:T(8,128)(2,1)S(1)}, u32[]{:S(2)}, u32[]{:S(2)}) async-start(bf16[8,112,256]{2,1,0:T(8,128)(2,1)} %get-tuple-element.33), calls=%async_computation.2 | async-start | bytes 917504 | tf_op jit(solution)/shard_map/all_to_all | solution.py:480
  68.0 8.1 %slope_half.3 = (bf16[2048,512]{1,0:T(8,128)(2,1)}, bf16[2048,512]{1,0:T(8,128)(2,1)}) custom-call(bf16[2048,1024]{1,0:T(8,128)(2,1)} %bitcast.30, bf16[1024,512]{1,0:T(8,128)(2,1)} %bitcast.38, f32[1,512]{1,0:T(1,128)} %bitcast.41), custom_call_target="tpu_custom_call" | custom-call | flops 2147483648 | bytes 8388608 | tf_op jit(solution)/shard_map/slope_half/pallas_call | solution.py:108
  76.1 1.2 all-to-all-done.2.refs_1_
  77.3 0.8 copy-done.11
  78.0 10.2 %cotangents.1 = (bf16[2048,512]{1,0:T(8,128)(2,1)}, bf16[2048,512]{1,0:T(8,128)(2,1)}, bf16[1024,128]{1,0:T(8,128)(2,1)}, bf16[1024,512]{1,0:T(8,128)(2,1)}) custom-call(s32[1]{0:T(128)} %bitcast.1.refs_0_, bf16[8,112,256]{2,1,0:T(8,128)(2,1)} %copy-done.11, bf16[2048,512]{1,0:T(8,128)(2,1)} %get-tuple-element.37.refs_2_, ...), custom_call_target="tpu_custom_call" | custom-call | flops 3087007744 | bytes 16777216 | tf_op jit(solution)/shard_map/cotangents/pallas_call | solution.py:214
  88.2 0.9 collective-permute-start.1
  89.1 5.3 %all-to-all-start.3 = ((bf16[128,8,128]{2,1,0:T(8,128)(2,1)}), bf16[128,8,128]{2,1,0:T(8,128)(2,1)S(1)}, u32[]{:S(2)}, u32[]{:S(2)}) async-start(bf16[128,8,128]{2,1,0:T(8,128)(2,1)} %bitcast.45), calls=%async_computation.3 | async-start | bytes 524288 | tf_op jit(solution)/shard_map/all_to_all | solution.py:488
  94.4 0.0 collective-permute-done.1.refs_2_
  94.4 0.0 copy-start.12
  94.4 1.0 copy-done.12
  95.4 4.9 %weight_half.1.refs_2_ = bf16[1024,512]{1,0:T(8,128)(2,1)} custom-call(bf16[2048,1024]{1,0:T(8,128)(2,1)} %bitcast.32, bf16[2048,512]{1,0:T(8,128)(2,1)} %get-tuple-element.48.refs_1_, bf16[1024,512]{1,0:T(8,128)(2,1)} %copy-done.12), custom_call_target="tpu_custom_call" | custom-call | flops 2147483648 | bytes 8388608 | tf_op jit(solution)/shard_map/weight_half/pallas_call | solution.py:285
  100.3 5.0 %all-to-all-done.3 = bf16[128,8,128]{2,1,0:T(8,128)(2,1)S(1)} async-done(((bf16[128,8,128]{2,1,0:T(8,128)(2,1)}), bf16[128,8,128]{2,1,0:T(8,128)(2,1)S(1)}, u32[]{:S(2)}, u32[]{:S(2)}) %all-to-all-start.3) | async-done | bytes 262176 | tf_op jit(solution)/shard_map/all_to_all | solution.py:488
  105.3 1.2 copy-done.2
  106.5 1.3 join.1
  107.7 4.8 %all-to-all-start.4 = ((bf16[128,8,640]{2,1,0:T(8,128)(2,1)}), bf16[128,8,640]{2,1,0:T(8,128)(2,1)S(1)}, u32[]{:S(2)}, u32[]{:S(2)}) async-start(bf16[128,8,640]{2,1,0:T(8,128)(2,1)} %bitcast.12), calls=%async_computation.4 | async-start | bytes 2621440 | tf_op jit(solution)/shard_map/all_to_all | solution.py:493
  112.5 0.0 copy-done.4
  112.5 0.0 copy-start.16
  112.6 4.2 %fusion.1 = f32[2048,1024]{1,0:T(8,128)S(1)} fusion(bf16[2048,512]{1,0:T(8,128)(2,1)} %get-tuple-element.48.refs_1_, bf16[128,8,512]{2,1,0:T(8,128)(2,1)S(1)} %copy-done.4), kind=kOutput, calls=%fused_computation.12 | convolution fusion | flops 2147483648 | bytes 11534336 | tf_op jit(solution)/shard_map/dot_general | solution.py:495
  116.8 5.7 %fusion = bf16[1,2048,1024]{2,1,0:T(8,128)(2,1)} fusion(f32[2048,1024]{1,0:T(8,128)S(1)} %fusion.1, bf16[2048,512]{1,0:T(8,128)(2,1)S(1)} %copy-done.16, bf16[1024,512]{1,0:T(8,128)(2,1)} %collective-permute-done.refs_1_), kind=kOutput, calls=%fused_computation.1 | convolution fusion | flops 2151677952 | bytes 15728640 | tf_op jit(solution)/shard_map/dot_general | solution.py:495
  122.5 11.8 %all-to-all-done.4 = bf16[128,8,640]{2,1,0:T(8,128)(2,1)S(1)} async-done(((bf16[128,8,640]{2,1,0:T(8,128)(2,1)}), bf16[128,8,640]{2,1,0:T(8,128)(2,1)S(1)}, u32[]{:S(2)}, u32[]{:S(2)}) %all-to-all-start.4) | async-done | bytes 1310752 | tf_op jit(solution)/shard_map/all_to_all | solution.py:493
  134.3 0.9 finish.1
  135.2 0.5 slice_bitcast_fusion.2
  (25 shorter events, 0.1 us)
Async XLA Ops:
  0.6 46.9 %copy-start = (f32[100,2048]{1,0:T(8,128)S(1)}, f32[100,2048]{1,0:T(8,128)}, u32[]{:S(2)}) copy-start(f32[100,2048]{1,0:T(8,128)} %param.13) | copy-start | bytes 2457604
  0.6 31.2 %copy-start.17 = (f32[100]{0:T(128)S(1)}, f32[100]{0:T(128)}, u32[]{:S(2)}) copy-start(f32[100]{0:T(128)} %param.12) | copy-start | bytes 1204
  0.7 31.3 %copy-start.14 = (f32[1024]{0:T(1024)S(1)}, f32[1024]{0:T(1024)}, u32[]{:S(2)}) copy-start(f32[1024]{0:T(1024)} %param.10) | copy-start | bytes 12292
  0.7 31.4 %copy-start.13 = (bf16[100,1024]{1,0:T(8,128)(2,1)S(1)}, bf16[100,1024]{1,0:T(8,128)(2,1)}, u32[]{:S(2)}) copy-start(bf16[100,1024]{1,0:T(8,128)(2,1)} %param.11) | copy-start | bytes 614404
  31.8 6.2 %copy-start.3 = (bf16[128,8,512]{2,1,0:T(8,128)(2,1)}, bf16[128,8,512]{2,1,0:T(8,128)(2,1)S(1)}, u32[]{:S(2)}) copy-start(bf16[128,8,512]{2,1,0:T(8,128)(2,1)S(1)} %all_to_all.43) | copy-start | bytes 3145732
  31.8 6.3 %collective-permute-start = (bf16[1024,512]{1,0:T(8,128)(2,1)S(1)}, bf16[1024,512]{1,0:T(8,128)(2,1)}, u32[]{:S(2)}, u32[]{:S(2)}) collective-permute-start(bf16[1024,512]{1,0:T(8,128)(2,1)S(1)} %bitcast.36), channel_id=1, source_target_pairs={{0,1},{1,0},{2,3},{3,2},{4,5},{5,4},{6,7},{7,6},{8,9},{9,8},{10,11... | collective-permute-start | bytes 3145736 | tf_op jit(solution)/shard_map/ppermute | solution.py:449
  32.1 6.0 %copy-start.8 = (f32[512]{0:T(512)}, f32[512]{0:T(512)S(1)}, u32[]{:S(2)}) copy-start(f32[512]{0:T(512)S(1)} %get-tuple-element.58) | copy-start | bytes 6148
  32.1 6.0 %copy-start.9 = (f32[512]{0:T(512)}, f32[512]{0:T(512)S(1)}, u32[]{:S(2)}) copy-start(f32[512]{0:T(512)S(1)} %get-tuple-element.59) | copy-start | bytes 6148
  32.1 6.0 %copy-start.5 = (bf16[112,512]{1,0:T(8,128)(2,1)}, bf16[112,512]{1,0:T(8,128)(2,1)S(1)}, u32[]{:S(2)}) copy-start(bf16[112,512]{1,0:T(8,128)(2,1)S(1)} %get-tuple-element.54.refs_3_.refs_7_) | copy-start | bytes 344068
  32.1 6.0 %copy-start.6 = (bf16[112,512]{1,0:T(8,128)(2,1)}, bf16[112,512]{1,0:T(8,128)(2,1)S(1)}, u32[]{:S(2)}) copy-start(bf16[112,512]{1,0:T(8,128)(2,1)S(1)} %get-tuple-element.55.refs_3_.refs_8_) | copy-start | bytes 344068
  32.1 2.4 %copy-start.1 = (bf16[1,2048,1024]{2,1,0:T(8,128)(2,1)S(1)}, bf16[1,2048,1024]{2,1,0:T(8,128)(2,1)}, u32[]{:S(2)}) copy-start(bf16[1,2048,1024]{2,1,0:T(8,128)(2,1)} %param.8) | copy-start | bytes 12582916
  38.1 9.3 %copy-start.15 = (f32[100]{0:T(128)S(1)}, f32[100]{0:T(128)}, u32[]{:S(2)}) copy-start(f32[100]{0:T(128)} %param.14) | copy-start | bytes 1204
  43.8 17.3 %all-to-all-start.1 = ((f32[8,104,256]{2,1,0:T(8,128)}), f32[8,104,256]{2,1,0:T(8,128)S(1)}, u32[]{:S(2)}, u32[]{:S(2)}) async-start(f32[8,104,256]{2,1,0:T(8,128)} %forward_half.3), calls=%async_computation.1 | async-start | bytes 1703936 | tf_op jit(solution)/shard_map/all_to_all | solution.py:470
  47.6 13.5 %copy-start.7 = (s32[3,8]{1,0:T(4,128)S(1)}, s32[3,8]{1,0:T(4,128)}, u32[]{:S(2)}) copy-start(s32[3,8]{1,0:T(4,128)} %plan_ref.1) | copy-start | bytes 292
  63.7 0.6 copy-start.10
  64.3 12.9 %all-to-all-start.2 = ((bf16[8,112,256]{2,1,0:T(8,128)(2,1)}), bf16[8,112,256]{2,1,0:T(8,128)(2,1)S(1)}, u32[]{:S(2)}, u32[]{:S(2)}) async-start(bf16[8,112,256]{2,1,0:T(8,128)(2,1)} %get-tuple-element.33), calls=%async_computation.2 | async-start | bytes 917504 | tf_op jit(solution)/shard_map/all_to_all | solution.py:480
  77.2 0.8 copy-start.11
  88.2 6.2 %collective-permute-start.1 = (bf16[1024,512]{1,0:T(8,128)(2,1)}, bf16[1024,512]{1,0:T(8,128)(2,1)S(1)}, u32[]{:S(2)}, u32[]{:S(2)}) collective-permute-start(bf16[1024,512]{1,0:T(8,128)(2,1)} %get-tuple-element.44), channel_id=1, source_target_pairs={{0,1},{1,0},{2,3},{3,2},{4,5},{5,4},{6,7},{7,6},{8,9},{9,8},{10,11... | collective-permute-start | bytes 3145736 | tf_op jit(solution)/shard_map/ppermute | solution.py:489
  89.1 16.1 %all-to-all-start.3 = ((bf16[128,8,128]{2,1,0:T(8,128)(2,1)}), bf16[128,8,128]{2,1,0:T(8,128)(2,1)S(1)}, u32[]{:S(2)}, u32[]{:S(2)}) async-start(bf16[128,8,128]{2,1,0:T(8,128)(2,1)} %bitcast.45), calls=%async_computation.3 | async-start | bytes 524288 | tf_op jit(solution)/shard_map/all_to_all | solution.py:488
  94.4 1.0 copy-start.12
  105.2 1.2 copy-start.2
  106.5 6.1 %copy-start.4 = (bf16[128,8,512]{2,1,0:T(8,128)(2,1)S(1)}, bf16[128,8,512]{2,1,0:T(8,128)(2,1)}, u32[]{:S(2)}) copy-start(bf16[128,8,512]{2,1,0:T(8,128)(2,1)} %copy-done.3) | copy-start | bytes 3145732
  107.7 26.6 %all-to-all-start.4 = ((bf16[128,8,640]{2,1,0:T(8,128)(2,1)}), bf16[128,8,640]{2,1,0:T(8,128)(2,1)S(1)}, u32[]{:S(2)}, u32[]{:S(2)}) async-start(bf16[128,8,640]{2,1,0:T(8,128)(2,1)} %bitcast.12), calls=%async_computation.4 | async-start | bytes 2621440 | tf_op jit(solution)/shard_map/all_to_all | solution.py:493
  112.5 4.2 %copy-start.16 = (bf16[2048,512]{1,0:T(8,128)(2,1)S(1)}, bf16[2048,512]{1,0:T(8,128)(2,1)}, u32[]{:S(2)}) copy-start(bf16[2048,512]{1,0:T(8,128)(2,1)} %get-tuple-element.49) | copy-start | bytes 6291460

commit v7 on v6

--- a/solution.py
+++ b/solution.py
@@ -354,10 +354,10 @@
                     w2_ref[low : low + keep, cols] = piece[:keep] * kappa
                 at = variables - low
                 if 0 <= at < 8:
-                    b1_ref[:, cols] = piece[at : at + 1] * kappa
+                    b1_ref[cols] = piece[at] * kappa
                     tail[:, cols] = piece[at + 1 : at + 2] + piece[at + 2 : at + 3]
     both = tail[:, :half] + tail[:, half:]
-    b2_ref[...] = both[:, :128] * kappa
+    b2_ref[...] = both[0, :128] * kappa
     loss_ref[...] = both[:, 128:256] * share
 
 
@@ -369,8 +369,8 @@
         out_shape=[
             shape((rows, width), jnp.float32),
             shape((variables, width), jnp.float32),
-            shape((1, width), jnp.float32),
-            shape((1, 128), jnp.float32),
+            shape((width,), jnp.float32),
+            shape((128,), jnp.float32),
             shape((1, 128), jnp.float32),
         ],
         scratch_shapes=[pltpu.VMEM((1, width), jnp.float32)],
@@ -502,9 +502,9 @@
         loss[0, 0],
         grad_hidden[None],
         own_rows,
-        grad_bias[0],
+        grad_bias,
         grad_out,
-        grad_b_out[0, :variables],
+        grad_b_out[:variables],
     )
 
 

time: 136 us -> 136 us (level)
  no operation moved by 1% of the time
where the time goes in v7:
time: 136 us; the launch traced here: 135 us
  Pallas kernels  45.4 us (33%)
  blocking collectives  30.2 us (22%)
  waiting for transfers between devices  23.3 us (17%)
  starting transfers between devices  18.2 us (13%)
  matrix products  9.93 us (7%)
  local copies, waits for them, and re-layouts  7.11 us (5%)
    all_to_all x1, blocking collectives, shards(): lax.all_to_all(send.reshape(devices * rows, half), BOTH, 0, 0, tiled=True)  30.2 us
    pallas_call x2, Pallas kernels, slope_half(): pl.pallas_call(lambda *refs: slope_kernel(parts, *refs), in_specs=[HBM] *...  16.2 us
    all_to_all x1, waiting for transfers between devices, shards(): parts = lax.all_to_all(chunks, BOTH, 0, 0, tiled=True)  11.8 us
    pallas_call x1, Pallas kernels, cotangents(): pl.pallas_call(lambda *refs: cotangent_kernel(variables, parts, *refs), i...  10.2 us
    dot_general x2, matrix products, shards(): jnp.dot(d, w.T, preferred_element_type=jnp.float32)  9.93 us
    pallas_call x2, Pallas kernels, forward_half(): pl.pallas_call(lambda *refs: forward_kernel(first, 2, *refs), in_specs=[W...  9.27 us
    unnamed x36, local copies, waits for them, and re-layouts  5.94 us
    all_to_all x1, waiting for transfers between devices, shards(): fields = lax.all_to_all(out, 'member', 0, 0, tiled=True)  5.34 us
  transfers between devices with their start and end apart: 6, of which 4 were waited for; matrix products, arithmetic and copies ran while one was open for 8% of the time, Pallas kernels for 18%

profile of v7, /device:TPU:1, one launch (start us, length us, event | category | flops | bytes accessed | tf_op | source)
XLA Modules:
  0.0 135.2 jit_solution(18400593070351814516)
XLA Ops:
  0.6 0.0 copy-start
  0.6 0.0 copy-start.17
  0.7 0.0 copy-start.14
  0.7 0.0 copy-start.13
  0.7 0.8 slice_bitcast_fusion.1
  1.5 0.1 broadcast_in_dim.26
  1.6 30.2 %all_to_all.43 = bf16[128,8,512]{2,1,0:T(8,128)(2,1)S(1)} all-to-all(bf16[128,8,512]{2,1,0:T(8,128)(2,1)S(1)} %bitcast.42), channel_id=1, replica_groups=mesh['member'=8,'grid'=16] {'member','grid'}, dimensions={0} | all-to-all | bytes 2097152 | tf_op jit(solution)/shard_map/all_to_all | solution.py:448
  31.8 0.0 collective-permute-start
  31.9 0.0 copy-done.17
  31.9 0.1 copy.14.refs_4_
  32.0 0.0 copy-done.14
  32.0 0.1 fusion.3
  32.1 0.0 copy-done.13
  32.1 0.0 copy-start.5
  32.1 0.0 copy-start.1
  32.1 2.3 %copy-done.1 = bf16[1,2048,1024]{2,1,0:T(8,128)(2,1)S(1)} copy-done((bf16[1,2048,1024]{2,1,0:T(8,128)(2,1)S(1)}, bf16[1,2048,1024]{2,1,0:T(8,128)(2,1)}, u32[]{:S(2)}) %copy-start.1) | copy-done | bytes 4194328
  34.5 3.6 %forward_half.2.refs_4_ = f32[8,104,256]{2,1,0:T(8,128)S(1)} custom-call(bf16[2048,1024]{1,0:T(8,128)(2,1)S(1)} %bitcast.31, bf16[1024,512]{1,0:T(8,128)(2,1)S(1)} %bitcast.35, f32[1,512]{1,0:T(1,128)S(1)} %bitcast.38, bf16[112,512]{1,0:T(8,128)(2,1)S(1)} %get-tuple-element.54.refs_3_.refs_7_, f32[104,1]{1,0:T(8,128)S(1)} %copy.14.refs_4_), custom_call_target="tpu_custom_call" | custom-call | flops 2365587456 | bytes 4194304 | tf_op jit(solution)/shard_map/forward_half/pallas_call | solution.py:63
  38.1 0.0 collective-permute-done.refs_1_
  38.1 0.0 copy-start.15
  38.1 5.7 %forward_half.3 = f32[8,104,256]{2,1,0:T(8,128)} custom-call(bf16[2048,1024]{1,0:T(8,128)(2,1)S(1)} %bitcast.32, bf16[1024,512]{1,0:T(8,128)(2,1)} %collective-permute-done.refs_1_, f32[1,512]{1,0:T(1,128)S(1)} %bitcast.40, bf16[112,512]{1,0:T(8,128)(2,1)S(1)} %get-tuple-element.55.refs_3_.refs_8_, f32[8,104,256]{2,1,0:T(8,128)S(1)} %forward_half.2.refs_4_), custom_call_target="tpu_custom_call" | custom-call | flops 2365587456 | bytes 4194304 | tf_op jit(solution)/shard_map/forward_half/pallas_call | solution.py:63
  43.8 3.6 %all-to-all-start.1 = ((f32[8,104,256]{2,1,0:T(8,128)}), f32[8,104,256]{2,1,0:T(8,128)S(1)}, u32[]{:S(2)}, u32[]{:S(2)}) async-start(f32[8,104,256]{2,1,0:T(8,128)} %forward_half.3), calls=%async_computation.1 | async-start | bytes 1703936 | tf_op jit(solution)/shard_map/all_to_all | solution.py:470
  47.5 0.1 broadcast_multiply_fusion
  47.6 0.0 copy-start.7
  47.6 8.1 %slope_half.2 = (bf16[2048,512]{1,0:T(8,128)(2,1)}, bf16[2048,512]{1,0:T(8,128)(2,1)}) custom-call(bf16[2048,1024]{1,0:T(8,128)(2,1)} %bitcast.27, bf16[1024,512]{1,0:T(8,128)(2,1)} %collective-permute-done.refs_1_, f32[1,512]{1,0:T(1,128)} %bitcast.41), custom_call_target="tpu_custom_call" | custom-call | flops 2147483648 | bytes 8388608 | tf_op jit(solution)/shard_map/slope_half/pallas_call | solution.py:108
  55.8 5.3 %all-to-all-done.1.f_ref = f32[8,104,256]{2,1,0:T(8,128)S(1)} async-done(((f32[8,104,256]{2,1,0:T(8,128)}), f32[8,104,256]{2,1,0:T(8,128)S(1)}, u32[]{:S(2)}, u32[]{:S(2)}) %all-to-all-start.1) | async-done | bytes 852000 | tf_op jit(solution)/shard_map/all_to_all | solution.py:470
  61.1 0.0 copy-done.7
  61.1 2.6 %pair_terms.1 = (bf16[8,112,256]{2,1,0:T(8,128)(2,1)}, f32[1,256]{1,0:T(1,128)S(1)}) custom-call(s32[3,8]{1,0:T(4,128)S(1)} %copy-done.7, f32[8,104,256]{2,1,0:T(8,128)S(1)} %all-to-all-done.1.f_ref, f32[104,256]{1,0:T(8,128)S(1)} %pad.17.t_ref, f32[104,256]{1,0:T(8,128)S(1)} %pad.18.s_ref), custom_call_target="tpu_custom_call" | custom-call | tf_op jit(solution)/shard_map/pair_terms/pallas_call | solution.py:424
  63.7 0.6 copy-done.10
  64.3 3.7 %all-to-all-start.2 = ((bf16[8,112,256]{2,1,0:T(8,128)(2,1)}), bf16[8,112,256]{2,1,0:T(8,128)(2,1)S(1)}, u32[]{:S(2)}, u32[]{:S(2)}) async-start(bf16[8,112,256]{2,1,0:T(8,128)(2,1)} %get-tuple-element.33), calls=%async_computation.2 | async-start | bytes 917504 | tf_op jit(solution)/shard_map/all_to_all | solution.py:480
  68.0 8.1 %slope_half.3 = (bf16[2048,512]{1,0:T(8,128)(2,1)}, bf16[2048,512]{1,0:T(8,128)(2,1)}) custom-call(bf16[2048,1024]{1,0:T(8,128)(2,1)} %bitcast.28, bf16[1024,512]{1,0:T(8,128)(2,1)} %bitcast.36, f32[1,512]{1,0:T(1,128)} %bitcast.39), custom_call_target="tpu_custom_call" | custom-call | flops 2147483648 | bytes 8388608 | tf_op jit(solution)/shard_map/slope_half/pallas_call | solution.py:108
  76.1 1.2 all-to-all-done.2.refs_1_
  77.3 0.8 copy-done.11
  78.0 10.2 %cotangents.1 = (bf16[2048,512]{1,0:T(8,128)(2,1)}, bf16[2048,512]{1,0:T(8,128)(2,1)}, bf16[1024,128]{1,0:T(8,128)(2,1)}, bf16[1024,512]{1,0:T(8,128)(2,1)}) custom-call(s32[1]{0:T(128)} %bitcast.1.refs_0_, bf16[8,112,256]{2,1,0:T(8,128)(2,1)} %copy-done.11, bf16[2048,512]{1,0:T(8,128)(2,1)} %get-tuple-element.37.refs_2_, ...), custom_call_target="tpu_custom_call" | custom-call | flops 3087007744 | bytes 16777216 | tf_op jit(solution)/shard_map/cotangents/pallas_call | solution.py:214
  88.2 0.9 collective-permute-start.1
  89.1 5.3 %all-to-all-start.3 = ((bf16[128,8,128]{2,1,0:T(8,128)(2,1)}), bf16[128,8,128]{2,1,0:T(8,128)(2,1)S(1)}, u32[]{:S(2)}, u32[]{:S(2)}) async-start(bf16[128,8,128]{2,1,0:T(8,128)(2,1)} %bitcast.43), calls=%async_computation.3 | async-start | bytes 524288 | tf_op jit(solution)/shard_map/all_to_all | solution.py:488
  94.4 0.0 collective-permute-done.1.refs_2_
  94.4 0.0 copy-start.12
  94.4 1.0 copy-done.12
  95.4 4.9 %weight_half.1.refs_2_ = bf16[1024,512]{1,0:T(8,128)(2,1)} custom-call(bf16[2048,1024]{1,0:T(8,128)(2,1)} %bitcast.30, bf16[2048,512]{1,0:T(8,128)(2,1)} %get-tuple-element.48.refs_1_, bf16[1024,512]{1,0:T(8,128)(2,1)} %copy-done.12), custom_call_target="tpu_custom_call" | custom-call | flops 2147483648 | bytes 8388608 | tf_op jit(solution)/shard_map/weight_half/pallas_call | solution.py:285
  100.3 5.0 %all-to-all-done.3 = bf16[128,8,128]{2,1,0:T(8,128)(2,1)S(1)} async-done(((bf16[128,8,128]{2,1,0:T(8,128)(2,1)}), bf16[128,8,128]{2,1,0:T(8,128)(2,1)S(1)}, u32[]{:S(2)}, u32[]{:S(2)}) %all-to-all-start.3) | async-done | bytes 262176 | tf_op jit(solution)/shard_map/all_to_all | solution.py:488
  105.3 1.2 copy-done.2
  106.5 1.3 join.1
  107.7 4.8 %all-to-all-start.4 = ((bf16[128,8,640]{2,1,0:T(8,128)(2,1)}), bf16[128,8,640]{2,1,0:T(8,128)(2,1)S(1)}, u32[]{:S(2)}, u32[]{:S(2)}) async-start(bf16[128,8,640]{2,1,0:T(8,128)(2,1)} %bitcast.12), calls=%async_computation.4 | async-start | bytes 2621440 | tf_op jit(solution)/shard_map/all_to_all | solution.py:493
  112.6 4.2 %fusion.1 = f32[2048,1024]{1,0:T(8,128)S(1)} fusion(bf16[2048,512]{1,0:T(8,128)(2,1)} %get-tuple-element.48.refs_1_, bf16[128,8,512]{2,1,0:T(8,128)(2,1)S(1)} %copy-done.4), kind=kOutput, calls=%fused_computation.11 | convolution fusion | flops 2147483648 | bytes 11534336 | tf_op jit(solution)/shard_map/dot_general | solution.py:495
  116.8 0.0 copy-done.16
  116.8 5.7 %fusion = bf16[1,2048,1024]{2,1,0:T(8,128)(2,1)} fusion(f32[2048,1024]{1,0:T(8,128)S(1)} %fusion.1, bf16[2048,512]{1,0:T(8,128)(2,1)S(1)} %copy-done.16, bf16[1024,512]{1,0:T(8,128)(2,1)} %collective-permute-done.refs_1_), kind=kOutput, calls=%fused_computation.1 | convolution fusion | flops 2151677952 | bytes 15728640 | tf_op jit(solution)/shard_map/dot_general | solution.py:495
  122.5 11.8 %all-to-all-done.4 = bf16[128,8,640]{2,1,0:T(8,128)(2,1)S(1)} async-done(((bf16[128,8,640]{2,1,0:T(8,128)(2,1)}), bf16[128,8,640]{2,1,0:T(8,128)(2,1)S(1)}, u32[]{:S(2)}, u32[]{:S(2)}) %all-to-all-start.4) | async-done | bytes 1310752 | tf_op jit(solution)/shard_map/all_to_all | solution.py:493
  134.3 0.9 finish.1
  (24 shorter events, 0.1 us)
Async XLA Ops:
  0.6 46.9 %copy-start = (f32[100,2048]{1,0:T(8,128)S(1)}, f32[100,2048]{1,0:T(8,128)}, u32[]{:S(2)}) copy-start(f32[100,2048]{1,0:T(8,128)} %param.13) | copy-start | bytes 2457604
  0.6 31.2 %copy-start.17 = (f32[100]{0:T(128)S(1)}, f32[100]{0:T(128)}, u32[]{:S(2)}) copy-start(f32[100]{0:T(128)} %param.12) | copy-start | bytes 1204
  0.7 31.3 %copy-start.14 = (f32[1024]{0:T(1024)S(1)}, f32[1024]{0:T(1024)}, u32[]{:S(2)}) copy-start(f32[1024]{0:T(1024)} %param.10) | copy-start | bytes 12292
  0.7 31.4 %copy-start.13 = (bf16[100,1024]{1,0:T(8,128)(2,1)S(1)}, bf16[100,1024]{1,0:T(8,128)(2,1)}, u32[]{:S(2)}) copy-start(bf16[100,1024]{1,0:T(8,128)(2,1)} %param.11) | copy-start | bytes 614404
  31.8 6.2 %copy-start.3 = (bf16[128,8,512]{2,1,0:T(8,128)(2,1)}, bf16[128,8,512]{2,1,0:T(8,128)(2,1)S(1)}, u32[]{:S(2)}) copy-start(bf16[128,8,512]{2,1,0:T(8,128)(2,1)S(1)} %all_to_all.43) | copy-start | bytes 3145732
  31.8 6.3 %collective-permute-start = (bf16[1024,512]{1,0:T(8,128)(2,1)S(1)}, bf16[1024,512]{1,0:T(8,128)(2,1)}, u32[]{:S(2)}, u32[]{:S(2)}) collective-permute-start(bf16[1024,512]{1,0:T(8,128)(2,1)S(1)} %bitcast.34), channel_id=1, source_target_pairs={{0,1},{1,0},{2,3},{3,2},{4,5},{5,4},{6,7},{7,6},{8,9},{9,8},{10,11... | collective-permute-start | bytes 3145736 | tf_op jit(solution)/shard_map/ppermute | solution.py:449
  32.1 6.0 %copy-start.8 = (f32[512]{0:T(512)}, f32[512]{0:T(512)S(1)}, u32[]{:S(2)}) copy-start(f32[512]{0:T(512)S(1)} %get-tuple-element.58) | copy-start | bytes 6148
  32.1 6.0 %copy-start.9 = (f32[512]{0:T(512)}, f32[512]{0:T(512)S(1)}, u32[]{:S(2)}) copy-start(f32[512]{0:T(512)S(1)} %get-tuple-element.59) | copy-start | bytes 6148
  32.1 6.0 %copy-start.5 = (bf16[112,512]{1,0:T(8,128)(2,1)}, bf16[112,512]{1,0:T(8,128)(2,1)S(1)}, u32[]{:S(2)}) copy-start(bf16[112,512]{1,0:T(8,128)(2,1)S(1)} %get-tuple-element.54.refs_3_.refs_7_) | copy-start | bytes 344068
  32.1 6.0 %copy-start.6 = (bf16[112,512]{1,0:T(8,128)(2,1)}, bf16[112,512]{1,0:T(8,128)(2,1)S(1)}, u32[]{:S(2)}) copy-start(bf16[112,512]{1,0:T(8,128)(2,1)S(1)} %get-tuple-element.55.refs_3_.refs_8_) | copy-start | bytes 344068
  32.1 2.4 %copy-start.1 = (bf16[1,2048,1024]{2,1,0:T(8,128)(2,1)S(1)}, bf16[1,2048,1024]{2,1,0:T(8,128)(2,1)}, u32[]{:S(2)}) copy-start(bf16[1,2048,1024]{2,1,0:T(8,128)(2,1)} %param.8) | copy-start | bytes 12582916
  38.1 9.3 %copy-start.15 = (f32[100]{0:T(128)S(1)}, f32[100]{0:T(128)}, u32[]{:S(2)}) copy-start(f32[100]{0:T(128)} %param.14) | copy-start | bytes 1204
  43.8 17.3 %all-to-all-start.1 = ((f32[8,104,256]{2,1,0:T(8,128)}), f32[8,104,256]{2,1,0:T(8,128)S(1)}, u32[]{:S(2)}, u32[]{:S(2)}) async-start(f32[8,104,256]{2,1,0:T(8,128)} %forward_half.3), calls=%async_computation.1 | async-start | bytes 1703936 | tf_op jit(solution)/shard_map/all_to_all | solution.py:470
  47.6 13.5 %copy-start.7 = (s32[3,8]{1,0:T(4,128)S(1)}, s32[3,8]{1,0:T(4,128)}, u32[]{:S(2)}) copy-start(s32[3,8]{1,0:T(4,128)} %plan_ref.1) | copy-start | bytes 292
  63.7 0.6 copy-start.10
  64.3 12.9 %all-to-all-start.2 = ((bf16[8,112,256]{2,1,0:T(8,128)(2,1)}), bf16[8,112,256]{2,1,0:T(8,128)(2,1)S(1)}, u32[]{:S(2)}, u32[]{:S(2)}) async-start(bf16[8,112,256]{2,1,0:T(8,128)(2,1)} %get-tuple-element.33), calls=%async_computation.2 | async-start | bytes 917504 | tf_op jit(solution)/shard_map/all_to_all | solution.py:480
  77.2 0.8 copy-start.11
  88.2 6.2 %collective-permute-start.1 = (bf16[1024,512]{1,0:T(8,128)(2,1)}, bf16[1024,512]{1,0:T(8,128)(2,1)S(1)}, u32[]{:S(2)}, u32[]{:S(2)}) collective-permute-start(bf16[1024,512]{1,0:T(8,128)(2,1)} %get-tuple-element.44), channel_id=1, source_target_pairs={{0,1},{1,0},{2,3},{3,2},{4,5},{5,4},{6,7},{7,6},{8,9},{9,8},{10,11... | collective-permute-start | bytes 3145736 | tf_op jit(solution)/shard_map/ppermute | solution.py:489
  89.1 16.1 %all-to-all-start.3 = ((bf16[128,8,128]{2,1,0:T(8,128)(2,1)}), bf16[128,8,128]{2,1,0:T(8,128)(2,1)S(1)}, u32[]{:S(2)}, u32[]{:S(2)}) async-start(bf16[128,8,128]{2,1,0:T(8,128)(2,1)} %bitcast.43), calls=%async_computation.3 | async-start | bytes 524288 | tf_op jit(solution)/shard_map/all_to_all | solution.py:488
  94.4 1.0 copy-start.12
  105.2 1.2 copy-start.2
  106.5 6.1 %copy-start.4 = (bf16[128,8,512]{2,1,0:T(8,128)(2,1)S(1)}, bf16[128,8,512]{2,1,0:T(8,128)(2,1)}, u32[]{:S(2)}) copy-start(bf16[128,8,512]{2,1,0:T(8,128)(2,1)} %copy-done.3) | copy-start | bytes 3145732
  107.7 26.6 %all-to-all-start.4 = ((bf16[128,8,640]{2,1,0:T(8,128)(2,1)}), bf16[128,8,640]{2,1,0:T(8,128)(2,1)S(1)}, u32[]{:S(2)}, u32[]{:S(2)}) async-start(bf16[128,8,640]{2,1,0:T(8,128)(2,1)} %bitcast.12), calls=%async_computation.4 | async-start | bytes 2621440 | tf_op jit(solution)/shard_map/all_to_all | solution.py:493
  112.5 4.2 %copy-start.16 = (bf16[2048,512]{1,0:T(8,128)(2,1)S(1)}, bf16[2048,512]{1,0:T(8,128)(2,1)}, u32[]{:S(2)}) copy-start(bf16[2048,512]{1,0:T(8,128)(2,1)} %get-tuple-element.49) | copy-start | bytes 6291460
